TPU v7x, 32 devices: a whole 2x2x4 slice. The times are simulated.
32 devices in a mesh: grp: 2 (over y), loan: 4 (over z), feat: 4 (over x, core).
Axes of the slice: x: 2, y: 2, z: 4, core: 2. Of those that a mesh axis runs over, the one named last changes fastest.
Arguments:
- design: bfloat16 [16384, 4096], P(('grp', 'loan'), 'feat'), parts along dimension 0, may hold values from -6 to 6
- labels: int32 [16384], P(('grp', 'loan')), parts along dimension 0, may hold values from 0 to 1
- pool_ids: int32 [16384], P(('grp', 'loan')), parts along dimension 0, may hold values from 0 to 255, as said below
- pool_region_index: int32 [512], P(('grp', 'loan')), parts along dimension 0, may hold values from 0 to 63
- step_size: float32 [32], P('grp'), parts along dimension 0, may hold values from 0.005 to 0.02
- beta: float32 [32, 4096], P('grp', 'feat'), parts along dimension 0, may hold values from -0.09375 to 0.09375
- pools: float32 [32, 256, 256], P('grp', 'loan', 'feat'), parts along dimension 0, may hold values from -0.5 to 0.5
- regions: float32 [32, 64, 256], P('grp', None, 'feat'), parts along dimension 0, may hold values from -0.5 to 0.5
- beta_momentum: float32 [32, 4096], P('grp', 'feat'), parts along dimension 0, may hold values from -6 to 6
- pool_momentum: float32 [32, 256, 256], P('grp', 'loan', 'feat'), parts along dimension 0, may hold values from -6 to 6
- region_momentum: float32 [32, 64, 256], P('grp', None, 'feat'), parts along dimension 0, may hold values from -6 to 6
Outputs:
- beta_next: float32 [32, 4096], P('grp', 'feat'), parts along dimension 0
- pools_next: float32 [32, 256, 256], P('grp', 'loan', 'feat'), parts along dimension 0
- regions_next: float32 [32, 64, 256], P('grp', None, 'feat'), parts along dimension 0
- beta_momentum_next: float32 [32, 4096], P('grp', 'feat'), parts along dimension 0
- pool_momentum_next: float32 [32, 256, 256], P('grp', 'loan', 'feat'), parts along dimension 0
- region_momentum_next: float32 [32, 64, 256], P('grp', None, 'feat'), parts along dimension 0
There are 2 independent parts, one for each index of `grp`. A program takes and returns all parts, laid end to end along the dimension named above; each array names one. Nothing has to cross between parts.
Inputs may be any that keep to these rules, and one draw needn't show every extreme that they name: `pool_ids`: in each aligned block of 2048 loans (block l counted from 0) the pool ids lie in l * 64 to (l + 1) * 64 - 1 and do not fall along the block.
All inputs are finite; a program needn't handle non-finite values.
Results may differ from a plain program's by a relative error of at most 0.0006.
Values may be sent and summed in bfloat16 or wider, within the bound.
No kernel may reach another device: no remote copies, remote signals or barrier semaphores. Data moves between devices by JAX's collectives and lax.ppermute only.
A program may use at most 64 MiB of HBM per device.

v0:
```python
import jax
import jax.numpy as jnp
from jax import lax
from jax.sharding import PartitionSpec as P

F = 4096
G = 256


MATMUL_ACCURACY = 256.0


def gradient(
    design, labels, pool_ids, pool_region_index, b_full, b_own, upper_operand, lower_operand
):
    stride = F // G
    slope_bf = design[:, ::stride]
    slope_feats = slope_bf.astype(jnp.float32)
    rows = design.shape[0]
    owned = upper_operand.shape[1]
    first = lax.axis_index("loan") * owned
    local_ids = pool_ids - first
    b16 = b_full.astype(jnp.bfloat16)
    linear = lax.dot_general(
        b16, design, (((1,), (1,)), ((), ())), preferred_element_type=jnp.float32
    )
    chosen = jnp.take(upper_operand, local_ids, axis=1)
    term = jnp.einsum("ng,cng->cn", slope_feats, chosen, precision=lax.Precision.HIGHEST)
    partial_logit = linear + term
    width = rows // lax.axis_size("feat")
    share = lax.psum_scatter(partial_logit, "feat", scatter_dimension=1, tiled=True)
    mine = lax.dynamic_slice_in_dim(labels, lax.axis_index("feat") * width, width)
    resid_share = (mine.astype(jnp.float32)[None, :] - jax.nn.sigmoid(share)).astype(jnp.bfloat16)
    resid = lax.all_gather(resid_share, "feat", axis=1, tiled=True)
    xt = lax.dot_general(
        resid, design, (((1,), (0,)), ((), ())), preferred_element_type=jnp.float32
    )
    member = (local_ids[:, None] == jnp.arange(owned, dtype=jnp.int32)[None, :]).astype(
        jnp.bfloat16
    )
    resid_table = resid[:, :, None] * member[None, :, :]
    lik = jnp.einsum("cnp,ng->cpg", resid_table, slope_bf, preferred_element_type=jnp.float32)
    region_lookup_matrix = (
        pool_region_index[:, None] == jnp.arange(lower_operand.shape[1], dtype=jnp.int32)[None, :]
    ).astype(jnp.float32)
    selected_operand = jnp.einsum(
        "bv,yva->yba", region_lookup_matrix, lower_operand, precision=lax.Precision.HIGHEST
    )
    device_index = MATMUL_ACCURACY * (upper_operand - selected_operand)
    gu = lik - device_index
    region_part = jnp.einsum(
        "pr,cpg->crg", region_lookup_matrix, device_index, precision=lax.Precision.HIGHEST
    )
    xt_total, region_total = lax.psum((xt, region_part), "loan")
    gb = xt_total - F * b_own
    gv = region_total - MATMUL_ACCURACY * lower_operand
    return (gb, gu, gv)


def body(
    design,
    labels,
    pool_ids,
    pool_region_index,
    step_size,
    beta,
    pools,
    regions,
    beta_momentum,
    pool_momentum,
    region_momentum,
):
    half = 0.5 * step_size
    h2 = half[:, None]
    h3 = half[:, None, None]
    e2 = step_size[:, None]
    e3 = step_size[:, None, None]
    gb, gu, gv = gradient(design, labels, pool_ids, pool_region_index, beta, beta, pools, regions)
    mb = beta_momentum + h2 * gb
    mu = pool_momentum + h3 * gu
    mv = region_momentum + h3 * gv
    beta_next_own = beta + e2 * mb
    pools_next = pools + e3 * mu
    regions_next = regions + e3 * mv
    gb, gu, gv = gradient(
        design,
        labels,
        pool_ids,
        pool_region_index,
        beta_next_own,
        beta_next_own,
        pools_next,
        regions_next,
    )
    mb_next = mb + h2 * gb
    return (beta_next_own, pools_next, regions_next, mb_next, mu + h3 * gu, mv + h3 * gv)


def solution(mesh):
    in_specs = (
        P(("grp", "loan"), "feat"),
        P(("grp", "loan")),
        P(("grp", "loan")),
        P(("grp", "loan")),
        P("grp"),
        P("grp", "feat"),
        P("grp", "loan", "feat"),
        P("grp", None, "feat"),
        P("grp", "feat"),
        P("grp", "loan", "feat"),
        P("grp", None, "feat"),
    )
    out_specs = (
        P("grp", "feat"),
        P("grp", "loan", "feat"),
        P("grp", None, "feat"),
        P("grp", "feat"),
        P("grp", "loan", "feat"),
        P("grp", None, "feat"),
    )
    return jax.shard_map(body, mesh=mesh, in_specs=in_specs, out_specs=out_specs, check_vma=False)
```

profile of v0, /device:TPU:0, one launch (start us, length us, event | category | flops | bytes accessed | tf_op | source)
XLA Modules:
  0.0 294.1 jit_solution(9873602378691993713)
XLA Ops:
  8.0 11.7 %slice.4 = bf16[2048,64]{1,0:T(8,128)(2,1)S(1)} slice(bf16[2048,1024]{1,0:T(8,128)(2,1)} %param.13), slice={[0:2048:1], [0:1024:16]} | slice | bytes 524288 | tf_op jit(solution)/shard_map/slice | solution.py:17
  20.1 50.2 %gather_fusion = f32[2048,16,64]{2,0,1:T(8,128)} fusion(f32[16,64,64]{2,1,0:T(8,128)S(1)} %copy-done, s32[2048]{0:T(1024)S(1)} %fusion.46), kind=kCustom, calls=%fused_computation.clone | custom fusion | bytes 16785408 | tf_op jit(solution)/shard_map/jit(_take)/gather | solution.py:27
  70.3 9.0 %fusion.1 = f32[2048,16]{0,1:T(8,128)S(1)} fusion(f32[2048,16,64]{2,0,1:T(8,128)} %gather_fusion, f32[2048,64]{1,0:T(8,128)S(1)} %copy.49, pred[2048]{0:T(1024)(128)(4,1)S(1)} %get-tuple-element.11), kind=kLoop, calls=%fused_computation.5 | loop fusion | flops 6258688 | bytes 9046016 | tf_op jit(solution)/shard_map/ng,cng->cn/dot_general | solution.py:28
  79.4 1.9 convolution_add_fusion.1
  81.7 0.8 dynamic-slice_convert_fusion
  82.5 1.3 convolution_bitcast_fusion.2
  83.8 19.9 %reduce-scatter.3.cloned.1.call-done = f32[16,512]{1,0:T(8,128)} async-done(((f32[16,2048]{1,0:T(8,128)}), f32[16,512]{1,0:T(8,128)}) %reduce-scatter.3.cloned.1.call-update) | async-done | bytes 32784 | tf_op jit(solution)/shard_map/reduce_scatter | solution.py:31
  103.7 0.8 subtract_convert_fusion.1
  104.5 5.2 %all_gather.6 = bf16[16,2048]{1,0:T(8,128)(2,1)S(1)} all-gather(bf16[16,512]{1,0:T(8,128)(2,1)S(1)} %subtract_convert_fusion.1), channel_id=1, replica_groups=mesh['grp'=2,'loan'=4,'feat'=4] {'feat'}, dimensions={1}, use_global_device_ids=true | all-gather | bytes 81920 | tf_op jit(solution)/shard_map/all_gather | solution.py:34
  109.7 3.5 %fusion.47 = f32[16,1024]{1,0:T(8,128)} fusion(bf16[16,2048]{1,0:T(8,128)(2,1)S(1)} %all_gather.6, bf16[2048,1024]{1,0:T(8,128)(2,1)} %param.13), kind=kOutput, calls=%fused_computation.57 | convolution fusion | flops 67108864 | bytes 4325376 | tf_op jit(solution)/shard_map/dot_general | solution.py:35
  114.2 38.8 %all-reduce.7.cloned.1.call-done = (f32[16,1024]{1,0:T(8,128)}, f32[16,64,64]{2,1,0:T(8,128)}) async-done(((f32[16,1024]{1,0:T(8,128)}, f32[16,64,64]{2,1,0:T(8,128)}), (f32[16,1024]{1,0:T(8,128)}, f32[16,64,64]{2,1,0:T(8,128)})) %all-reduce.7.cloned.1.call-update) | async-done | bytes 327696 | tf_op jit(solution)/shard_map/psum | solution.py:54
  152.9 3.7 %multiply_add_fusion.1 = (f32[16,64,64]{2,1,0:T(8,128)}, f32[16,64,64]{2,1,0:T(8,128)S(1)}, f32[16,64,64]{2,1,0:T(8,128)}) fusion(f32[16,64,64]{2,1,0:T(8,128)} %param.20, f32[16]{0:T(128)} %param.17, f32[16,64,64]{2,1,0:T(8,128)} %param.23, f32[16,64,64]{2,1,0:T(8,128)} %get-tuple-element.10, f32[16]{0:T(128)S(1)} %broadcast_multiply_fusion, ...), kind=kOutput, calls=%fused_computation.33 | convolution fusion | flops 271253504 | bytes 2949248 | tf_op jit(solution)/shard_map/cnp,ng->cpg/dot_general | solution.py:42
  157.4 20.7 %gather_fusion.1 = f32[2048,16,64]{2,1,0:T(8,128)} fusion(f32[16,64,64]{2,0,1:T(8,128)S(1)} %copy.27, s32[2048]{0:T(1024)S(1)} %fusion.46), kind=kCustom, calls=%fused_computation.1.clone | custom fusion | bytes 16785408 | tf_op jit(solution)/shard_map/jit(_take)/gather | solution.py:27
  178.2 32.8 %fusion = f32[2048,16]{1,0:T(8,128)S(1)} fusion(f32[2048,16,64]{2,1,0:T(8,128)} %gather_fusion.1, f32[2048,64]{1,0:T(8,128)S(1)} %copy.49, pred[2048]{0:T(1024)(128)(4,1)S(1)} %copy-done.14), kind=kLoop, calls=%fused_computation.3 | loop fusion | flops 6258688 | bytes 9046016
  211.4 4.1 %convolution_add_fusion = f32[16,2048]{1,0:T(8,128)} fusion(bf16[2048,1024]{1,0:T(8,128)(2,1)} %param.13, f32[2048,16]{0,1:T(8,128)S(1)} %copy.43, f32[16,1024]{1,0:T(8,128)S(1)} %multiply_add_fusion.5), kind=kOutput, calls=%fused_computation.10 | convolution fusion | flops 67158016 | bytes 4521984 | tf_op jit(solution)/shard_map/dot_general | solution.py:24
  216.0 1.3 convolution_bitcast_fusion
  217.3 17.3 %reduce-scatter.5.cloned.1.call-done = f32[16,512]{1,0:T(8,128)} async-done(((f32[16,2048]{1,0:T(8,128)}), f32[16,512]{1,0:T(8,128)}) %reduce-scatter.5.cloned.1.call-update) | async-done | bytes 32784 | tf_op jit(solution)/shard_map/reduce_scatter | solution.py:31
  234.6 0.8 subtract_convert_fusion
  235.4 5.2 %all_gather.7 = bf16[16,2048]{1,0:T(8,128)(2,1)S(1)} all-gather(bf16[16,512]{1,0:T(8,128)(2,1)S(1)} %subtract_convert_fusion), channel_id=1, replica_groups=mesh['grp'=2,'loan'=4,'feat'=4] {'feat'}, dimensions={1}, use_global_device_ids=true | all-gather | bytes 81920 | tf_op jit(solution)/shard_map/all_gather | solution.py:34
  240.6 3.5 %fusion.48 = f32[16,1024]{1,0:T(8,128)} fusion(bf16[16,2048]{1,0:T(8,128)(2,1)S(1)} %all_gather.7, bf16[2048,1024]{1,0:T(8,128)(2,1)} %param.13), kind=kOutput, calls=%fused_computation.58 | convolution fusion | flops 67108864 | bytes 4325376 | tf_op jit(solution)/shard_map/dot_general | solution.py:35
  244.1 3.2 %fusion.25 = f32[16,64,64]{2,1,0:T(8,128)} fusion(f32[16,64,64]{2,1,0:T(8,128)} %get-tuple-element.15, f32[16,64,64]{2,1,0:T(8,128)S(1)} %fusion.31, bf16[16,2048]{1,0:T(8,128)(2,1)S(1)} %all_gather.7, bf16[2048,64]{0,1:T(8,128)(2,1)S(1)} %fusion.34, bf16[2048,64]{1,0:T(8,128)(2,1)S(1)} %slice.4, f32[16]{0:T(128)S(1)} %broadcast_multiply_fusion), kind=kOutput, calls=%fused_computation.21 | convolution fusion | flops 270729216 | bytes 1376320 | tf_op jit(solution)/shard_map/cnp,ng->cpg/dot_general | solution.py:42
  247.3 36.6 %all-reduce.5.cloned.1.call-done = (f32[16,1024]{1,0:T(8,128)}, f32[16,64,64]{2,1,0:T(8,128)}) async-done(((f32[16,1024]{1,0:T(8,128)}, f32[16,64,64]{2,1,0:T(8,128)}), (f32[16,1024]{1,0:T(8,128)}, f32[16,64,64]{2,1,0:T(8,128)})) %all-reduce.5.cloned.1.call-update) | async-done | bytes 327696 | tf_op jit(solution)/shard_map/psum | solution.py:54
  283.9 1.5 multiply_add_fusion.4
  285.4 2.2 multiply_add_fusion
  (59 shorter events, 4.4 us)
Async XLA Ops:
  7.2 12.9 %copy-start = (f32[16,64,64]{2,1,0:T(8,128)S(1)}, f32[16,64,64]{2,1,0:T(8,128)}, u32[]{:S(2)}) copy-start(f32[16,64,64]{2,1,0:T(8,128)} %param.19) | copy-start | bytes 786436
  7.2 96.5 %reduce-scatter.3.cloned.1.call-start = ((), (), s32[]{:S(2)}) async-start(), calls=%async_computation.2 | async-start | bytes 163840 | tf_op jit(solution)/shard_map/reduce_scatter | solution.py:31
  8.0 62.4 %copy-start.13 = (pred[2048]{0:T(1024)(128)(4,1)}, pred[2048]{0:T(1024)(128)(4,1)S(1)}, u32[]{:S(2)}) copy-start(pred[2048]{0:T(1024)(128)(4,1)S(1)} %get-tuple-element.11) | copy-start | bytes 6148
  70.3 9.0 %copy-start.1 = (bf16[2048,1024]{1,0:T(8,128)(2,1)S(1)}, bf16[2048,1024]{1,0:T(8,128)(2,1)}, u32[]{:S(2)}) copy-start(bf16[2048,1024]{1,0:T(8,128)(2,1)} %param.13) | copy-start | bytes 12582916
  70.3 9.0 %copy-start.7 = (f32[16,1024]{1,0:T(8,128)S(1)}, f32[16,1024]{1,0:T(8,128)}, u32[]{:S(2)}) copy-start(f32[16,1024]{1,0:T(8,128)} %param.18) | copy-start | bytes 196612
  79.3 2.0 copy-start.4
  79.3 2.0 copy-start.17
  81.2 71.7 %all-reduce.7.cloned.1.call-start = ((), (), s32[]{:S(2)}) async-start(), calls=%async_computation.5 | async-start | bytes 1179648 | tf_op jit(solution)/shard_map/psum | solution.py:54
  82.5 21.2 %copy-start.15 = (f32[512]{0:T(512)}, f32[512]{0:T(512)S(1)}, u32[]{:S(2)}) copy-start(f32[512]{0:T(512)S(1)} %dynamic-slice_convert_fusion) | copy-start | bytes 6148
  113.2 121.4 %reduce-scatter.5.cloned.1.call-start = ((), (), s32[]{:S(2)}) async-start(), calls=%async_computation.3 | async-start | bytes 163840 | tf_op jit(solution)/shard_map/reduce_scatter | solution.py:31
  156.6 0.8 copy-start.2
  157.4 20.7 %copy-start.14 = (pred[2048]{0:T(1024)(128)(4,1)S(1)}, pred[2048]{0:T(1024)(128)(4,1)}, u32[]{:S(2)}) copy-start(pred[2048]{0:T(1024)(128)(4,1)} %copy-done.13) | copy-start | bytes 6148
  178.2 33.1 %copy-start.10 = (f32[16,1024]{1,0:T(8,128)S(1)}, f32[16,1024]{1,0:T(8,128)}, u32[]{:S(2)}) copy-start(f32[16,1024]{1,0:T(8,128)} %param.21) | copy-start | bytes 196612
  178.2 33.1 %copy-start.11 = (f32[16,1024]{1,0:T(8,128)S(1)}, f32[16,1024]{1,0:T(8,128)}, u32[]{:S(2)}) copy-start(f32[16,1024]{1,0:T(8,128)} %get-tuple-element.9) | copy-start | bytes 196612
  178.2 33.1 %copy-start.19 = (f32[16]{0:T(128)S(1)}, f32[16]{0:T(128)}, u32[]{:S(2)}) copy-start(f32[16]{0:T(128)} %param.17) | copy-start | bytes 196
  211.0 4.6 %copy-start.3 = (f32[16,64,64]{2,1,0:T(8,128)S(1)}, f32[16,64,64]{2,1,0:T(8,128)}, u32[]{:S(2)}) copy-start(f32[16,64,64]{2,1,0:T(8,128)} %copy-done.2) | copy-start | bytes 786436
  211.0 4.6 %copy-start.6 = (f32[16,64,64]{2,1,0:T(8,128)S(1)}, f32[16,64,64]{2,1,0:T(8,128)}, u32[]{:S(2)}) copy-start(f32[16,64,64]{2,1,0:T(8,128)} %get-tuple-element.13) | copy-start | bytes 786436
  211.0 4.6 %copy-start.18 = (s32[64]{0:T(128)S(1)}, s32[64]{0:T(128)}, u32[]{:S(2)}) copy-start(s32[64]{0:T(128)} %param.16) | copy-start | bytes 772
  211.0 23.6 %copy-start.16 = (f32[512]{0:T(512)S(1)}, f32[512]{0:T(512)}, u32[]{:S(2)}) copy-start(f32[512]{0:T(512)} %copy-done.15) | copy-start | bytes 6148
  211.4 72.5 %copy-start.8 = (f32[16,1024]{1,0:T(8,128)}, f32[16,1024]{1,0:T(8,128)S(1)}, u32[]{:S(2)}) copy-start(f32[16,1024]{1,0:T(8,128)S(1)} %multiply_add_fusion.5) | copy-start | bytes 196612
  215.5 68.4 %all-reduce.5.cloned.1.call-start = ((), (), s32[]{:S(2)}) async-start(), calls=%async_computation.4 | async-start | bytes 1179648 | tf_op jit(solution)/shard_map/psum | solution.py:54
  244.1 39.8 %copy-start.12 = (f32[16,1024]{1,0:T(8,128)S(1)}, f32[16,1024]{1,0:T(8,128)}, u32[]{:S(2)}) copy-start(f32[16,1024]{1,0:T(8,128)} %get-tuple-element.9) | copy-start | bytes 196612
  244.1 41.3 %copy-start.5 = (f32[16,64,64]{2,1,0:T(8,128)S(1)}, f32[16,64,64]{2,1,0:T(8,128)}, u32[]{:S(2)}) copy-start(f32[16,64,64]{2,1,0:T(8,128)} %param.20) | copy-start | bytes 786436
  244.1 41.3 %copy-start.9 = (f32[16,64,64]{2,1,0:T(8,128)S(1)}, f32[16,64,64]{2,1,0:T(8,128)}, u32[]{:S(2)}) copy-start(f32[16,64,64]{2,1,0:T(8,128)} %param.23) | copy-start | bytes 786436
Sparse Core Ops, SparseCore 0:
  81.4 22.2 reduce-scatter.2
  113.3 39.5 all-reduce.6
  215.6 18.9 reduce-scatter.4
  244.3 39.5 all-reduce.4
where the time goes:
time: 295 us; the launch traced here: 294 us
  waiting for transfers between devices  113 us (38%)
  local copies, waits for them, and re-layouts  84.2 us (29%)
  other arithmetic  49.3 us (17%)
  matrix products  23.1 us (8%)
  between operations  14 us (5%)
  blocking collectives  10.5 us (4%)
    psum x2, waiting for transfers between devices, gradient(): xt_total, region_total = lax.psum((xt, region_part), 'loan')  75.4 us
    gather x2, local copies, waits for them, and re-layouts, gradient(): chosen = jnp.take(upper_operand, local_ids, axis=1)  71 us
    reduce_scatter x2, waiting for transfers between devices, gradient(): lax.psum_scatter(partial_logit, 'feat', scatter_dimension=1, tiled=True)  37.2 us
    unnamed x1, other arithmetic  32.8 us
    slice x1, local copies, waits for them, and re-layouts, gradient(): slope_bf = design[:, ::stride]  11.7 us
    all_gather x2, blocking collectives, gradient(): resid = lax.all_gather(resid_share, 'feat', axis=1, tiled=True)  10.5 us
    dot_general x1, other arithmetic, gradient(): jnp.einsum('ng,cng->cn', slope_feats, chosen, precision=lax.Precision.HIG...  8.96 us
    dot_general x2, matrix products, gradient(): lax.dot_general(resid, design, (((1,), (0,)), ((), ())), preferred_elemen...  6.95 us
  transfers between devices with their start and end apart: 4, of which 4 were waited for; matrix products, arithmetic and copies ran while one was open for 3% of the time, Pallas kernels for 0%

commit v1 on v0

v1 whole, which is shorter than its diff:
```python
import jax
import jax.numpy as jnp
from jax import lax
from jax.experimental import pallas as pl
from jax.experimental.pallas import tpu as pltpu
from jax.sharding import PartitionSpec as P

PREC = 256.0
SCALE = 1.0 / 16.0
TILE = 256
VMEM_LIMIT = 24 * 1024 * 1024
NT = (((1,), (1,)), ((), ()))
NN = (((1,), (0,)), ((), ()))
F32 = jnp.float32
BF16 = jnp.bfloat16


def whole():
    return pl.BlockSpec(memory_space=pltpu.VMEM)


def params():
    return pltpu.CompilerParams(vmem_limit_bytes=VMEM_LIMIT)


def split_table(u):
    flat = u.reshape(u.shape[0] * u.shape[1], u.shape[2])
    high = flat.astype(BF16)
    low = (flat - high.astype(F32)).astype(BF16)
    return jnp.concatenate([high, low], axis=1)


def slope_term(table_ref, slopes, ids, chains, owned):
    tile = slopes.shape[1]
    stacked = jnp.concatenate([slopes, slopes], axis=0)
    sub = lax.broadcasted_iota(jnp.int32, (8, tile), 0)
    masks = [(sub + 8 * q) == ids for q in range(owned // 8)]
    rows = []
    few = 4
    for c in range(0, chains, few):
        part = lax.dot_general(
            table_ref[c * owned : (c + few) * owned, :], stacked, NN, preferred_element_type=F32
        ).reshape(few, owned, tile)
        for k in range(few):
            acc = jnp.zeros((8, tile), F32)
            for q in range(owned // 8):
                acc = jnp.where(masks[q], part[k, 8 * q : 8 * q + 8, :], acc)
            rows.append(jnp.sum(acc, axis=0, keepdims=True))
    return jnp.concatenate(rows, axis=0)


def in_hbm(x):
    return pltpu.with_memory_space_constraint(x, pltpu.HBM)


def tile_copies(source, target, sems):
    copies = []
    for t in range(source.shape[0] // TILE):
        rows = pl.ds(t * TILE, TILE)
        copies.append(pltpu.make_async_copy(source.at[rows], target.at[rows], sems.at[t]))
    for copy in copies:
        copy.start()
    return copies


def design_scratch(design):
    rows, feats = design.shape
    return [pltpu.VMEM((rows, feats), BF16), pltpu.SemaphoreType.DMA((rows // TILE,))]


def first_logits(design, ids, beta, pools, stride):
    rows, feats = design.shape
    chains, owned, slopes = pools.shape

    def kernel(design_hbm, ids_ref, beta_hbm, pools_hbm, slope_ref, part_ref, w, table, b_ref, u_ref, sem, kept, sems):
        small = [
            pltpu.make_async_copy(pools_hbm, u_ref, sem.at[0]),
            pltpu.make_async_copy(beta_hbm, b_ref, sem.at[1]),
        ]
        for copy in small:
            copy.start()
        copies = tile_copies(design_hbm, kept, sems)
        g = lax.broadcasted_iota(jnp.int32, (slopes, feats), 0)
        f = lax.broadcasted_iota(jnp.int32, (slopes, feats), 1)
        w[:slopes, :] = jnp.where(f == g * stride, 1.0, 0.0).astype(BF16)
        small[0].wait()
        table[...] = split_table(u_ref[...])
        small[1].wait()
        w[slopes:, :] = b_ref[...].astype(BF16)
        first = lax.axis_index("loan") * owned
        for t, copy in enumerate(copies):
            copy.wait()
            cols = slice(t * TILE, (t + 1) * TILE)
            both = lax.dot_general(w[...], kept[cols, :], NT, preferred_element_type=F32)
            slope = both[:slopes, :].astype(BF16)
            slope_ref[:, cols] = slope
            term = slope_term(table, slope, ids_ref[:, cols] - first, chains, owned)
            part_ref[:, cols] = (both[slopes:, :] + term) * SCALE

    return pl.pallas_call(
        kernel,
        in_specs=[pl.BlockSpec(memory_space=pl.ANY), whole()] + [pl.BlockSpec(memory_space=pl.ANY)] * 2,
        out_specs=[whole(), whole()],
        out_shape=[
            jax.ShapeDtypeStruct((slopes, rows), BF16),
            jax.ShapeDtypeStruct((chains, rows), F32),
        ],
        scratch_shapes=[
            pltpu.VMEM((slopes + chains, feats), BF16),
            pltpu.VMEM((chains * owned, 2 * slopes), BF16),
            pltpu.VMEM(beta.shape, F32),
            pltpu.VMEM(pools.shape, F32),
            pltpu.SemaphoreType.DMA((2,)),
        ]
        + design_scratch(design),
        compiler_params=params(),
        name="first_logits",
    )(in_hbm(design), ids, in_hbm(beta), in_hbm(pools))


def population_gradient(resid, design):
    def kernel(resid_ref, design_hbm, out_ref, kept, sems):
        total = None
        for t, copy in enumerate(tile_copies(design_hbm, kept, sems)):
            copy.wait()
            cols = slice(t * TILE, (t + 1) * TILE)
            part = lax.dot_general(
                resid_ref[:, cols], kept[cols, :], NN, preferred_element_type=F32
            )
            total = part if total is None else total + part
        out_ref[...] = SCALE * total

    return pl.pallas_call(
        kernel,
        in_specs=[whole(), pl.BlockSpec(memory_space=pl.ANY)],
        out_specs=whole(),
        out_shape=jax.ShapeDtypeStruct((resid.shape[0], design.shape[1]), F32),
        scratch_shapes=design_scratch(design),
        compiler_params=params(),
        name="population_gradient",
    )(resid, in_hbm(design))


def pool_sums(resid_ref, slope_ref, ids_ref, chains, owned):
    rows = resid_ref.shape[1]
    total = None
    sub = lax.broadcasted_iota(jnp.int32, (owned, TILE), 0)
    for t in range(rows // TILE):
        cols = slice(t * TILE, (t + 1) * TILE)
        mask = sub == ids_ref[:, cols] - lax.axis_index("loan") * owned
        resid = resid_ref[:, cols].astype(F32)
        table = jnp.concatenate(
            [jnp.where(mask, resid[c : c + 1, :], 0.0).astype(BF16) for c in range(chains)], axis=0
        )
        part = lax.dot_general(table, slope_ref[:, cols], NT, preferred_element_type=F32)
        total = part if total is None else total + part
    return total.reshape(chains, owned, slope_ref.shape[0])


def pool_step(resid, slope, ids, base, scale_pos, scale_mom, mom_base):
    chains, owned, slopes = base.shape
    rows = resid.shape[1]

    def kernel(resid_ref, slope_ref, ids_ref, base_ref, sp_ref, sm_ref, mb_ref, next_ref, half_ref, term_ref, table):
        lik = pool_sums(resid_ref, slope_ref, ids_ref, chains, owned)
        half = mb_ref[...] + sm_ref[...] * lik
        half_ref[...] = half
        ahead = base_ref[...] + sp_ref[...] * half
        next_ref[...] = ahead
        table[...] = split_table(ahead)
        for t in range(rows // TILE):
            cols = slice(t * TILE, (t + 1) * TILE)
            term_ref[:, cols] = slope_term(
                table,
                slope_ref[:, cols],
                ids_ref[:, cols] - lax.axis_index("loan") * owned,
                chains,
                owned,
            )

    return pl.pallas_call(
        kernel,
        in_specs=[whole()] * 7,
        out_specs=[whole()] * 3,
        out_shape=[
            jax.ShapeDtypeStruct(base.shape, F32),
            jax.ShapeDtypeStruct(base.shape, F32),
            jax.ShapeDtypeStruct((chains, rows), F32),
        ],
        scratch_shapes=[pltpu.VMEM((chains * owned, 2 * slopes), BF16)],
        compiler_params=params(),
        name="pool_step",
    )(resid, slope, ids, base, scale_pos, scale_mom, mom_base)


def pool_likelihood(resid, slope, ids, chains, owned):
    def kernel(resid_ref, slope_ref, ids_ref, out_ref):
        out_ref[...] = pool_sums(resid_ref, slope_ref, ids_ref, chains, owned)

    return pl.pallas_call(
        kernel,
        in_specs=[whole()] * 3,
        out_specs=whole(),
        out_shape=jax.ShapeDtypeStruct((chains, owned, slope.shape[0]), F32),
        compiler_params=params(),
        name="pool_likelihood",
    )(resid, slope, ids)


def next_logits(design, coef, term):
    def kernel(design_hbm, coef_ref, term_ref, out_ref, kept, sems):
        coef16 = coef_ref[...].astype(BF16)
        for t, copy in enumerate(tile_copies(design_hbm, kept, sems)):
            copy.wait()
            cols = slice(t * TILE, (t + 1) * TILE)
            linear = lax.dot_general(coef16, kept[cols, :], NT, preferred_element_type=F32)
            out_ref[:, cols] = SCALE * (term_ref[:, cols] + linear)

    return pl.pallas_call(
        kernel,
        in_specs=[pl.BlockSpec(memory_space=pl.ANY), whole(), whole()],
        out_specs=whole(),
        out_shape=jax.ShapeDtypeStruct(term.shape, F32),
        scratch_shapes=design_scratch(design),
        compiler_params=params(),
        name="next_logits",
    )(in_hbm(design), coef, term)


def ahead_by(k, size, stride, group):
    perm = []
    for i in range(size):
        digit = (i // stride) % group
        perm.append((i, i + ((digit + k) % group - digit) * stride))
    return perm


def total_over(x, axis):
    size = lax.axis_size(axis)
    stride = 1
    while stride < size:
        group = min(4, size // stride)
        own = lax.optimization_barrier(x.astype(jnp.float16))
        parts = [own] + [
            lax.ppermute(own, axis, ahead_by(k, size, stride, group)) for k in range(1, group)
        ]
        parts = [p.astype(F32) for p in parts]
        x = parts[0] + parts[1] if group == 2 else (parts[0] + parts[2]) + (parts[1] + parts[3])
        stride *= group
    return x


def shared_sum(x, axis):
    size = lax.axis_size(axis)
    me = lax.axis_index(axis)
    width = x.shape[1] // size
    x = lax.optimization_barrier(x.astype(jnp.float16))

    def block(k):
        return lax.dynamic_slice_in_dim(x, lax.rem(me + k, size) * width, width, 1)

    mine = block(0).astype(F32)
    for k in range(1, size):
        mine = mine + lax.ppermute(block(k), axis, ahead_by(k, size, 1, size)).astype(F32)
    mine = lax.optimization_barrier(mine.astype(jnp.float16))
    found = [mine] + [lax.ppermute(mine, axis, ahead_by(k, size, 1, size)) for k in range(1, size)]
    back = jnp.concatenate(found[::-1], axis=1)
    return jnp.roll(back, (me + 1) * width, axis=1).astype(F32)


def couple(x):
    return jnp.concatenate(jnp.split(x, 2, axis=0), axis=2)


def uncouple(x):
    return jnp.concatenate(jnp.split(x, 2, axis=2), axis=0)


def residual(part, labels):
    logit = total_over(part, "feat") * (1.0 / SCALE)
    return (labels.astype(F32)[None, :] - jax.nn.sigmoid(logit)).astype(BF16)


def body(
    design,
    labels,
    pool_ids,
    pool_region_index,
    step_size,
    beta,
    pools,
    regions,
    beta_momentum,
    pool_momentum,
    region_momentum,
):
    rows, feats = design.shape
    chains, owned, slopes = pools.shape
    n_regions = regions.shape[1]
    total_feats = float(feats * lax.axis_size("feat"))
    half = 0.5 * step_size
    h2, h3 = half[:, None], half[:, None, None]
    e2, e3 = step_size[:, None], step_size[:, None, None]
    ids = pool_ids[None, :]

    slope, part = first_logits(design, ids, beta, pools, feats // slopes)

    lookup = (
        pool_region_index[:, None] == jnp.arange(n_regions, dtype=jnp.int32)[None, :]
    ).astype(F32)
    chosen = jnp.einsum("pr,crg->cpg", lookup, regions, precision=lax.Precision.HIGHEST)
    dev = PREC * (pools - chosen)
    counts = jnp.sum(lookup, axis=0)[None, :, None]
    region_dev = jnp.einsum("pr,cpg->crg", lookup, dev, precision=lax.Precision.HIGHEST)
    counts = jnp.broadcast_to(counts, (1, n_regions, 2 * slopes))
    mom_base = pool_momentum - h3 * dev

    resid = residual(part, labels)
    gb = population_gradient(resid, design)
    resid, gb = lax.optimization_barrier((resid, gb))
    pools_next, pool_half, term = pool_step(
        resid,
        slope,
        ids,
        pools,
        jnp.broadcast_to(e3, (chains, 1, slopes)),
        jnp.broadcast_to(h3, (chains, 1, slopes)),
        mom_base,
    )
    gb = total_over(gb, "loan") * (1.0 / SCALE) - total_feats * beta
    beta_half = beta_momentum + h2 * gb
    beta_next = beta + e2 * beta_half

    part = next_logits(design, beta_next, term)
    moved = jnp.einsum("pr,cpg->crg", lookup, e3 * pool_half, precision=lax.Precision.HIGHEST)
    shared = jnp.concatenate([couple(region_dev), couple(moved), counts], axis=0)
    shared = shared_sum(SCALE * shared, "loan") * (1.0 / SCALE)
    pairs = chains // 2
    region_dev, moved = uncouple(shared[:pairs]), uncouple(shared[pairs : 2 * pairs])
    counts = shared[2 * pairs :, :, :slopes]
    region_half = region_momentum + h3 * (region_dev - PREC * regions)
    regions_next = regions + e3 * region_half

    resid = residual(part, labels)
    gb = population_gradient(resid, design)
    resid, gb = lax.optimization_barrier((resid, gb))
    lik = pool_likelihood(resid, slope, ids, chains, owned)
    gb = total_over(gb, "loan") * (1.0 / SCALE) - total_feats * beta_next
    beta_out = beta_half + h2 * gb

    chosen = jnp.einsum("pr,crg->cpg", lookup, regions_next, precision=lax.Precision.HIGHEST)
    pool_out = pool_half + h3 * (lik - PREC * (pools_next - chosen))
    gv = region_dev + PREC * (moved - counts * (regions_next - regions)) - PREC * regions_next
    region_out = region_half + h3 * gv
    return (beta_next, pools_next, regions_next, beta_out, pool_out, region_out)


def solution(mesh):
    in_specs = (
        P(("grp", "loan"), "feat"),
        P(("grp", "loan")),
        P(("grp", "loan")),
        P(("grp", "loan")),
        P("grp"),
        P("grp", "feat"),
        P("grp", "loan", "feat"),
        P("grp", None, "feat"),
        P("grp", "feat"),
        P("grp", "loan", "feat"),
        P("grp", None, "feat"),
    )
    out_specs = (
        P("grp", "feat"),
        P("grp", "loan", "feat"),
        P("grp", None, "feat"),
        P("grp", "feat"),
        P("grp", "loan", "feat"),
        P("grp", None, "feat"),
    )
    return jax.shard_map(body, mesh=mesh, in_specs=in_specs, out_specs=out_specs, check_vma=False)
```

time: 295 us -> 64.8 us (0.22)
  waiting for transfers between devices: 113 us -> 8.04 us
  local copies, waits for them, and re-layouts: 84.2 us -> 1.61 us
  other arithmetic: 49.3 us -> 2.57 us
  starting transfers between devices: 0.34 us -> 24.8 us
  Pallas kernels: 0 us -> 23.7 us
  matrix products: 23.1 us -> 2.73 us
  between operations: 14 us -> 1.07 us
  blocking collectives: 10.5 us -> 0 us
    psum x2 -> x0, waiting for transfers between devices: 75.4 us -> none  [gradient(): xt_total, region_total = lax.psum((xt, region_part), 'loan')]
    gather x2 -> x0, local copies, waits for them, and re-layouts: 71 us -> none  [gradient(): chosen = jnp.take(upper_operand, local_ids, axis=1)]
    reduce_scatter x2 -> x0, waiting for transfers between devices: 37.2 us -> none  [gradient(): lax.psum_scatter(partial_logit, 'feat', scatter_dimension=1, tiled=True)]
    unnamed x1 -> x0, other arithmetic: 32.8 us -> none
    ppermute x0 -> x18, starting transfers between devices: none -> 24.8 us  [the longest x12 14.6 us: total_over(): lax.ppermute(own, axis, ahead_by(k, size, stride, group))]
    pallas_call x0 -> x6, Pallas kernels: none -> 23.7 us  [the longest x1 8.82 us: first_logits(): pl.pallas_call(kernel, in_specs=[pl.BlockSpec(memory_space=pl.ANY), whole...]
    dot_general x10 -> x4, matrix products: 23.1 us -> 2.73 us  [the longest x1 1.3 us: body(): jnp.einsum('pr,crg->cpg', lookup, regions_next, precision=lax.Precision.H...]
    slice x1 -> x0, local copies, waits for them, and re-layouts: 11.7 us -> none  [gradient(): slope_bf = design[:, ::stride]]
  transfers between devices with their start and end apart: 4 -> 18, of which waited for: 4 -> 5; matrix products, arithmetic and copies ran while one was open for 3% -> 5% of each run, Pallas kernels for 0% -> 13%
where the time goes in v1:
time: 64.8 us; the launch traced here: 64.5 us
  starting transfers between devices  24.8 us (38%)
  Pallas kernels  23.7 us (37%)
  waiting for transfers between devices  8.04 us (12%)
  matrix products  2.73 us (4%)
  other arithmetic  2.57 us (4%)
  local copies, waits for them, and re-layouts  1.61 us (2%)
  between operations  1.07 us (2%)
    ppermute x12, starting transfers between devices, total_over(): lax.ppermute(own, axis, ahead_by(k, size, stride, group))  14.6 us
    pallas_call x1, Pallas kernels, first_logits(): pl.pallas_call(kernel, in_specs=[pl.BlockSpec(memory_space=pl.ANY), whole...  8.82 us
    ppermute x3, starting transfers between devices, shared_sum(): lax.ppermute(mine, axis, ahead_by(k, size, 1, size))  5.33 us
    ppermute x3, waiting for transfers between devices, shared_sum(): lax.ppermute(mine, axis, ahead_by(k, size, 1, size))  5.3 us
    pallas_call x2, Pallas kernels, population_gradient(): pl.pallas_call(kernel, in_specs=[whole(), pl.BlockSpec(memory_space=pl.AN...  4.9 us
    ppermute x3, starting transfers between devices, shared_sum(): lax.ppermute(block(k), axis, ahead_by(k, size, 1, size)).astype(F32)  4.89 us
    pallas_call x1, Pallas kernels, pool_step(): pl.pallas_call(kernel, in_specs=[whole()] * 7, out_specs=[whole()] * 3, o...  4.5 us
    pallas_call x1, Pallas kernels, next_logits(): pl.pallas_call(kernel, in_specs=[pl.BlockSpec(memory_space=pl.ANY), whole...  4.26 us
  transfers between devices with their start and end apart: 18, of which 5 were waited for; matrix products, arithmetic and copies ran while one was open for 5% of the time, Pallas kernels for 13%

profile of v1, /device:TPU:0, one launch (start us, length us, event | category | flops | bytes accessed | tf_op | source)
XLA Modules:
  0.0 64.5 jit_solution(8566581858406750635)
XLA Ops:
  0.7 0.7 %copy-done.2 = s32[2048]{0:T(1024)S(1)} copy-done((s32[2048]{0:T(1024)S(1)}, s32[2048]{0:T(1024)}, u32[]{:S(2)}) %copy-start.2) | copy-done | bytes 8216
  1.4 8.8 %first_logits.1 = (bf16[64,2048]{1,0:T(8,128)(2,1)S(1)}, f32[16,2048]{1,0:T(8,128)S(1)}) custom-call(bf16[2048,1024]{1,0:T(8,128)(2,1)} %design_hbm.7, s32[1,2048]{1,0:T(1,128)S(1)} %bitcast.35, f32[16,1024]{1,0:T(8,128)} %beta_hbm.1, f32[16,64,64]{2,1,0:T(8,128)} %base_ref.1), custom_call_target="tpu_custom_call" | custom-call | tf_op jit(solution)/shard_map/first_logits/pallas_call | solution.py:100
  10.3 2.4 %collective-permute-start.2 = (f16[16,2048]{1,0:T(8,128)(2,1)S(1)}, f16[16,2048]{1,0:T(8,128)(2,1)S(1)}, u32[]{:S(2)}, u32[]{:S(2)}) collective-permute-start(f16[16,2048]{1,0:T(8,128)(2,1)S(1)} %convert_element_type.95), channel_id=1, source_target_pairs={{0,3},{1,0},{2,1},{3,2},{4,7},{5,4},{6,5},{7,6},{8,11},{9,8},{10,9... | collective-permute-start | bytes 196616 | tf_op jit(solution)/shard_map/ppermute | solution.py:245
  12.7 1.1 %collective-permute-start = (f16[16,2048]{1,0:T(8,128)(2,1)S(1)}, f16[16,2048]{1,0:T(8,128)(2,1)S(1)}, u32[]{:S(2)}, u32[]{:S(2)}) collective-permute-start(f16[16,2048]{1,0:T(8,128)(2,1)S(1)} %convert_element_type.95), channel_id=1, source_target_pairs={{0,2},{1,3},{2,0},{3,1},{4,6},{5,7},{6,4},{7,5},{8,10},{9,11},{10,... | collective-permute-start | bytes 196616 | tf_op jit(solution)/shard_map/ppermute | solution.py:245
  15.1 1.4 %collective-permute-done.1 = f16[16,2048]{1,0:T(8,128)(2,1)S(1)} collective-permute-done((f16[16,2048]{1,0:T(8,128)(2,1)S(1)}, f16[16,2048]{1,0:T(8,128)(2,1)S(1)}, u32[]{:S(2)}, u32[]{:S(2)}) %collective-permute-start.1) | collective-permute-done | bytes 65568 | tf_op jit(solution)/shard_map/ppermute | solution.py:245
  16.5 1.1 %collective-permute-done = f16[16,2048]{1,0:T(8,128)(2,1)S(1)} collective-permute-done((f16[16,2048]{1,0:T(8,128)(2,1)S(1)}, f16[16,2048]{1,0:T(8,128)(2,1)S(1)}, u32[]{:S(2)}, u32[]{:S(2)}) %collective-permute-start) | collective-permute-done | bytes 65568 | tf_op jit(solution)/shard_map/ppermute | solution.py:245
  17.7 2.4 %population_gradient.2 = f32[16,1024]{1,0:T(8,128)S(1)} custom-call(bf16[16,2048]{1,0:T(8,128)(2,1)S(1)} %subtract_convert_fusion.1.resid_ref, bf16[2048,1024]{1,0:T(8,128)(2,1)} %design_hbm.7), custom_call_target="tpu_custom_call" | custom-call | tf_op jit(solution)/shard_map/population_gradient/pallas_call | solution.py:133
  20.2 3.7 %collective-permute-start.5 = (f16[16,1024]{1,0:T(8,128)(2,1)S(1)}, f16[16,1024]{1,0:T(8,128)(2,1)S(1)}, u32[]{:S(2)}, u32[]{:S(2)}) collective-permute-start(f16[16,1024]{1,0:T(8,128)(2,1)S(1)} %convert_element_type.101), channel_id=1, source_target_pairs={{0,12},{4,0},{8,4},{12,8},{1,13},{5,1},{9,5},{13,9},{2,14},{6,2},{... | collective-permute-start | bytes 98312 | tf_op jit(solution)/shard_map/ppermute | solution.py:245
  23.9 1.0 %collective-permute-start.3 = (f16[16,1024]{1,0:T(8,128)(2,1)S(1)}, f16[16,1024]{1,0:T(8,128)(2,1)S(1)}, u32[]{:S(2)}, u32[]{:S(2)}) collective-permute-start(f16[16,1024]{1,0:T(8,128)(2,1)S(1)} %convert_element_type.101), channel_id=1, source_target_pairs={{0,8},{4,12},{8,0},{12,4},{1,9},{5,13},{9,1},{13,5},{2,10},{6,14},... | collective-permute-start | bytes 98312 | tf_op jit(solution)/shard_map/ppermute | solution.py:245
  25.0 4.5 %pool_step.1 = (f32[16,64,64]{2,1,0:T(8,128)}, f32[16,64,64]{2,1,0:T(8,128)S(1)}, f32[16,2048]{1,0:T(8,128)S(1)}) custom-call(bf16[16,2048]{1,0:T(8,128)(2,1)S(1)} %subtract_convert_fusion.1.resid_ref, bf16[64,2048]{1,0:T(8,128)(2,1)S(1)} %get-tuple-element.18.slope_ref, s32[1,2048]{1,0:T(1,128)S(1)} %bitcast.36, f32[16,64,64]{2,1,0:T(8,128)S(1)} %copy-done, ...), custom_call_target="tpu_custom_call" | custom-call | tf_op jit(solution)/shard_map/pool_step/pallas_call | solution.py:181
  30.6 4.3 %next_logits.1 = f32[16,2048]{1,0:T(8,128)S(1)} custom-call(bf16[2048,1024]{1,0:T(8,128)(2,1)} %design_hbm.7, f32[16,1024]{1,0:T(8,128)S(1)} %multiply_add_fusion.3.coef_ref, f32[16,2048]{1,0:T(8,128)S(1)} %get-tuple-element.21.term_ref), custom_call_target="tpu_custom_call" | custom-call | tf_op jit(solution)/shard_map/next_logits/pallas_call | solution.py:219
  35.4 1.4 %collective-permute-start.12 = (f16[16,2048]{1,0:T(8,128)(2,1)S(1)}, f16[16,2048]{1,0:T(8,128)(2,1)S(1)}, u32[]{:S(2)}, u32[]{:S(2)}) collective-permute-start(f16[16,2048]{1,0:T(8,128)(2,1)S(1)} %convert_element_type.114), channel_id=1, source_target_pairs={{0,2},{1,3},{2,0},{3,1},{4,6},{5,7},{6,4},{7,5},{8,10},{9,11},{10,... | collective-permute-start | bytes 196616 | tf_op jit(solution)/shard_map/ppermute | solution.py:245
  36.9 2.9 %collective-permute-start.8 = (f16[17,16,128]{2,1,0:T(8,128)(2,1)S(1)}, f16[17,16,128]{2,1,0:T(8,128)(2,1)S(1)}, u32[]{:S(2)}, u32[]{:S(2)}) collective-permute-start(f16[17,16,128]{2,1,0:T(8,128)(2,1)S(1)} %get-tuple-element.35), channel_id=1, source_target_pairs={{0,12},{4,0},{8,4},{12,8},{1,13},{5,1},{9,5},{13,9},{2,14},{6,2},{... | collective-permute-start | bytes 208904 | tf_op jit(solution)/shard_map/ppermute | solution.py:264
  39.7 2.0 %collective-permute-start.7 = (f16[17,16,128]{2,1,0:T(8,128)(2,1)S(1)}, f16[17,16,128]{2,1,0:T(8,128)(2,1)S(1)}, u32[]{:S(2)}, u32[]{:S(2)}) collective-permute-start(f16[17,16,128]{2,1,0:T(8,128)(2,1)S(1)} %get-tuple-element.36), channel_id=1, source_target_pairs={{0,8},{4,12},{8,0},{12,4},{1,9},{5,13},{9,1},{13,5},{2,10},{6,14},... | collective-permute-start | bytes 208904 | tf_op jit(solution)/shard_map/ppermute | solution.py:264
  41.9 2.5 %population_gradient.3 = f32[16,1024]{1,0:T(8,128)S(1)} custom-call(bf16[16,2048]{1,0:T(8,128)(2,1)S(1)} %subtract_convert_fusion.resid_ref, bf16[2048,1024]{1,0:T(8,128)(2,1)} %design_hbm.7), custom_call_target="tpu_custom_call" | custom-call | tf_op jit(solution)/shard_map/population_gradient/pallas_call | solution.py:133
  44.4 3.9 %collective-permute-start.17 = (f16[16,1024]{1,0:T(8,128)(2,1)S(1)}, f16[16,1024]{1,0:T(8,128)(2,1)S(1)}, u32[]{:S(2)}, u32[]{:S(2)}) collective-permute-start(f16[16,1024]{1,0:T(8,128)(2,1)S(1)} %convert_element_type.120), channel_id=1, source_target_pairs={{0,12},{4,0},{8,4},{12,8},{1,13},{5,1},{9,5},{13,9},{2,14},{6,2},{... | collective-permute-start | bytes 98312 | tf_op jit(solution)/shard_map/ppermute | solution.py:245
  48.9 3.3 %collective-permute-start.9 = (f16[17,16,128]{2,1,0:T(8,128)(2,1)S(1)}, f16[17,16,128]{2,1,0:T(8,128)(2,1)S(1)}, u32[]{:S(2)}, u32[]{:S(2)}) collective-permute-start(f16[17,16,128]{2,1,0:T(8,128)(2,1)S(1)} %add_convert_fusion), channel_id=1, source_target_pairs={{0,12},{4,0},{8,4},{12,8},{1,13},{5,1},{9,5},{13,9},{2,14},{6,2},{... | collective-permute-start | bytes 208904 | tf_op jit(solution)/shard_map/ppermute | solution.py:266
  52.2 2.0 %collective-permute-start.10 = (f16[17,16,128]{2,1,0:T(8,128)(2,1)S(1)}, f16[17,16,128]{2,1,0:T(8,128)(2,1)S(1)}, u32[]{:S(2)}, u32[]{:S(2)}) collective-permute-start(f16[17,16,128]{2,1,0:T(8,128)(2,1)S(1)} %add_convert_fusion), channel_id=1, source_target_pairs={{0,8},{4,12},{8,0},{12,4},{1,9},{5,13},{9,1},{13,5},{2,10},{6,14},... | collective-permute-start | bytes 208904 | tf_op jit(solution)/shard_map/ppermute | solution.py:266
  54.2 1.2 %pool_likelihood.1 = f32[16,64,64]{2,1,0:T(8,128)S(1)} custom-call(bf16[16,2048]{1,0:T(8,128)(2,1)S(1)} %subtract_convert_fusion.resid_ref, bf16[64,2048]{1,0:T(8,128)(2,1)S(1)} %get-tuple-element.18.slope_ref, s32[1,2048]{1,0:T(1,128)S(1)} %bitcast.37), custom_call_target="tpu_custom_call" | custom-call | tf_op jit(solution)/shard_map/pool_likelihood/pallas_call | solution.py:200
  55.5 0.7 %multiply_add_fusion.2 = f32[16,1024]{1,0:T(8,128)} fusion(f32[16,1024]{1,0:T(8,128)S(1)} %multiply_add_fusion.3.coef_ref, f16[16,1024]{1,0:T(8,128)(2,1)S(1)} %collective-permute-done.17, f16[16,1024]{1,0:T(8,128)(2,1)S(1)} %collective-permute-done.16, f16[16,1024]{1,0:T(8,128)(2,1)S(1)} %collective-permute-done.15, ...), kind=kLoop, calls=%fused_computation.30 | loop fusion | flops 393216 | bytes 524352 | tf_op jit(solution)/shard_map/add | solution.py:349
  56.3 3.0 %collective-permute-done.10 = f16[17,16,128]{2,1,0:T(8,128)(2,1)S(1)} collective-permute-done((f16[17,16,128]{2,1,0:T(8,128)(2,1)S(1)}, f16[17,16,128]{2,1,0:T(8,128)(2,1)S(1)}, u32[]{:S(2)}, u32[]{:S(2)}) %collective-permute-start.10) | collective-permute-done | bytes 69664 | tf_op jit(solution)/shard_map/ppermute | solution.py:266
  59.3 2.3 %collective-permute-done.11 = f16[17,16,128]{2,1,0:T(8,128)(2,1)S(1)} collective-permute-done((f16[17,16,128]{2,1,0:T(8,128)(2,1)S(1)}, f16[17,16,128]{2,1,0:T(8,128)(2,1)S(1)}, u32[]{:S(2)}, u32[]{:S(2)}) %collective-permute-start.11) | collective-permute-done | bytes 69664 | tf_op jit(solution)/shard_map/ppermute | solution.py:266
  62.1 1.2 %fusion.11 = (f32[16,64,64]{2,1,0:T(8,128)}, f32[16,64,64]{2,1,0:T(8,128)S(1)}) fusion(f32[8,64,64]{2,1,0:T(8,128)S(1)} %get-tuple-element.27, f32[8,64,64]{2,1,0:T(8,128)S(1)} %get-tuple-element.28, f32[16,64,64]{2,1,0:T(8,128)S(1)} %copy-done.4, f32[16,64,64]{2,1,0:T(8,128)S(1)} %copy-done.9, f32[8,64,64]{2,1,0:T(8,128)S(1)} %get-tuple-element.29, ...), kind=kLoop, calls=%fused_computation.19 | loop fusion | flops 1114112 | bytes 1589376 | tf_op jit(solution)/shard_map/add | solution.py:354
  63.2 1.3 %fusion.5 = f32[16,64,64]{2,1,0:T(8,128)} fusion(f32[16,64,64]{2,1,0:T(8,128)S(1)} %get-tuple-element.20, f32[16,64,64]{2,1,0:T(8,128)S(1)} %pool_likelihood.1, f32[16,64,64]{2,1,0:T(8,128)S(1)} %copy-done.8, f32[16,64,64]{2,1,0:T(8,128)S(1)} %get-tuple-element.25, f32[16]{0:T(128)S(1)} %get-tuple-element.38, s32[64]{0:T(128)S(1)} %copy-done.11), kind=kOutput, calls=%fused_computation.9 | convolution fusion | flops 50663424 | bytes 1311040 | tf_op jit(solution)/shard_map/pr,crg->cpg/dot_general | solution.py:351
  (80 shorter events, 4.5 us)
Async XLA Ops:
  0.6 13.2 %copy-start = (f32[16,64,64]{2,1,0:T(8,128)S(1)}, f32[16,64,64]{2,1,0:T(8,128)}, u32[]{:S(2)}) copy-start(f32[16,64,64]{2,1,0:T(8,128)} %base_ref.1) | copy-start | bytes 786436
  10.3 4.9 %collective-permute-start.2 = (f16[16,2048]{1,0:T(8,128)(2,1)S(1)}, f16[16,2048]{1,0:T(8,128)(2,1)S(1)}, u32[]{:S(2)}, u32[]{:S(2)}) collective-permute-start(f16[16,2048]{1,0:T(8,128)(2,1)S(1)} %convert_element_type.95), channel_id=1, source_target_pairs={{0,3},{1,0},{2,1},{3,2},{4,7},{5,4},{6,5},{7,6},{8,11},{9,8},{10,9... | collective-permute-start | bytes 196616 | tf_op jit(solution)/shard_map/ppermute | solution.py:245
  12.7 3.8 %collective-permute-start.1 = (f16[16,2048]{1,0:T(8,128)(2,1)S(1)}, f16[16,2048]{1,0:T(8,128)(2,1)S(1)}, u32[]{:S(2)}, u32[]{:S(2)}) collective-permute-start(f16[16,2048]{1,0:T(8,128)(2,1)S(1)} %convert_element_type.95), channel_id=1, source_target_pairs={{0,1},{1,2},{2,3},{3,0},{4,5},{5,6},{6,7},{7,4},{8,9},{9,10},{10,1... | collective-permute-start | bytes 196616 | tf_op jit(solution)/shard_map/ppermute | solution.py:245
  12.7 4.9 %collective-permute-start = (f16[16,2048]{1,0:T(8,128)(2,1)S(1)}, f16[16,2048]{1,0:T(8,128)(2,1)S(1)}, u32[]{:S(2)}, u32[]{:S(2)}) collective-permute-start(f16[16,2048]{1,0:T(8,128)(2,1)S(1)} %convert_element_type.95), channel_id=1, source_target_pairs={{0,2},{1,3},{2,0},{3,1},{4,6},{5,7},{6,4},{7,5},{8,10},{9,11},{10,... | collective-permute-start | bytes 196616 | tf_op jit(solution)/shard_map/ppermute | solution.py:245
  17.7 12.8 %copy-start.6 = (f32[16,1024]{1,0:T(8,128)S(1)}, f32[16,1024]{1,0:T(8,128)}, u32[]{:S(2)}) copy-start(f32[16,1024]{1,0:T(8,128)} %beta_hbm.1) | copy-start | bytes 196612
  17.7 12.8 %copy-start.10 = (f32[16,1024]{1,0:T(8,128)S(1)}, f32[16,1024]{1,0:T(8,128)}, u32[]{:S(2)}) copy-start(f32[16,1024]{1,0:T(8,128)} %param.19) | copy-start | bytes 196612
  20.2 10.2 %collective-permute-start.5 = (f16[16,1024]{1,0:T(8,128)(2,1)S(1)}, f16[16,1024]{1,0:T(8,128)(2,1)S(1)}, u32[]{:S(2)}, u32[]{:S(2)}) collective-permute-start(f16[16,1024]{1,0:T(8,128)(2,1)S(1)} %convert_element_type.101), channel_id=1, source_target_pairs={{0,12},{4,0},{8,4},{12,8},{1,13},{5,1},{9,5},{13,9},{2,14},{6,2},{... | collective-permute-start | bytes 98312 | tf_op jit(solution)/shard_map/ppermute | solution.py:245
  23.9 6.6 %collective-permute-start.4 = (f16[16,1024]{1,0:T(8,128)(2,1)S(1)}, f16[16,1024]{1,0:T(8,128)(2,1)S(1)}, u32[]{:S(2)}, u32[]{:S(2)}) collective-permute-start(f16[16,1024]{1,0:T(8,128)(2,1)S(1)} %convert_element_type.101), channel_id=1, source_target_pairs={{0,4},{4,8},{8,12},{12,0},{1,5},{5,9},{9,13},{13,1},{2,6},{6,10},{... | collective-permute-start | bytes 98312 | tf_op jit(solution)/shard_map/ppermute | solution.py:245
  23.9 6.6 %collective-permute-start.3 = (f16[16,1024]{1,0:T(8,128)(2,1)S(1)}, f16[16,1024]{1,0:T(8,128)(2,1)S(1)}, u32[]{:S(2)}, u32[]{:S(2)}) collective-permute-start(f16[16,1024]{1,0:T(8,128)(2,1)S(1)} %convert_element_type.101), channel_id=1, source_target_pairs={{0,8},{4,12},{8,0},{12,4},{1,9},{5,13},{9,1},{13,5},{2,10},{6,14},... | collective-permute-start | bytes 98312 | tf_op jit(solution)/shard_map/ppermute | solution.py:245
  30.6 24.9 %copy-start.1 = (f32[16,1024]{1,0:T(8,128)}, f32[16,1024]{1,0:T(8,128)S(1)}, u32[]{:S(2)}) copy-start(f32[16,1024]{1,0:T(8,128)S(1)} %multiply_add_fusion.3.coef_ref) | copy-start | bytes 196612
  34.9 6.9 %collective-permute-start.14 = (f16[16,2048]{1,0:T(8,128)(2,1)S(1)}, f16[16,2048]{1,0:T(8,128)(2,1)S(1)}, u32[]{:S(2)}, u32[]{:S(2)}) collective-permute-start(f16[16,2048]{1,0:T(8,128)(2,1)S(1)} %convert_element_type.114), channel_id=1, source_target_pairs={{0,3},{1,0},{2,1},{3,2},{4,7},{5,4},{6,5},{7,6},{8,11},{9,8},{10,9... | collective-permute-start | bytes 196616 | tf_op jit(solution)/shard_map/ppermute | solution.py:245
  35.2 6.6 %collective-permute-start.13 = (f16[16,2048]{1,0:T(8,128)(2,1)S(1)}, f16[16,2048]{1,0:T(8,128)(2,1)S(1)}, u32[]{:S(2)}, u32[]{:S(2)}) collective-permute-start(f16[16,2048]{1,0:T(8,128)(2,1)S(1)} %convert_element_type.114), channel_id=1, source_target_pairs={{0,1},{1,2},{2,3},{3,0},{4,5},{5,6},{6,7},{7,4},{8,9},{9,10},{10,1... | collective-permute-start | bytes 196616 | tf_op jit(solution)/shard_map/ppermute | solution.py:245
  35.4 6.3 %collective-permute-start.12 = (f16[16,2048]{1,0:T(8,128)(2,1)S(1)}, f16[16,2048]{1,0:T(8,128)(2,1)S(1)}, u32[]{:S(2)}, u32[]{:S(2)}) collective-permute-start(f16[16,2048]{1,0:T(8,128)(2,1)S(1)} %convert_element_type.114), channel_id=1, source_target_pairs={{0,2},{1,3},{2,0},{3,1},{4,6},{5,7},{6,4},{7,5},{8,10},{9,11},{10,... | collective-permute-start | bytes 196616 | tf_op jit(solution)/shard_map/ppermute | solution.py:245
  36.9 11.4 %collective-permute-start.8 = (f16[17,16,128]{2,1,0:T(8,128)(2,1)S(1)}, f16[17,16,128]{2,1,0:T(8,128)(2,1)S(1)}, u32[]{:S(2)}, u32[]{:S(2)}) collective-permute-start(f16[17,16,128]{2,1,0:T(8,128)(2,1)S(1)} %get-tuple-element.35), channel_id=1, source_target_pairs={{0,12},{4,0},{8,4},{12,8},{1,13},{5,1},{9,5},{13,9},{2,14},{6,2},{... | collective-permute-start | bytes 208904 | tf_op jit(solution)/shard_map/ppermute | solution.py:264
  39.7 9.1 %collective-permute-start.7 = (f16[17,16,128]{2,1,0:T(8,128)(2,1)S(1)}, f16[17,16,128]{2,1,0:T(8,128)(2,1)S(1)}, u32[]{:S(2)}, u32[]{:S(2)}) collective-permute-start(f16[17,16,128]{2,1,0:T(8,128)(2,1)S(1)} %get-tuple-element.36), channel_id=1, source_target_pairs={{0,8},{4,12},{8,0},{12,4},{1,9},{5,13},{9,1},{13,5},{2,10},{6,14},... | collective-permute-start | bytes 208904 | tf_op jit(solution)/shard_map/ppermute | solution.py:264
  41.8 7.1 %collective-permute-start.6 = (f16[17,16,128]{2,1,0:T(8,128)(2,1)S(1)}, f16[17,16,128]{2,1,0:T(8,128)(2,1)S(1)}, u32[]{:S(2)}, u32[]{:S(2)}) collective-permute-start(f16[17,16,128]{2,1,0:T(8,128)(2,1)S(1)} %get-tuple-element.34), channel_id=1, source_target_pairs={{0,4},{4,8},{8,12},{12,0},{1,5},{5,9},{9,13},{13,1},{2,6},{6,10},{... | collective-permute-start | bytes 208904 | tf_op jit(solution)/shard_map/ppermute | solution.py:264
  41.9 20.2 %copy-start.9 = (f32[16,64,64]{2,1,0:T(8,128)S(1)}, f32[16,64,64]{2,1,0:T(8,128)}, u32[]{:S(2)}) copy-start(f32[16,64,64]{2,1,0:T(8,128)} %param.21) | copy-start | bytes 786436
  44.4 11.1 %collective-permute-start.17 = (f16[16,1024]{1,0:T(8,128)(2,1)S(1)}, f16[16,1024]{1,0:T(8,128)(2,1)S(1)}, u32[]{:S(2)}, u32[]{:S(2)}) collective-permute-start(f16[16,1024]{1,0:T(8,128)(2,1)S(1)} %convert_element_type.120), channel_id=1, source_target_pairs={{0,12},{4,0},{8,4},{12,8},{1,13},{5,1},{9,5},{13,9},{2,14},{6,2},{... | collective-permute-start | bytes 98312 | tf_op jit(solution)/shard_map/ppermute | solution.py:245
  48.2 7.3 %collective-permute-start.16 = (f16[16,1024]{1,0:T(8,128)(2,1)S(1)}, f16[16,1024]{1,0:T(8,128)(2,1)S(1)}, u32[]{:S(2)}, u32[]{:S(2)}) collective-permute-start(f16[16,1024]{1,0:T(8,128)(2,1)S(1)} %convert_element_type.120), channel_id=1, source_target_pairs={{0,4},{4,8},{8,12},{12,0},{1,5},{5,9},{9,13},{13,1},{2,6},{6,10},{... | collective-permute-start | bytes 98312 | tf_op jit(solution)/shard_map/ppermute | solution.py:245
  48.2 7.3 %collective-permute-start.15 = (f16[16,1024]{1,0:T(8,128)(2,1)S(1)}, f16[16,1024]{1,0:T(8,128)(2,1)S(1)}, u32[]{:S(2)}, u32[]{:S(2)}) collective-permute-start(f16[16,1024]{1,0:T(8,128)(2,1)S(1)} %convert_element_type.120), channel_id=1, source_target_pairs={{0,8},{4,12},{8,0},{12,4},{1,9},{5,13},{9,1},{13,5},{2,10},{6,14},... | collective-permute-start | bytes 98312 | tf_op jit(solution)/shard_map/ppermute | solution.py:245
  48.9 14.3 %copy-start.8 = (f32[16,64,64]{2,1,0:T(8,128)S(1)}, f32[16,64,64]{2,1,0:T(8,128)}, u32[]{:S(2)}) copy-start(f32[16,64,64]{2,1,0:T(8,128)} %get-tuple-element.10) | copy-start | bytes 786436
  48.9 7.3 %collective-permute-start.9 = (f16[17,16,128]{2,1,0:T(8,128)(2,1)S(1)}, f16[17,16,128]{2,1,0:T(8,128)(2,1)S(1)}, u32[]{:S(2)}, u32[]{:S(2)}) collective-permute-start(f16[17,16,128]{2,1,0:T(8,128)(2,1)S(1)} %add_convert_fusion), channel_id=1, source_target_pairs={{0,12},{4,0},{8,4},{12,8},{1,13},{5,1},{9,5},{13,9},{2,14},{6,2},{... | collective-permute-start | bytes 208904 | tf_op jit(solution)/shard_map/ppermute | solution.py:266
  52.2 7.1 %collective-permute-start.10 = (f16[17,16,128]{2,1,0:T(8,128)(2,1)S(1)}, f16[17,16,128]{2,1,0:T(8,128)(2,1)S(1)}, u32[]{:S(2)}, u32[]{:S(2)}) collective-permute-start(f16[17,16,128]{2,1,0:T(8,128)(2,1)S(1)} %add_convert_fusion), channel_id=1, source_target_pairs={{0,8},{4,12},{8,0},{12,4},{1,9},{5,13},{9,1},{13,5},{2,10},{6,14},... | collective-permute-start | bytes 208904 | tf_op jit(solution)/shard_map/ppermute | solution.py:266
  55.4 6.2 %collective-permute-start.11 = (f16[17,16,128]{2,1,0:T(8,128)(2,1)S(1)}, f16[17,16,128]{2,1,0:T(8,128)(2,1)S(1)}, u32[]{:S(2)}, u32[]{:S(2)}) collective-permute-start(f16[17,16,128]{2,1,0:T(8,128)(2,1)S(1)} %add_convert_fusion), channel_id=1, source_target_pairs={{0,4},{4,8},{8,12},{12,0},{1,5},{5,9},{9,13},{13,1},{2,6},{6,10},{... | collective-permute-start | bytes 208904 | tf_op jit(solution)/shard_map/ppermute | solution.py:266
  (8 other events, 75.2 us)

commit v2 on v1

v2 whole, which is shorter than its diff:
```python
import jax
import jax.numpy as jnp
from jax import lax
from jax.experimental import pallas as pl
from jax.experimental.pallas import tpu as pltpu
from jax.sharding import PartitionSpec as P

PREC = 256.0
SCALE = 1.0 / 16.0
TILE = 256
OCTET = 8
SPAN = 3
VMEM_LIMIT = 24 * 1024 * 1024
NT = (((1,), (1,)), ((), ()))
NN = (((1,), (0,)), ((), ()))
F32 = jnp.float32
BF16 = jnp.bfloat16


def whole():
    return pl.BlockSpec(memory_space=pltpu.VMEM)


def params():
    return pltpu.CompilerParams(vmem_limit_bytes=VMEM_LIMIT)


def fill_table(table_ref, u):
    chains, octets = len(u), u[0].shape[0] // OCTET
    for q in range(octets):
        rows = jnp.concatenate([x[q * OCTET : (q + 1) * OCTET, :] for x in u], axis=0)
        high = rows.astype(BF16)
        low = (rows - high.astype(F32)).astype(BF16)
        table_ref[q * chains * OCTET : (q + 1) * chains * OCTET, :] = jnp.concatenate([high, low], axis=1)


def window_of(ids, octets, span):
    start = jnp.clip(jnp.min(ids) // OCTET, 0, octets - span)
    return start, ids - start * OCTET


def octet_masks(ids, span):
    sub = lax.broadcasted_iota(jnp.int32, (OCTET, ids.shape[1]), 0)
    return [sub + OCTET * k == ids for k in range(span)]


def term_of_window(table_ref, slopes, ids, start, chains, span):
    tile = slopes.shape[1]
    block = chains * OCTET
    rows = pl.ds(pl.multiple_of(start * block, block), span * block)
    stacked = jnp.concatenate([slopes, slopes], axis=0)
    part = lax.dot_general(table_ref[rows, :], stacked, NN, preferred_element_type=F32)
    part = part.reshape(span, chains, OCTET, tile)
    picked = jnp.zeros((chains, OCTET, tile), F32)
    for k, mask in enumerate(octet_masks(ids, span)):
        picked = jnp.where(mask[None], part[k], picked)
    return jnp.sum(picked, axis=1)


def sums_of_window(total_ref, resid, slopes, ids, start, chains, span):
    tile = slopes.shape[1]
    block = chains * OCTET
    rows = pl.ds(pl.multiple_of(start * block, block), span * block)
    spread = jnp.broadcast_to(resid.astype(F32)[:, None, :], (chains, OCTET, tile))
    table = [jnp.where(mask[None], spread, 0.0).reshape(block, tile) for mask in octet_masks(ids, span)]
    table = jnp.concatenate(table, axis=0).astype(BF16)
    total_ref[rows, :] += lax.dot_general(table, slopes, NT, preferred_element_type=F32)


def each_tile(ids_ref, owned, visit, rest):
    octets = owned // OCTET
    span = min(SPAN, octets)
    first = lax.axis_index("loan") * owned
    tiles = ids_ref.shape[1] // TILE
    most = None
    for t in range(tiles):
        ids = ids_ref[:, t * TILE : (t + 1) * TILE] - first
        start, ids = window_of(ids, octets, span)
        visit(t, ids, start, span)
        most = ids if most is None else jnp.maximum(most, ids)

    @pl.when(jnp.max(most) >= span * OCTET)
    def _():
        @pl.loop(0, tiles)
        def _(t):
            cols = pl.ds(pl.multiple_of(t * TILE, TILE), TILE)
            ids = ids_ref[:, cols] - first
            start, _ = window_of(ids, octets, span)

            @pl.loop(start + span, jnp.max(ids) // OCTET + 1)
            def _(q):
                rest(cols, ids - q * OCTET, q)


def all_terms(table_ref, slope_ref, ids_ref, out_ref, chains, owned):
    def visit(t, ids, start, span):
        cols = slice(t * TILE, (t + 1) * TILE)
        out_ref[:, cols] = term_of_window(table_ref, slope_ref[:, cols], ids, start, chains, span)

    def rest(cols, ids, q):
        out_ref[:, cols] += term_of_window(table_ref, slope_ref[:, cols], ids, q, chains, 1)

    each_tile(ids_ref, owned, visit, rest)


def all_sums(total_ref, resid_ref, slope_ref, ids_ref, chains, owned):
    total_ref[...] = jnp.zeros(total_ref.shape, F32)

    def visit(t, ids, start, span):
        cols = slice(t * TILE, (t + 1) * TILE)
        sums_of_window(total_ref, resid_ref[:, cols], slope_ref[:, cols], ids, start, chains, span)

    def rest(cols, ids, q):
        sums_of_window(total_ref, resid_ref[:, cols], slope_ref[:, cols], ids, q, chains, 1)

    each_tile(ids_ref, owned, visit, rest)
    block = chains * OCTET
    return [
        jnp.concatenate(
            [
                total_ref[q * block + c * OCTET : q * block + (c + 1) * OCTET, :]
                for q in range(owned // OCTET)
            ],
            axis=0,
        )
        for c in range(chains)
    ]


def in_vmem(x):
    return pltpu.with_memory_space_constraint(x, pltpu.VMEM)


def in_hbm(x):
    return pltpu.with_memory_space_constraint(x, pltpu.HBM)


def tile_copies(source, target, sems):
    copies = []
    for t in range(source.shape[0] // TILE):
        rows = pl.ds(t * TILE, TILE)
        copies.append(pltpu.make_async_copy(source.at[rows], target.at[rows], sems.at[t]))
    for copy in copies:
        copy.start()
    return copies


def design_scratch(design):
    rows, feats = design.shape
    return [pltpu.VMEM((rows, feats), BF16), pltpu.SemaphoreType.DMA((rows // TILE,))]


def first_logits(design, ids, beta, pools, stride):
    rows, feats = design.shape
    chains, owned, slopes = pools.shape

    def kernel(design_ref, ids_ref, beta_hbm, pools_hbm, slope_ref, part_ref, w, table, linear, b_ref, u_ref, sem):
        small = [
            pltpu.make_async_copy(pools_hbm, u_ref, sem.at[0]),
            pltpu.make_async_copy(beta_hbm, b_ref, sem.at[1]),
        ]
        for copy in small:
            copy.start()
        g = lax.broadcasted_iota(jnp.int32, (slopes, feats), 0)
        f = lax.broadcasted_iota(jnp.int32, (slopes, feats), 1)
        w[:slopes, :] = jnp.where(f == g * stride, 1.0, 0.0).astype(BF16)
        small[0].wait()
        fill_table(table, [u_ref[c] for c in range(chains)])
        small[1].wait()
        w[slopes:, :] = b_ref[...].astype(BF16)
        for t in range(rows // TILE):
            cols = slice(t * TILE, (t + 1) * TILE)
            both = lax.dot_general(w[...], design_ref[cols, :], NT, preferred_element_type=F32)
            slope_ref[:, cols] = both[:slopes, :].astype(BF16)
            linear[:, cols] = both[slopes:, :]
        all_terms(table, slope_ref, ids_ref, part_ref, chains, owned)
        part_ref[...] = SCALE * (part_ref[...] + linear[...])

    return pl.pallas_call(
        kernel,
        in_specs=[whole(), whole()] + [pl.BlockSpec(memory_space=pl.ANY)] * 2,
        out_specs=[whole(), whole()],
        out_shape=[
            jax.ShapeDtypeStruct((slopes, rows), BF16),
            jax.ShapeDtypeStruct((chains, rows), F32),
        ],
        scratch_shapes=[
            pltpu.VMEM((slopes + chains, feats), BF16),
            pltpu.VMEM((chains * owned, 2 * slopes), BF16),
            pltpu.VMEM((chains, rows), F32),
            pltpu.VMEM(beta.shape, F32),
            pltpu.VMEM(pools.shape, F32),
            pltpu.SemaphoreType.DMA((2,)),
        ],
        compiler_params=params(),
        name="first_logits",
    )(in_vmem(design), ids, in_hbm(beta), in_hbm(pools))


def population_gradient(resid, design):
    def kernel(resid_ref, design_ref, out_ref):
        out_ref[...] = SCALE * lax.dot_general(
            resid_ref[...], design_ref[...], NN, preferred_element_type=F32
        )

    return pl.pallas_call(
        kernel,
        in_specs=[whole(), whole()],
        out_specs=whole(),
        out_shape=jax.ShapeDtypeStruct((resid.shape[0], design.shape[1]), F32),
        compiler_params=params(),
        name="population_gradient",
    )(resid, in_vmem(design))


def stacked_split(x, pieces):
    parts = []
    for _ in range(pieces):
        part = x.astype(BF16)
        parts.append(part)
        x = x - part.astype(F32)
    return jnp.concatenate(parts, axis=0)


def quad(x, j, pairs):
    return jnp.concatenate([x[k] for k in (2 * j, 2 * j + pairs, 2 * j + 1, 2 * j + 1 + pairs)], axis=1)


def region_onehot(index_ref, regions):
    shape = (regions, index_ref.shape[1])
    return jnp.where(lax.broadcasted_iota(jnp.int32, shape, 0) == index_ref[...], 1.0, 0.0)


def chosen_regions(onehot, v):
    chains, _, slopes = v.shape
    pairs = chains // 2
    table = jnp.concatenate([onehot.T.astype(BF16)] * 3, axis=1)
    found = [None] * chains
    for j in range(pairs // 2):
        got = lax.dot_general(
            table, stacked_split(quad(v, j, pairs), 3), NN, preferred_element_type=F32
        )
        for k, c in enumerate((2 * j, 2 * j + pairs, 2 * j + 1, 2 * j + 1 + pairs)):
            found[c] = got[:, k * slopes : (k + 1) * slopes]
    return found


def region_sums(onehot, x, pieces, store):
    pairs = len(x) // 2
    width = 2 * x[0].shape[1]
    table = jnp.concatenate([onehot.astype(BF16)] * pieces, axis=1)
    for j in range(pairs // 2):
        got = lax.dot_general(
            table, stacked_split(quad(x, j, pairs), pieces), NN, preferred_element_type=F32
        )
        store(2 * j, got[:, :width])
        store(2 * j + 1, got[:, width:])


def smem():
    return pl.BlockSpec(memory_space=pltpu.SMEM)


def prior(index, step, pools, regions, momentum, design):
    chains, owned, slopes = pools.shape
    n_regions = regions.shape[1]
    pairs = chains // 2

    def kernel(index_ref, step_ref, pools_ref, regions_ref, mom_ref, design_hbm, base_ref, sums_ref, kept, sem):
        copy = pltpu.make_async_copy(design_hbm, kept, sem)
        copy.start()
        onehot = region_onehot(index_ref, n_regions)
        chosen = chosen_regions(onehot, regions_ref[...])
        dev = [PREC * (pools_ref[c] - chosen[c]) for c in range(chains)]
        for c in range(chains):
            base_ref[c] = mom_ref[c] - (0.5 * step_ref[c]) * dev[c]

        def store(k, value):
            sums_ref[k] = SCALE * value

        region_sums(onehot, dev, 3, store)
        count = jnp.sum(onehot, axis=1, keepdims=True)
        sums_ref[pairs] = SCALE * jnp.broadcast_to(count, (n_regions, 2 * slopes))
        copy.wait()

    return pl.pallas_call(
        kernel,
        in_specs=[whole(), smem(), whole(), whole(), whole(), pl.BlockSpec(memory_space=pl.ANY)],
        out_specs=[whole()] * 3,
        out_shape=[
            jax.ShapeDtypeStruct(pools.shape, F32),
            jax.ShapeDtypeStruct((pairs + 1, n_regions, 2 * slopes), F32),
            pltpu.VMEM(design.shape, BF16),
        ],
        scratch_shapes=[pltpu.SemaphoreType.DMA],
        compiler_params=params(),
        name="prior",
    )(index, step, pools, regions, momentum, in_hbm(design))


def pool_step(resid, slope, ids, index, step, base, mom_base, n_regions):
    chains, owned, slopes = base.shape
    rows = resid.shape[1]
    pairs = chains // 2

    def kernel(resid_ref, slope_ref, ids_ref, index_ref, step_ref, base_ref, mb_ref, next_ref, half_ref, term_ref, sums_ref, table, total):
        lik = all_sums(total, resid_ref, slope_ref, ids_ref, chains, owned)
        way, ahead = [], []
        for c in range(chains):
            half = mb_ref[c] + (0.5 * step_ref[c]) * lik[c]
            half_ref[c] = half
            way.append(step_ref[c] * half)
            ahead.append(base_ref[c] + way[c])
            next_ref[c] = ahead[c]
        fill_table(table, ahead)
        all_terms(table, slope_ref, ids_ref, term_ref, chains, owned)

        def store(k, value):
            sums_ref[k] = SCALE * value

        region_sums(region_onehot(index_ref, n_regions), way, 2, store)

    return pl.pallas_call(
        kernel,
        in_specs=[whole()] * 4 + [smem()] + [whole()] * 2,
        out_specs=[whole()] * 4,
        out_shape=[
            jax.ShapeDtypeStruct(base.shape, F32),
            jax.ShapeDtypeStruct(base.shape, F32),
            jax.ShapeDtypeStruct((chains, rows), F32),
            jax.ShapeDtypeStruct((pairs, n_regions, 2 * slopes), F32),
        ],
        scratch_shapes=[
            pltpu.VMEM((chains * owned, 2 * slopes), BF16),
            pltpu.VMEM((chains * owned, slopes), F32),
        ],
        compiler_params=params(),
        name="pool_step",
    )(resid, slope, ids, index, step, base, mom_base)


def region_step(index, step, sums, regions, momentum, pools_next, pool_half):
    chains, owned, slopes = pools_next.shape
    n_regions = regions.shape[1]
    pairs = chains // 2

    def kernel(index_ref, step_ref, sums_ref, v_ref, m_ref, u_ref, half_ref, next_ref, mom_ref, pool_ref):
        def part(k, c):
            side = slice((c // pairs) * slopes, (c // pairs + 1) * slopes)
            return (1.0 / SCALE) * sums_ref[k + c % pairs][:, side]

        count = (1.0 / SCALE) * sums_ref[pairs][:, :slopes]
        for c in range(chains):
            v, h = v_ref[c], 0.5 * step_ref[c]
            dev = part(0, c)
            half = m_ref[c] + h * (dev - PREC * v)
            ahead = v + step_ref[c] * half
            next_ref[c] = ahead
            gain = dev + PREC * (part(pairs + 1, c) - count * (ahead - v)) - PREC * ahead
            mom_ref[c] = half + h * gain
        chosen = chosen_regions(region_onehot(index_ref, n_regions), next_ref[...])
        for c in range(chains):
            pool_ref[c] = half_ref[c] - (0.5 * step_ref[c]) * (PREC * (u_ref[c] - chosen[c]))

    return pl.pallas_call(
        kernel,
        in_specs=[whole(), smem()] + [whole()] * 5,
        out_specs=[whole()] * 3,
        out_shape=[
            jax.ShapeDtypeStruct(regions.shape, F32),
            jax.ShapeDtypeStruct(regions.shape, F32),
            jax.ShapeDtypeStruct(pools_next.shape, F32),
        ],
        compiler_params=params(),
        name="region_step",
    )(index, step, sums, regions, momentum, pools_next, pool_half)


def pool_likelihood(resid, slope, ids, step, part):
    chains, owned, slopes = part.shape

    def kernel(resid_ref, slope_ref, ids_ref, step_ref, part_ref, out_ref, total):
        lik = all_sums(total, resid_ref, slope_ref, ids_ref, chains, owned)
        for c in range(chains):
            out_ref[c] = part_ref[c] + (0.5 * step_ref[c]) * lik[c]

    return pl.pallas_call(
        kernel,
        in_specs=[whole()] * 3 + [smem(), whole()],
        out_specs=whole(),
        out_shape=jax.ShapeDtypeStruct(part.shape, F32),
        scratch_shapes=[pltpu.VMEM((chains * owned, slopes), F32)],
        compiler_params=params(),
        name="pool_likelihood",
    )(resid, slope, ids, step, part)


def next_logits(design, coef, term):
    rows = design.shape[0]

    def kernel(design_ref, coef_ref, term_ref, out_ref):
        coef16 = coef_ref[...].astype(BF16)
        for t in range(rows // TILE):
            cols = slice(t * TILE, (t + 1) * TILE)
            linear = lax.dot_general(coef16, design_ref[cols, :], NT, preferred_element_type=F32)
            out_ref[:, cols] = SCALE * (term_ref[:, cols] + linear)

    return pl.pallas_call(
        kernel,
        in_specs=[whole(), whole(), whole()],
        out_specs=whole(),
        out_shape=jax.ShapeDtypeStruct(term.shape, F32),
        compiler_params=params(),
        name="next_logits",
    )(in_vmem(design), coef, term)


def ahead_by(k, size, stride, group):
    perm = []
    for i in range(size):
        digit = (i // stride) % group
        perm.append((i, i + ((digit + k) % group - digit) * stride))
    return perm


def total_over(x, axis):
    size = lax.axis_size(axis)
    stride = 1
    while stride < size:
        group = min(4, size // stride)
        own = lax.optimization_barrier(x.astype(jnp.float16))
        parts = [own] + [
            lax.ppermute(own, axis, ahead_by(k, size, stride, group)) for k in range(1, group)
        ]
        parts = [p.astype(F32) for p in parts]
        x = parts[0] + parts[1] if group == 2 else (parts[0] + parts[2]) + (parts[1] + parts[3])
        stride *= group
    return x


def shared_sum(x, axis):
    size = lax.axis_size(axis)
    me = lax.axis_index(axis)
    width = x.shape[1] // size
    x = lax.optimization_barrier(x.astype(jnp.float16))

    def block(k):
        return lax.dynamic_slice_in_dim(x, lax.rem(me + k, size) * width, width, 1)

    mine = block(0).astype(F32)
    for k in range(1, size):
        mine = mine + lax.ppermute(block(k), axis, ahead_by(k, size, 1, size)).astype(F32)
    mine = lax.optimization_barrier(mine.astype(jnp.float16))
    found = [mine] + [lax.ppermute(mine, axis, ahead_by(k, size, 1, size)) for k in range(1, size)]
    back = jnp.concatenate(found[::-1], axis=1)
    return jnp.roll(back, (me + 1) * width, axis=1).astype(F32)


def residual(part, labels):
    logit = total_over(part, "feat") * (1.0 / SCALE)
    return (labels.astype(F32)[None, :] - jax.nn.sigmoid(logit)).astype(BF16)


def body(
    design,
    labels,
    pool_ids,
    pool_region_index,
    step_size,
    beta,
    pools,
    regions,
    beta_momentum,
    pool_momentum,
    region_momentum,
):
    rows, feats = design.shape
    chains, owned, slopes = pools.shape
    n_regions = regions.shape[1]
    total_feats = float(feats * lax.axis_size("feat"))
    half = 0.5 * step_size
    ids = pool_ids[None, :]
    index = pool_region_index[None, :]

    slope, part = first_logits(design, ids, beta, pools, feats // slopes)
    pools_at, part = lax.optimization_barrier((pools, part))
    mom_base, dev_sums, kept = prior(
        index, step_size, pools_at, regions, pool_momentum, design
    )

    resid = residual(part, labels)
    gb = population_gradient(resid, kept)
    resid, gb, mom_base, dev_sums = lax.optimization_barrier((resid, gb, mom_base, dev_sums))
    pools_next, pool_half, term, way_sums = pool_step(
        resid, slope, ids, index, step_size, pools, mom_base, n_regions
    )
    sums = shared_sum(jnp.concatenate([dev_sums, way_sums], axis=0), "loan")
    gb = total_over(gb, "loan") * (1.0 / SCALE) - total_feats * beta
    beta_half = beta_momentum + half[:, None] * gb
    beta_next = beta + step_size[:, None] * beta_half

    part = next_logits(design, beta_next, term)
    resid = residual(part, labels)
    gb = population_gradient(resid, design)
    resid, gb = lax.optimization_barrier((resid, gb))
    regions_next, region_out, pool_part = region_step(
        index, step_size, sums, regions, region_momentum, pools_next, pool_half
    )
    pool_out = pool_likelihood(resid, slope, ids, step_size, pool_part)
    gb = total_over(gb, "loan") * (1.0 / SCALE) - total_feats * beta_next
    beta_out = beta_half + half[:, None] * gb
    return (beta_next, pools_next, regions_next, beta_out, pool_out, region_out)


def solution(mesh):
    in_specs = (
        P(("grp", "loan"), "feat"),
        P(("grp", "loan")),
        P(("grp", "loan")),
        P(("grp", "loan")),
        P("grp"),
        P("grp", "feat"),
        P("grp", "loan", "feat"),
        P("grp", None, "feat"),
        P("grp", "feat"),
        P("grp", "loan", "feat"),
        P("grp", None, "feat"),
    )
    out_specs = (
        P("grp", "feat"),
        P("grp", "loan", "feat"),
        P("grp", None, "feat"),
        P("grp", "feat"),
        P("grp", "loan", "feat"),
        P("grp", None, "feat"),
    )
    return jax.shard_map(body, mesh=mesh, in_specs=in_specs, out_specs=out_specs, check_vma=False)
```

time: 64.8 us -> 53.5 us (0.83)
  Pallas kernels: 23.7 us -> 16.3 us
  matrix products: 2.73 us -> 0 us
  waiting for transfers between devices: 8.04 us -> 5.55 us
  local copies, waits for them, and re-layouts: 1.61 us -> 3.23 us
  other arithmetic: 2.57 us -> 1.24 us
  starting transfers between devices: 24.8 us -> 25.9 us
    pallas_call x6 -> x8, Pallas kernels: 23.7 us -> 16.3 us  [the longest x1 3.21 us: first_logits(): pl.pallas_call(kernel, in_specs=[whole(), whole()] + [pl.BlockSpec(memory...]
    ppermute x12, starting transfers between devices: 14.6 us -> 18.2 us  [total_over(): lax.ppermute(own, axis, ahead_by(k, size, stride, group))]
    dot_general x4 -> x0, matrix products: 2.73 us -> none  [the longest x1 1.3 us: body(): jnp.einsum('pr,crg->cpg', lookup, regions_next, precision=lax.Precision.H...]
    ppermute x12, waiting for transfers between devices: 2.74 us -> 0.03 us  [total_over(): lax.ppermute(own, axis, ahead_by(k, size, stride, group))]
    ppermute x3, starting transfers between devices: 5.33 us -> 2.75 us  [shared_sum(): lax.ppermute(mine, axis, ahead_by(k, size, 1, size))]
    unnamed x35 -> x37, local copies, waits for them, and re-layouts: 1.01 us -> 3.15 us
    add x3 -> x2, other arithmetic: 1.95 us -> 0.79 us  [the longest x1 0.71 us: body(): beta_out = beta_half + half[:, None] * gb]
  transfers between devices with their start and end apart: 18 -> 18, of which waited for: 5 -> 4; matrix products, arithmetic and copies ran while one was open for 5% -> 2% of each run, Pallas kernels for 13% -> 12%
where the time goes in v2:
time: 53.5 us; the launch traced here: 53.2 us
  starting transfers between devices  25.9 us (48%)
  Pallas kernels  16.3 us (30%)
  waiting for transfers between devices  5.55 us (10%)
  local copies, waits for them, and re-layouts  3.23 us (6%)
  other arithmetic  1.24 us (2%)
  between operations  1.03 us (2%)
    ppermute x12, starting transfers between devices, total_over(): lax.ppermute(own, axis, ahead_by(k, size, stride, group))  18.2 us
    ppermute x3, waiting for transfers between devices, shared_sum(): lax.ppermute(mine, axis, ahead_by(k, size, 1, size))  5.32 us
    ppermute x3, starting transfers between devices, shared_sum(): lax.ppermute(block(k), axis, ahead_by(k, size, 1, size)).astype(F32)  4.96 us
    pallas_call x1, Pallas kernels, first_logits(): pl.pallas_call(kernel, in_specs=[whole(), whole()] + [pl.BlockSpec(memory...  3.21 us
    unnamed x37, local copies, waits for them, and re-layouts  3.15 us
    pallas_call x1, Pallas kernels, pool_step(): pl.pallas_call(kernel, in_specs=[whole()] * 4 + [smem()] + [whole()] * 2,...  3.14 us
    ppermute x3, starting transfers between devices, shared_sum(): lax.ppermute(mine, axis, ahead_by(k, size, 1, size))  2.75 us
    pallas_call x1, Pallas kernels, prior(): pl.pallas_call(kernel, in_specs=[whole(), smem(), whole(), whole(), whole...  2.75 us
  transfers between devices with their start and end apart: 18, of which 4 were waited for; matrix products, arithmetic and copies ran while one was open for 2% of the time, Pallas kernels for 12%

profile of v2, /device:TPU:0, one launch (start us, length us, event | category | flops | bytes accessed | tf_op | source)
XLA Modules:
  0.0 53.2 jit_solution(8060427324494112538)
XLA Ops:
  0.7 2.2 %copy-done = bf16[2048,1024]{1,0:T(8,128)(2,1)S(1)} copy-done((bf16[2048,1024]{1,0:T(8,128)(2,1)S(1)}, bf16[2048,1024]{1,0:T(8,128)(2,1)}, u32[]{:S(2)}) %copy-start) | copy-done | bytes 4194328
  2.9 0.7 %copy-done.8 = s32[2048]{0:T(1024)S(1)} copy-done((s32[2048]{0:T(1024)S(1)}, s32[2048]{0:T(1024)}, u32[]{:S(2)}) %copy-start.8) | copy-done | bytes 8216
  3.6 3.2 %first_logits.1 = (bf16[64,2048]{1,0:T(8,128)(2,1)S(1)}, f32[16,2048]{1,0:T(8,128)S(1)}) custom-call(bf16[2048,1024]{1,0:T(8,128)(2,1)S(1)} %copy-done, s32[1,2048]{1,0:T(1,128)S(1)} %bitcast.2, f32[16,1024]{1,0:T(8,128)} %beta_hbm.1, f32[16,64,64]{2,1,0:T(8,128)} %base_ref.1), custom_call_target="tpu_custom_call" | custom-call | tf_op jit(solution)/shard_map/first_logits/pallas_call | solution.py:179
  6.8 3.0 %collective-permute-start = (f16[16,2048]{1,0:T(8,128)(2,1)S(1)}, f16[16,2048]{1,0:T(8,128)(2,1)S(1)}, u32[]{:S(2)}, u32[]{:S(2)}) collective-permute-start(f16[16,2048]{1,0:T(8,128)(2,1)S(1)} %convert_element_type.90), channel_id=1, source_target_pairs={{0,2},{1,3},{2,0},{3,1},{4,6},{5,7},{6,4},{7,5},{8,10},{9,11},{10,... | collective-permute-start | bytes 196616 | tf_op jit(solution)/shard_map/ppermute | solution.py:433
  9.8 1.7 %collective-permute-start.2 = (f16[16,2048]{1,0:T(8,128)(2,1)S(1)}, f16[16,2048]{1,0:T(8,128)(2,1)S(1)}, u32[]{:S(2)}, u32[]{:S(2)}) collective-permute-start(f16[16,2048]{1,0:T(8,128)(2,1)S(1)} %convert_element_type.90), channel_id=1, source_target_pairs={{0,3},{1,0},{2,1},{3,2},{4,7},{5,4},{6,5},{7,6},{8,11},{9,8},{10,9... | collective-permute-start | bytes 196616 | tf_op jit(solution)/shard_map/ppermute | solution.py:433
  11.7 2.7 %prior.1 = (f32[16,64,64]{2,1,0:T(8,128)S(1)}, f32[9,64,128]{2,1,0:T(8,128)S(1)}, bf16[2048,1024]{1,0:T(8,128)(2,1)S(1)}) custom-call(s32[1,64]{1,0:T(1,128)S(1)} %bitcast.5, f32[16]{0:T(128)S(1)} %copy-done.10, f32[16,64,64]{2,1,0:T(8,128)S(1)} %copy-done.2, f32[16,64,64]{2,1,0:T(8,128)S(1)} %copy-done.3, f32[16,64,64]{2,1,0:T(8,128)S(1)} %copy-done.5, ...), custom_call_target="tpu_custom_call" | custom-call | tf_op jit(solution)/shard_map/prior/pallas_call | solution.py:286
  15.2 2.6 %collective-permute-start.3 = (f16[16,1024]{1,0:T(8,128)(2,1)S(1)}, f16[16,1024]{1,0:T(8,128)(2,1)S(1)}, u32[]{:S(2)}, u32[]{:S(2)}) collective-permute-start(f16[16,1024]{1,0:T(8,128)(2,1)S(1)} %convert_element_type.96), channel_id=1, source_target_pairs={{0,8},{4,12},{8,0},{12,4},{1,9},{5,13},{9,1},{13,5},{2,10},{6,14},... | collective-permute-start | bytes 98312 | tf_op jit(solution)/shard_map/ppermute | solution.py:433
  17.9 1.6 %collective-permute-start.4 = (f16[16,1024]{1,0:T(8,128)(2,1)S(1)}, f16[16,1024]{1,0:T(8,128)(2,1)S(1)}, u32[]{:S(2)}, u32[]{:S(2)}) collective-permute-start(f16[16,1024]{1,0:T(8,128)(2,1)S(1)} %convert_element_type.96), channel_id=1, source_target_pairs={{0,4},{4,8},{8,12},{12,0},{1,5},{5,9},{9,13},{13,1},{2,6},{6,10},{... | collective-permute-start | bytes 98312 | tf_op jit(solution)/shard_map/ppermute | solution.py:433
  19.5 2.2 %collective-permute-start.5 = (f16[16,1024]{1,0:T(8,128)(2,1)S(1)}, f16[16,1024]{1,0:T(8,128)(2,1)S(1)}, u32[]{:S(2)}, u32[]{:S(2)}) collective-permute-start(f16[16,1024]{1,0:T(8,128)(2,1)S(1)} %convert_element_type.96), channel_id=1, source_target_pairs={{0,12},{4,0},{8,4},{12,8},{1,13},{5,1},{9,5},{13,9},{2,14},{6,2},{... | collective-permute-start | bytes 98312 | tf_op jit(solution)/shard_map/ppermute | solution.py:433
  21.7 3.1 %pool_step.1 = (f32[16,64,64]{2,1,0:T(8,128)}, f32[16,64,64]{2,1,0:T(8,128)S(1)}, f32[16,2048]{1,0:T(8,128)S(1)}, f32[8,64,128]{2,1,0:T(8,128)S(1)}) custom-call(bf16[16,2048]{1,0:T(8,128)(2,1)S(1)} %subtract_convert_fusion.1.resid_ref, bf16[64,2048]{1,0:T(8,128)(2,1)S(1)} %get-tuple-element.34.slope_ref, s32[1,2048]{1,0:T(1,128)S(1)} %bitcast.3, ...), custom_call_target="tpu_custom_call" | custom-call | tf_op jit(solution)/shard_map/pool_step/pallas_call | solution.py:323
  25.2 1.2 %next_logits.1 = f32[16,2048]{1,0:T(8,128)S(1)} custom-call(bf16[2048,1024]{1,0:T(8,128)(2,1)S(1)} %copy-done.1, f32[16,1024]{1,0:T(8,128)S(1)} %multiply_add_fusion.1.coef_ref, f32[16,2048]{1,0:T(8,128)S(1)} %get-tuple-element.41.term_ref), custom_call_target="tpu_custom_call" | custom-call | tf_op jit(solution)/shard_map/next_logits/pallas_call | solution.py:408
  27.0 1.7 %collective-permute-start.14 = (f16[16,2048]{1,0:T(8,128)(2,1)S(1)}, f16[16,2048]{1,0:T(8,128)(2,1)S(1)}, u32[]{:S(2)}, u32[]{:S(2)}) collective-permute-start(f16[16,2048]{1,0:T(8,128)(2,1)S(1)} %convert_element_type.107), channel_id=1, source_target_pairs={{0,3},{1,0},{2,1},{3,2},{4,7},{5,4},{6,5},{7,6},{8,11},{9,8},{10,9... | collective-permute-start | bytes 196616 | tf_op jit(solution)/shard_map/ppermute | solution.py:433
  28.9 2.9 %collective-permute-start.7 = (f16[17,16,128]{2,1,0:T(8,128)(2,1)S(1)}, f16[17,16,128]{2,1,0:T(8,128)(2,1)S(1)}, u32[]{:S(2)}, u32[]{:S(2)}) collective-permute-start(f16[17,16,128]{2,1,0:T(8,128)(2,1)S(1)} %get-tuple-element.48), channel_id=1, source_target_pairs={{0,8},{4,12},{8,0},{12,4},{1,9},{5,13},{9,1},{13,5},{2,10},{6,14},... | collective-permute-start | bytes 208904 | tf_op jit(solution)/shard_map/ppermute | solution.py:452
  31.8 2.0 %collective-permute-start.8 = (f16[17,16,128]{2,1,0:T(8,128)(2,1)S(1)}, f16[17,16,128]{2,1,0:T(8,128)(2,1)S(1)}, u32[]{:S(2)}, u32[]{:S(2)}) collective-permute-start(f16[17,16,128]{2,1,0:T(8,128)(2,1)S(1)} %get-tuple-element.47), channel_id=1, source_target_pairs={{0,12},{4,0},{8,4},{12,8},{1,13},{5,1},{9,5},{13,9},{2,14},{6,2},{... | collective-permute-start | bytes 208904 | tf_op jit(solution)/shard_map/ppermute | solution.py:452
  34.5 1.0 %collective-permute-start.15 = (f16[16,1024]{1,0:T(8,128)(2,1)S(1)}, f16[16,1024]{1,0:T(8,128)(2,1)S(1)}, u32[]{:S(2)}, u32[]{:S(2)}) collective-permute-start(f16[16,1024]{1,0:T(8,128)(2,1)S(1)} %convert_element_type.113), channel_id=1, source_target_pairs={{0,8},{4,12},{8,0},{12,4},{1,9},{5,13},{9,1},{13,5},{2,10},{6,14},... | collective-permute-start | bytes 98312 | tf_op jit(solution)/shard_map/ppermute | solution.py:433
  35.7 3.6 %collective-permute-start.17 = (f16[16,1024]{1,0:T(8,128)(2,1)S(1)}, f16[16,1024]{1,0:T(8,128)(2,1)S(1)}, u32[]{:S(2)}, u32[]{:S(2)}) collective-permute-start(f16[16,1024]{1,0:T(8,128)(2,1)S(1)} %convert_element_type.113), channel_id=1, source_target_pairs={{0,12},{4,0},{8,4},{12,8},{1,13},{5,1},{9,5},{13,9},{2,14},{6,2},{... | collective-permute-start | bytes 98312 | tf_op jit(solution)/shard_map/ppermute | solution.py:433
  39.4 1.4 %collective-permute-start.9 = (f16[17,16,128]{2,1,0:T(8,128)(2,1)S(1)}, f16[17,16,128]{2,1,0:T(8,128)(2,1)S(1)}, u32[]{:S(2)}, u32[]{:S(2)}) collective-permute-start(f16[17,16,128]{2,1,0:T(8,128)(2,1)S(1)} %add_convert_fusion), channel_id=1, source_target_pairs={{0,12},{4,0},{8,4},{12,8},{1,13},{5,1},{9,5},{13,9},{2,14},{6,2},{... | collective-permute-start | bytes 208904 | tf_op jit(solution)/shard_map/ppermute | solution.py:454
  40.9 1.3 %collective-permute-start.10 = (f16[17,16,128]{2,1,0:T(8,128)(2,1)S(1)}, f16[17,16,128]{2,1,0:T(8,128)(2,1)S(1)}, u32[]{:S(2)}, u32[]{:S(2)}) collective-permute-start(f16[17,16,128]{2,1,0:T(8,128)(2,1)S(1)} %add_convert_fusion), channel_id=1, source_target_pairs={{0,8},{4,12},{8,0},{12,4},{1,9},{5,13},{9,1},{13,5},{2,10},{6,14},... | collective-permute-start | bytes 208904 | tf_op jit(solution)/shard_map/ppermute | solution.py:454
  42.2 0.7 %multiply_add_fusion = f32[16,1024]{1,0:T(8,128)} fusion(f32[16,1024]{1,0:T(8,128)S(1)} %multiply_add_fusion.1.coef_ref, f16[16,1024]{1,0:T(8,128)(2,1)S(1)} %collective-permute-done.17, f16[16,1024]{1,0:T(8,128)(2,1)S(1)} %collective-permute-done.16, f16[16,1024]{1,0:T(8,128)(2,1)S(1)} %collective-permute-done.15, ...), kind=kLoop, calls=%fused_computation.5 | loop fusion | flops 393216 | bytes 524352 | tf_op jit(solution)/shard_map/add | solution.py:511
  42.9 0.9 %collective-permute-done.9 = f16[17,16,128]{2,1,0:T(8,128)(2,1)S(1)} collective-permute-done((f16[17,16,128]{2,1,0:T(8,128)(2,1)S(1)}, f16[17,16,128]{2,1,0:T(8,128)(2,1)S(1)}, u32[]{:S(2)}, u32[]{:S(2)}) %collective-permute-start.9) | collective-permute-done | bytes 69664 | tf_op jit(solution)/shard_map/ppermute | solution.py:454
  43.8 3.6 %collective-permute-done.10 = f16[17,16,128]{2,1,0:T(8,128)(2,1)S(1)} collective-permute-done((f16[17,16,128]{2,1,0:T(8,128)(2,1)S(1)}, f16[17,16,128]{2,1,0:T(8,128)(2,1)S(1)}, u32[]{:S(2)}, u32[]{:S(2)}) %collective-permute-start.10) | collective-permute-done | bytes 69664 | tf_op jit(solution)/shard_map/ppermute | solution.py:454
  47.5 0.8 %collective-permute-done.11 = f16[17,16,128]{2,1,0:T(8,128)(2,1)S(1)} collective-permute-done((f16[17,16,128]{2,1,0:T(8,128)(2,1)S(1)}, f16[17,16,128]{2,1,0:T(8,128)(2,1)S(1)}, u32[]{:S(2)}, u32[]{:S(2)}) %collective-permute-start.11) | collective-permute-done | bytes 69664 | tf_op jit(solution)/shard_map/ppermute | solution.py:454
  48.5 2.5 %region_step.1 = (f32[16,64,64]{2,1,0:T(8,128)}, f32[16,64,64]{2,1,0:T(8,128)}, f32[16,64,64]{2,1,0:T(8,128)S(1)}) custom-call(s32[1,64]{1,0:T(1,128)S(1)} %bitcast.7, f32[16]{0:T(128)S(1)} %copy-done.10, f32[17,64,128]{2,1,0:T(8,128)S(1)} %dynamic-slice_convert_fusion.sums_ref, f32[16,64,64]{2,1,0:T(8,128)S(1)} %copy-done.3, f32[16,64,64]{2,1,0:T(8,128)S(1)} %copy-done.6, ...), custom_call_target="tpu_custom_call" | custom-call | tf_op jit(solution)/shard_map/region_step/pallas_call | solution.py:365
  51.0 2.2 %pool_likelihood.1 = f32[16,64,64]{2,1,0:T(8,128)} custom-call(bf16[16,2048]{1,0:T(8,128)(2,1)S(1)} %subtract_convert_fusion.resid_ref, bf16[64,2048]{1,0:T(8,128)(2,1)S(1)} %get-tuple-element.34.slope_ref, s32[1,2048]{1,0:T(1,128)S(1)} %bitcast.4, f32[16]{0:T(128)S(1)} %copy-done.10, f32[16,64,64]{2,1,0:T(8,128)S(1)} %get-tuple-element.44.part_ref), custom_call_target="tpu_custom_call" | custom-call | tf_op jit(solution)/shard_map/pool_likelihood/pallas_call | solution.py:387
  (74 shorter events, 3.1 us)
Async XLA Ops:
  0.6 10.9 %copy-start.10 = (f32[16]{0:T(128)S(1)}, f32[16]{0:T(128)}, u32[]{:S(2)}) copy-start(f32[16]{0:T(128)} %step_ref.7) | copy-start | bytes 196
  0.6 11.0 %copy-start.11 = (s32[64]{0:T(128)S(1)}, s32[64]{0:T(128)}, u32[]{:S(2)}) copy-start(s32[64]{0:T(128)} %param.14) | copy-start | bytes 772
  6.8 7.7 %collective-permute-start = (f16[16,2048]{1,0:T(8,128)(2,1)S(1)}, f16[16,2048]{1,0:T(8,128)(2,1)S(1)}, u32[]{:S(2)}, u32[]{:S(2)}) collective-permute-start(f16[16,2048]{1,0:T(8,128)(2,1)S(1)} %convert_element_type.90), channel_id=1, source_target_pairs={{0,2},{1,3},{2,0},{3,1},{4,6},{5,7},{6,4},{7,5},{8,10},{9,11},{10,... | collective-permute-start | bytes 196616 | tf_op jit(solution)/shard_map/ppermute | solution.py:433
  9.8 4.7 %collective-permute-start.1 = (f16[16,2048]{1,0:T(8,128)(2,1)S(1)}, f16[16,2048]{1,0:T(8,128)(2,1)S(1)}, u32[]{:S(2)}, u32[]{:S(2)}) collective-permute-start(f16[16,2048]{1,0:T(8,128)(2,1)S(1)} %convert_element_type.90), channel_id=1, source_target_pairs={{0,1},{1,2},{2,3},{3,0},{4,5},{5,6},{6,7},{7,4},{8,9},{9,10},{10,1... | collective-permute-start | bytes 196616 | tf_op jit(solution)/shard_map/ppermute | solution.py:433
  9.8 4.7 %collective-permute-start.2 = (f16[16,2048]{1,0:T(8,128)(2,1)S(1)}, f16[16,2048]{1,0:T(8,128)(2,1)S(1)}, u32[]{:S(2)}, u32[]{:S(2)}) collective-permute-start(f16[16,2048]{1,0:T(8,128)(2,1)S(1)} %convert_element_type.90), channel_id=1, source_target_pairs={{0,3},{1,0},{2,1},{3,2},{4,7},{5,4},{6,5},{7,6},{8,11},{9,8},{10,9... | collective-permute-start | bytes 196616 | tf_op jit(solution)/shard_map/ppermute | solution.py:433
  14.4 10.7 %copy-start.1 = (bf16[2048,1024]{1,0:T(8,128)(2,1)S(1)}, bf16[2048,1024]{1,0:T(8,128)(2,1)}, u32[]{:S(2)}) copy-start(bf16[2048,1024]{1,0:T(8,128)(2,1)} %design_ref.5) | copy-start | bytes 12582916
  15.2 9.8 %collective-permute-start.3 = (f16[16,1024]{1,0:T(8,128)(2,1)S(1)}, f16[16,1024]{1,0:T(8,128)(2,1)S(1)}, u32[]{:S(2)}, u32[]{:S(2)}) collective-permute-start(f16[16,1024]{1,0:T(8,128)(2,1)S(1)} %convert_element_type.96), channel_id=1, source_target_pairs={{0,8},{4,12},{8,0},{12,4},{1,9},{5,13},{9,1},{13,5},{2,10},{6,14},... | collective-permute-start | bytes 98312 | tf_op jit(solution)/shard_map/ppermute | solution.py:433
  17.9 7.1 %collective-permute-start.4 = (f16[16,1024]{1,0:T(8,128)(2,1)S(1)}, f16[16,1024]{1,0:T(8,128)(2,1)S(1)}, u32[]{:S(2)}, u32[]{:S(2)}) collective-permute-start(f16[16,1024]{1,0:T(8,128)(2,1)S(1)} %convert_element_type.96), channel_id=1, source_target_pairs={{0,4},{4,8},{8,12},{12,0},{1,5},{5,9},{9,13},{13,1},{2,6},{6,10},{... | collective-permute-start | bytes 98312 | tf_op jit(solution)/shard_map/ppermute | solution.py:433
  19.5 5.6 %collective-permute-start.5 = (f16[16,1024]{1,0:T(8,128)(2,1)S(1)}, f16[16,1024]{1,0:T(8,128)(2,1)S(1)}, u32[]{:S(2)}, u32[]{:S(2)}) collective-permute-start(f16[16,1024]{1,0:T(8,128)(2,1)S(1)} %convert_element_type.96), channel_id=1, source_target_pairs={{0,12},{4,0},{8,4},{12,8},{1,13},{5,1},{9,5},{13,9},{2,14},{6,2},{... | collective-permute-start | bytes 98312 | tf_op jit(solution)/shard_map/ppermute | solution.py:433
  25.1 17.1 %copy-start.4 = (f32[16,1024]{1,0:T(8,128)}, f32[16,1024]{1,0:T(8,128)S(1)}, u32[]{:S(2)}) copy-start(f32[16,1024]{1,0:T(8,128)S(1)} %multiply_add_fusion.1.coef_ref) | copy-start | bytes 196612
  26.4 22.2 %copy-start.6 = (f32[16,64,64]{2,1,0:T(8,128)S(1)}, f32[16,64,64]{2,1,0:T(8,128)}, u32[]{:S(2)}) copy-start(f32[16,64,64]{2,1,0:T(8,128)} %m_ref.1) | copy-start | bytes 786436
  26.4 22.2 %copy-start.7 = (f32[16,64,64]{2,1,0:T(8,128)S(1)}, f32[16,64,64]{2,1,0:T(8,128)}, u32[]{:S(2)}) copy-start(f32[16,64,64]{2,1,0:T(8,128)} %get-tuple-element.21.u_ref) | copy-start | bytes 786436
  26.4 5.4 %collective-permute-start.12 = (f16[16,2048]{1,0:T(8,128)(2,1)S(1)}, f16[16,2048]{1,0:T(8,128)(2,1)S(1)}, u32[]{:S(2)}, u32[]{:S(2)}) collective-permute-start(f16[16,2048]{1,0:T(8,128)(2,1)S(1)} %convert_element_type.107), channel_id=1, source_target_pairs={{0,2},{1,3},{2,0},{3,1},{4,6},{5,7},{6,4},{7,5},{8,10},{9,11},{10,... | collective-permute-start | bytes 196616 | tf_op jit(solution)/shard_map/ppermute | solution.py:433
  27.0 6.8 %collective-permute-start.13 = (f16[16,2048]{1,0:T(8,128)(2,1)S(1)}, f16[16,2048]{1,0:T(8,128)(2,1)S(1)}, u32[]{:S(2)}, u32[]{:S(2)}) collective-permute-start(f16[16,2048]{1,0:T(8,128)(2,1)S(1)} %convert_element_type.107), channel_id=1, source_target_pairs={{0,1},{1,2},{2,3},{3,0},{4,5},{5,6},{6,7},{7,4},{8,9},{9,10},{10,1... | collective-permute-start | bytes 196616 | tf_op jit(solution)/shard_map/ppermute | solution.py:433
  27.0 6.8 %collective-permute-start.14 = (f16[16,2048]{1,0:T(8,128)(2,1)S(1)}, f16[16,2048]{1,0:T(8,128)(2,1)S(1)}, u32[]{:S(2)}, u32[]{:S(2)}) collective-permute-start(f16[16,2048]{1,0:T(8,128)(2,1)S(1)} %convert_element_type.107), channel_id=1, source_target_pairs={{0,3},{1,0},{2,1},{3,2},{4,7},{5,4},{6,5},{7,6},{8,11},{9,8},{10,9... | collective-permute-start | bytes 196616 | tf_op jit(solution)/shard_map/ppermute | solution.py:433
  28.8 6.9 %collective-permute-start.6 = (f16[17,16,128]{2,1,0:T(8,128)(2,1)S(1)}, f16[17,16,128]{2,1,0:T(8,128)(2,1)S(1)}, u32[]{:S(2)}, u32[]{:S(2)}) collective-permute-start(f16[17,16,128]{2,1,0:T(8,128)(2,1)S(1)} %get-tuple-element.46), channel_id=1, source_target_pairs={{0,4},{4,8},{8,12},{12,0},{1,5},{5,9},{9,13},{13,1},{2,6},{6,10},{... | collective-permute-start | bytes 208904 | tf_op jit(solution)/shard_map/ppermute | solution.py:452
  28.9 10.5 %collective-permute-start.7 = (f16[17,16,128]{2,1,0:T(8,128)(2,1)S(1)}, f16[17,16,128]{2,1,0:T(8,128)(2,1)S(1)}, u32[]{:S(2)}, u32[]{:S(2)}) collective-permute-start(f16[17,16,128]{2,1,0:T(8,128)(2,1)S(1)} %get-tuple-element.48), channel_id=1, source_target_pairs={{0,8},{4,12},{8,0},{12,4},{1,9},{5,13},{9,1},{13,5},{2,10},{6,14},... | collective-permute-start | bytes 208904 | tf_op jit(solution)/shard_map/ppermute | solution.py:452
  31.8 7.6 %collective-permute-start.8 = (f16[17,16,128]{2,1,0:T(8,128)(2,1)S(1)}, f16[17,16,128]{2,1,0:T(8,128)(2,1)S(1)}, u32[]{:S(2)}, u32[]{:S(2)}) collective-permute-start(f16[17,16,128]{2,1,0:T(8,128)(2,1)S(1)} %get-tuple-element.47), channel_id=1, source_target_pairs={{0,12},{4,0},{8,4},{12,8},{1,13},{5,1},{9,5},{13,9},{2,14},{6,2},{... | collective-permute-start | bytes 208904 | tf_op jit(solution)/shard_map/ppermute | solution.py:452
  34.5 7.7 %collective-permute-start.15 = (f16[16,1024]{1,0:T(8,128)(2,1)S(1)}, f16[16,1024]{1,0:T(8,128)(2,1)S(1)}, u32[]{:S(2)}, u32[]{:S(2)}) collective-permute-start(f16[16,1024]{1,0:T(8,128)(2,1)S(1)} %convert_element_type.113), channel_id=1, source_target_pairs={{0,8},{4,12},{8,0},{12,4},{1,9},{5,13},{9,1},{13,5},{2,10},{6,14},... | collective-permute-start | bytes 98312 | tf_op jit(solution)/shard_map/ppermute | solution.py:433
  35.5 6.7 %collective-permute-start.16 = (f16[16,1024]{1,0:T(8,128)(2,1)S(1)}, f16[16,1024]{1,0:T(8,128)(2,1)S(1)}, u32[]{:S(2)}, u32[]{:S(2)}) collective-permute-start(f16[16,1024]{1,0:T(8,128)(2,1)S(1)} %convert_element_type.113), channel_id=1, source_target_pairs={{0,4},{4,8},{8,12},{12,0},{1,5},{5,9},{9,13},{13,1},{2,6},{6,10},{... | collective-permute-start | bytes 98312 | tf_op jit(solution)/shard_map/ppermute | solution.py:433
  35.7 6.5 %collective-permute-start.17 = (f16[16,1024]{1,0:T(8,128)(2,1)S(1)}, f16[16,1024]{1,0:T(8,128)(2,1)S(1)}, u32[]{:S(2)}, u32[]{:S(2)}) collective-permute-start(f16[16,1024]{1,0:T(8,128)(2,1)S(1)} %convert_element_type.113), channel_id=1, source_target_pairs={{0,12},{4,0},{8,4},{12,8},{1,13},{5,1},{9,5},{13,9},{2,14},{6,2},{... | collective-permute-start | bytes 98312 | tf_op jit(solution)/shard_map/ppermute | solution.py:433
  39.4 4.4 %collective-permute-start.9 = (f16[17,16,128]{2,1,0:T(8,128)(2,1)S(1)}, f16[17,16,128]{2,1,0:T(8,128)(2,1)S(1)}, u32[]{:S(2)}, u32[]{:S(2)}) collective-permute-start(f16[17,16,128]{2,1,0:T(8,128)(2,1)S(1)} %add_convert_fusion), channel_id=1, source_target_pairs={{0,12},{4,0},{8,4},{12,8},{1,13},{5,1},{9,5},{13,9},{2,14},{6,2},{... | collective-permute-start | bytes 208904 | tf_op jit(solution)/shard_map/ppermute | solution.py:454
  40.9 6.6 %collective-permute-start.10 = (f16[17,16,128]{2,1,0:T(8,128)(2,1)S(1)}, f16[17,16,128]{2,1,0:T(8,128)(2,1)S(1)}, u32[]{:S(2)}, u32[]{:S(2)}) collective-permute-start(f16[17,16,128]{2,1,0:T(8,128)(2,1)S(1)} %add_convert_fusion), channel_id=1, source_target_pairs={{0,8},{4,12},{8,0},{12,4},{1,9},{5,13},{9,1},{13,5},{2,10},{6,14},... | collective-permute-start | bytes 208904 | tf_op jit(solution)/shard_map/ppermute | solution.py:454
  42.2 6.1 %collective-permute-start.11 = (f16[17,16,128]{2,1,0:T(8,128)(2,1)S(1)}, f16[17,16,128]{2,1,0:T(8,128)(2,1)S(1)}, u32[]{:S(2)}, u32[]{:S(2)}) collective-permute-start(f16[17,16,128]{2,1,0:T(8,128)(2,1)S(1)} %add_convert_fusion), channel_id=1, source_target_pairs={{0,4},{4,8},{8,12},{12,0},{1,5},{5,9},{9,13},{13,1},{2,6},{6,10},{... | collective-permute-start | bytes 208904 | tf_op jit(solution)/shard_map/ppermute | solution.py:454
  (9 other events, 66.4 us)

commit v3 on v2

--- a/solution.py
+++ b/solution.py
@@ -10,6 +10,7 @@
 TILE = 256
 OCTET = 8
 SPAN = 3
+CHUNKS = 2
 VMEM_LIMIT = 24 * 1024 * 1024
 NT = (((1,), (1,)), ((), ()))
 NN = (((1,), (0,)), ((), ()))
@@ -154,47 +155,60 @@
     rows, feats = design.shape
     chains, owned, slopes = pools.shape
 
-    def kernel(design_ref, ids_ref, beta_hbm, pools_hbm, slope_ref, part_ref, w, table, linear, b_ref, u_ref, sem):
+    def kernel(design_hbm, ids_hbm, beta_hbm, pools_hbm, slope_ref, part_ref, kept, w, table, linear, ids_ref, b_ref, u_ref, sem, sems):
         small = [
-            pltpu.make_async_copy(pools_hbm, u_ref, sem.at[0]),
-            pltpu.make_async_copy(beta_hbm, b_ref, sem.at[1]),
+            pltpu.make_async_copy(beta_hbm, b_ref, sem.at[0]),
+            pltpu.make_async_copy(pools_hbm, u_ref, sem.at[1]),
+            pltpu.make_async_copy(ids_hbm, ids_ref, sem.at[2]),
         ]
         for copy in small:
             copy.start()
+        size = rows // CHUNKS
+        chunks = []
+        for k in range(CHUNKS):
+            part = pl.ds(k * size, size)
+            chunks.append(pltpu.make_async_copy(design_hbm.at[part], kept.at[part], sems.at[k]))
+            chunks[k].start()
         g = lax.broadcasted_iota(jnp.int32, (slopes, feats), 0)
         f = lax.broadcasted_iota(jnp.int32, (slopes, feats), 1)
         w[:slopes, :] = jnp.where(f == g * stride, 1.0, 0.0).astype(BF16)
         small[0].wait()
+        w[slopes:, :] = b_ref[...].astype(BF16)
+        small[1].wait()
         fill_table(table, [u_ref[c] for c in range(chains)])
-        small[1].wait()
-        w[slopes:, :] = b_ref[...].astype(BF16)
-        for t in range(rows // TILE):
-            cols = slice(t * TILE, (t + 1) * TILE)
-            both = lax.dot_general(w[...], design_ref[cols, :], NT, preferred_element_type=F32)
-            slope_ref[:, cols] = both[:slopes, :].astype(BF16)
-            linear[:, cols] = both[slopes:, :]
+        small[2].wait()
+        for k in range(CHUNKS):
+            chunks[k].wait()
+            for t in range(k * size // TILE, (k + 1) * size // TILE):
+                cols = slice(t * TILE, (t + 1) * TILE)
+                both = lax.dot_general(w[...], kept[cols, :], NT, preferred_element_type=F32)
+                slope_ref[:, cols] = both[:slopes, :].astype(BF16)
+                linear[:, cols] = both[slopes:, :]
         all_terms(table, slope_ref, ids_ref, part_ref, chains, owned)
         part_ref[...] = SCALE * (part_ref[...] + linear[...])
 
     return pl.pallas_call(
         kernel,
-        in_specs=[whole(), whole()] + [pl.BlockSpec(memory_space=pl.ANY)] * 2,
+        in_specs=[pl.BlockSpec(memory_space=pl.ANY)] * 4,
         out_specs=[whole(), whole()],
         out_shape=[
             jax.ShapeDtypeStruct((slopes, rows), BF16),
             jax.ShapeDtypeStruct((chains, rows), F32),
         ],
         scratch_shapes=[
+            pltpu.VMEM((rows, feats), BF16),
             pltpu.VMEM((slopes + chains, feats), BF16),
             pltpu.VMEM((chains * owned, 2 * slopes), BF16),
             pltpu.VMEM((chains, rows), F32),
+            pltpu.VMEM(ids.shape, jnp.int32),
             pltpu.VMEM(beta.shape, F32),
             pltpu.VMEM(pools.shape, F32),
-            pltpu.SemaphoreType.DMA((2,)),
+            pltpu.SemaphoreType.DMA((3,)),
+            pltpu.SemaphoreType.DMA((CHUNKS,)),
         ],
         compiler_params=params(),
         name="first_logits",
-    )(in_vmem(design), ids, in_hbm(beta), in_hbm(pools))
+    )(in_hbm(design), in_hbm(ids), in_hbm(beta), in_hbm(pools))
 
 
 def population_gradient(resid, design):
@@ -339,12 +353,12 @@
     )(resid, slope, ids, index, step, base, mom_base)
 
 
-def region_step(index, step, sums, regions, momentum, pools_next, pool_half):
-    chains, owned, slopes = pools_next.shape
+def region_step(index, step, sums, regions, momentum, pool_part):
+    chains, owned, slopes = pool_part.shape
     n_regions = regions.shape[1]
     pairs = chains // 2
 
-    def kernel(index_ref, step_ref, sums_ref, v_ref, m_ref, u_ref, half_ref, next_ref, mom_ref, pool_ref):
+    def kernel(index_ref, step_ref, sums_ref, v_ref, m_ref, part_ref, next_ref, mom_ref, pool_ref):
         def part(k, c):
             side = slice((c // pairs) * slopes, (c // pairs + 1) * slopes)
             return (1.0 / SCALE) * sums_ref[k + c % pairs][:, side]
@@ -360,39 +374,39 @@
             mom_ref[c] = half + h * gain
         chosen = chosen_regions(region_onehot(index_ref, n_regions), next_ref[...])
         for c in range(chains):
-            pool_ref[c] = half_ref[c] - (0.5 * step_ref[c]) * (PREC * (u_ref[c] - chosen[c]))
-
-    return pl.pallas_call(
-        kernel,
-        in_specs=[whole(), smem()] + [whole()] * 5,
+            pool_ref[c] = part_ref[c] + (0.5 * step_ref[c]) * (PREC * chosen[c])
+
+    return pl.pallas_call(
+        kernel,
+        in_specs=[whole(), smem()] + [whole()] * 4,
         out_specs=[whole()] * 3,
         out_shape=[
             jax.ShapeDtypeStruct(regions.shape, F32),
             jax.ShapeDtypeStruct(regions.shape, F32),
-            jax.ShapeDtypeStruct(pools_next.shape, F32),
+            jax.ShapeDtypeStruct(pool_part.shape, F32),
         ],
         compiler_params=params(),
         name="region_step",
-    )(index, step, sums, regions, momentum, pools_next, pool_half)
-
-
-def pool_likelihood(resid, slope, ids, step, part):
-    chains, owned, slopes = part.shape
-
-    def kernel(resid_ref, slope_ref, ids_ref, step_ref, part_ref, out_ref, total):
+    )(index, step, sums, regions, momentum, pool_part)
+
+
+def pool_likelihood(resid, slope, ids, step, half, pools_next):
+    chains, owned, slopes = half.shape
+
+    def kernel(resid_ref, slope_ref, ids_ref, step_ref, half_ref, u_ref, out_ref, total):
         lik = all_sums(total, resid_ref, slope_ref, ids_ref, chains, owned)
         for c in range(chains):
-            out_ref[c] = part_ref[c] + (0.5 * step_ref[c]) * lik[c]
-
-    return pl.pallas_call(
-        kernel,
-        in_specs=[whole()] * 3 + [smem(), whole()],
+            out_ref[c] = half_ref[c] + (0.5 * step_ref[c]) * (lik[c] - PREC * u_ref[c])
+
+    return pl.pallas_call(
+        kernel,
+        in_specs=[whole()] * 3 + [smem(), whole(), whole()],
         out_specs=whole(),
-        out_shape=jax.ShapeDtypeStruct(part.shape, F32),
+        out_shape=jax.ShapeDtypeStruct(half.shape, F32),
         scratch_shapes=[pltpu.VMEM((chains * owned, slopes), F32)],
         compiler_params=params(),
         name="pool_likelihood",
-    )(resid, slope, ids, step, part)
+    )(resid, slope, ids, step, half, pools_next)
 
 
 def next_logits(design, coef, term):
@@ -503,10 +517,10 @@
     resid = residual(part, labels)
     gb = population_gradient(resid, design)
     resid, gb = lax.optimization_barrier((resid, gb))
-    regions_next, region_out, pool_part = region_step(
-        index, step_size, sums, regions, region_momentum, pools_next, pool_half
+    pool_part = pool_likelihood(resid, slope, ids, step_size, pool_half, pools_next)
+    regions_next, region_out, pool_out = region_step(
+        index, step_size, sums, regions, region_momentum, pool_part
     )
-    pool_out = pool_likelihood(resid, slope, ids, step_size, pool_part)
     gb = total_over(gb, "loan") * (1.0 / SCALE) - total_feats * beta_next
     beta_out = beta_half + half[:, None] * gb
     return (beta_next, pools_next, regions_next, beta_out, pool_out, region_out)

time: 53.5 us -> 50.8 us (0.950)
  local copies, waits for them, and re-layouts: 3.23 us -> 0.34 us
    unnamed x37 -> x33, local copies, waits for them, and re-layouts: 3.15 us -> 0.26 us
  transfers between devices with their start and end apart: 18 -> 18, of which waited for: 4 -> 3; matrix products, arithmetic and copies ran while one was open for 2% -> 2% of each run, Pallas kernels for 12% -> 16%
where the time goes in v3:
time: 50.8 us; the launch traced here: 50.6 us
  starting transfers between devices  26 us (51%)
  Pallas kernels  16.5 us (32%)
  waiting for transfers between devices  5.52 us (11%)
  other arithmetic  1.25 us (2%)
  between operations  1.07 us (2%)
    ppermute x12, starting transfers between devices, total_over(): lax.ppermute(own, axis, ahead_by(k, size, stride, group))  18.2 us
    ppermute x3, waiting for transfers between devices, shared_sum(): lax.ppermute(mine, axis, ahead_by(k, size, 1, size))  5.3 us
    ppermute x3, starting transfers between devices, shared_sum(): lax.ppermute(block(k), axis, ahead_by(k, size, 1, size)).astype(F32)  4.97 us
    pallas_call x1, Pallas kernels, first_logits(): pl.pallas_call(kernel, in_specs=[pl.BlockSpec(memory_space=pl.ANY)] * 4,...  3.96 us
    pallas_call x1, Pallas kernels, pool_step(): pl.pallas_call(kernel, in_specs=[whole()] * 4 + [smem()] + [whole()] * 2,...  3.13 us
    ppermute x3, starting transfers between devices, shared_sum(): lax.ppermute(mine, axis, ahead_by(k, size, 1, size))  2.79 us
    pallas_call x1, Pallas kernels, prior(): pl.pallas_call(kernel, in_specs=[whole(), smem(), whole(), whole(), whole...  2.75 us
    pallas_call x1, Pallas kernels, region_step(): pl.pallas_call(kernel, in_specs=[whole(), smem()] + [whole()] * 4, out_sp...  2.68 us
  transfers between devices with their start and end apart: 18, of which 3 were waited for; matrix products, arithmetic and copies ran while one was open for 2% of the time, Pallas kernels for 16%

profile of v3, /device:TPU:0, one launch (start us, length us, event | category | flops | bytes accessed | tf_op | source)
XLA Modules:
  0.0 50.6 jit_solution(7906034008695325041)
XLA Ops:
  0.7 4.0 %first_logits.1 = (bf16[64,2048]{1,0:T(8,128)(2,1)S(1)}, f32[16,2048]{1,0:T(8,128)S(1)}) custom-call(bf16[2048,1024]{1,0:T(8,128)(2,1)} %design_ref.3, s32[1,2048]{1,0:T(1,128)} %bitcast.2, f32[16,1024]{1,0:T(8,128)} %beta_hbm.1, f32[16,64,64]{2,1,0:T(8,128)} %base_ref.1), custom_call_target="tpu_custom_call" | custom-call | tf_op jit(solution)/shard_map/first_logits/pallas_call | solution.py:190
  4.7 3.0 %collective-permute-start = (f16[16,2048]{1,0:T(8,128)(2,1)S(1)}, f16[16,2048]{1,0:T(8,128)(2,1)S(1)}, u32[]{:S(2)}, u32[]{:S(2)}) collective-permute-start(f16[16,2048]{1,0:T(8,128)(2,1)S(1)} %convert_element_type.90), channel_id=1, source_target_pairs={{0,2},{1,3},{2,0},{3,1},{4,6},{5,7},{6,4},{7,5},{8,10},{9,11},{10,... | collective-permute-start | bytes 196616 | tf_op jit(solution)/shard_map/ppermute | solution.py:447
  7.7 1.7 %collective-permute-start.2 = (f16[16,2048]{1,0:T(8,128)(2,1)S(1)}, f16[16,2048]{1,0:T(8,128)(2,1)S(1)}, u32[]{:S(2)}, u32[]{:S(2)}) collective-permute-start(f16[16,2048]{1,0:T(8,128)(2,1)S(1)} %convert_element_type.90), channel_id=1, source_target_pairs={{0,3},{1,0},{2,1},{3,2},{4,7},{5,4},{6,5},{7,6},{8,11},{9,8},{10,9... | collective-permute-start | bytes 196616 | tf_op jit(solution)/shard_map/ppermute | solution.py:447
  9.5 2.7 %prior.1 = (f32[16,64,64]{2,1,0:T(8,128)S(1)}, f32[9,64,128]{2,1,0:T(8,128)S(1)}, bf16[2048,1024]{1,0:T(8,128)(2,1)S(1)}) custom-call(s32[1,64]{1,0:T(1,128)S(1)} %bitcast.5, f32[16]{0:T(128)S(1)} %copy-done.8, f32[16,64,64]{2,1,0:T(8,128)S(1)} %copy-done.1, f32[16,64,64]{2,1,0:T(8,128)S(1)} %copy-done.2, f32[16,64,64]{2,1,0:T(8,128)S(1)} %copy-done.4, ...), custom_call_target="tpu_custom_call" | custom-call | tf_op jit(solution)/shard_map/prior/pallas_call | solution.py:300
  12.4 0.6 %population_gradient.2 = f32[16,1024]{1,0:T(8,128)S(1)} custom-call(bf16[16,2048]{1,0:T(8,128)(2,1)S(1)} %subtract_convert_fusion.1.resid_ref, bf16[2048,1024]{1,0:T(8,128)(2,1)S(1)} %get-tuple-element.29.design_ref), custom_call_target="tpu_custom_call" | custom-call | tf_op jit(solution)/shard_map/population_gradient/pallas_call | solution.py:220
  13.1 2.7 %collective-permute-start.3 = (f16[16,1024]{1,0:T(8,128)(2,1)S(1)}, f16[16,1024]{1,0:T(8,128)(2,1)S(1)}, u32[]{:S(2)}, u32[]{:S(2)}) collective-permute-start(f16[16,1024]{1,0:T(8,128)(2,1)S(1)} %convert_element_type.96), channel_id=1, source_target_pairs={{0,8},{4,12},{8,0},{12,4},{1,9},{5,13},{9,1},{13,5},{2,10},{6,14},... | collective-permute-start | bytes 98312 | tf_op jit(solution)/shard_map/ppermute | solution.py:447
  15.8 1.6 %collective-permute-start.4 = (f16[16,1024]{1,0:T(8,128)(2,1)S(1)}, f16[16,1024]{1,0:T(8,128)(2,1)S(1)}, u32[]{:S(2)}, u32[]{:S(2)}) collective-permute-start(f16[16,1024]{1,0:T(8,128)(2,1)S(1)} %convert_element_type.96), channel_id=1, source_target_pairs={{0,4},{4,8},{8,12},{12,0},{1,5},{5,9},{9,13},{13,1},{2,6},{6,10},{... | collective-permute-start | bytes 98312 | tf_op jit(solution)/shard_map/ppermute | solution.py:447
  17.3 2.2 %collective-permute-start.5 = (f16[16,1024]{1,0:T(8,128)(2,1)S(1)}, f16[16,1024]{1,0:T(8,128)(2,1)S(1)}, u32[]{:S(2)}, u32[]{:S(2)}) collective-permute-start(f16[16,1024]{1,0:T(8,128)(2,1)S(1)} %convert_element_type.96), channel_id=1, source_target_pairs={{0,12},{4,0},{8,4},{12,8},{1,13},{5,1},{9,5},{13,9},{2,14},{6,2},{... | collective-permute-start | bytes 98312 | tf_op jit(solution)/shard_map/ppermute | solution.py:447
  19.6 3.1 %pool_step.1 = (f32[16,64,64]{2,1,0:T(8,128)}, f32[16,64,64]{2,1,0:T(8,128)S(1)}, f32[16,2048]{1,0:T(8,128)S(1)}, f32[8,64,128]{2,1,0:T(8,128)S(1)}) custom-call(bf16[16,2048]{1,0:T(8,128)(2,1)S(1)} %subtract_convert_fusion.1.resid_ref, bf16[64,2048]{1,0:T(8,128)(2,1)S(1)} %get-tuple-element.34.slope_ref, s32[1,2048]{1,0:T(1,128)S(1)} %bitcast.3, ...), custom_call_target="tpu_custom_call" | custom-call | tf_op jit(solution)/shard_map/pool_step/pallas_call | solution.py:337
  23.0 1.2 %next_logits.1 = f32[16,2048]{1,0:T(8,128)S(1)} custom-call(bf16[2048,1024]{1,0:T(8,128)(2,1)S(1)} %copy-done, f32[16,1024]{1,0:T(8,128)S(1)} %multiply_add_fusion.1.coef_ref, f32[16,2048]{1,0:T(8,128)S(1)} %get-tuple-element.39.term_ref), custom_call_target="tpu_custom_call" | custom-call | tf_op jit(solution)/shard_map/next_logits/pallas_call | solution.py:422
  24.3 0.6 %collective-permute-start.12 = (f16[16,2048]{1,0:T(8,128)(2,1)S(1)}, f16[16,2048]{1,0:T(8,128)(2,1)S(1)}, u32[]{:S(2)}, u32[]{:S(2)}) collective-permute-start(f16[16,2048]{1,0:T(8,128)(2,1)S(1)} %convert_element_type.107), channel_id=1, source_target_pairs={{0,2},{1,3},{2,0},{3,1},{4,6},{5,7},{6,4},{7,5},{8,10},{9,11},{10,... | collective-permute-start | bytes 196616 | tf_op jit(solution)/shard_map/ppermute | solution.py:447
  24.9 1.7 %collective-permute-start.14 = (f16[16,2048]{1,0:T(8,128)(2,1)S(1)}, f16[16,2048]{1,0:T(8,128)(2,1)S(1)}, u32[]{:S(2)}, u32[]{:S(2)}) collective-permute-start(f16[16,2048]{1,0:T(8,128)(2,1)S(1)} %convert_element_type.107), channel_id=1, source_target_pairs={{0,3},{1,0},{2,1},{3,2},{4,7},{5,4},{6,5},{7,6},{8,11},{9,8},{10,9... | collective-permute-start | bytes 196616 | tf_op jit(solution)/shard_map/ppermute | solution.py:447
  26.7 2.9 %collective-permute-start.7 = (f16[17,16,128]{2,1,0:T(8,128)(2,1)S(1)}, f16[17,16,128]{2,1,0:T(8,128)(2,1)S(1)}, u32[]{:S(2)}, u32[]{:S(2)}) collective-permute-start(f16[17,16,128]{2,1,0:T(8,128)(2,1)S(1)} %get-tuple-element.48), channel_id=1, source_target_pairs={{0,8},{4,12},{8,0},{12,4},{1,9},{5,13},{9,1},{13,5},{2,10},{6,14},... | collective-permute-start | bytes 208904 | tf_op jit(solution)/shard_map/ppermute | solution.py:466
  29.7 2.0 %collective-permute-start.8 = (f16[17,16,128]{2,1,0:T(8,128)(2,1)S(1)}, f16[17,16,128]{2,1,0:T(8,128)(2,1)S(1)}, u32[]{:S(2)}, u32[]{:S(2)}) collective-permute-start(f16[17,16,128]{2,1,0:T(8,128)(2,1)S(1)} %get-tuple-element.47), channel_id=1, source_target_pairs={{0,12},{4,0},{8,4},{12,8},{1,13},{5,1},{9,5},{13,9},{2,14},{6,2},{... | collective-permute-start | bytes 208904 | tf_op jit(solution)/shard_map/ppermute | solution.py:466
  31.7 0.6 %population_gradient.3 = f32[16,1024]{1,0:T(8,128)S(1)} custom-call(bf16[16,2048]{1,0:T(8,128)(2,1)S(1)} %subtract_convert_fusion.resid_ref, bf16[2048,1024]{1,0:T(8,128)(2,1)S(1)} %copy-done), custom_call_target="tpu_custom_call" | custom-call | tf_op jit(solution)/shard_map/population_gradient/pallas_call | solution.py:220
  32.4 1.0 %collective-permute-start.15 = (f16[16,1024]{1,0:T(8,128)(2,1)S(1)}, f16[16,1024]{1,0:T(8,128)(2,1)S(1)}, u32[]{:S(2)}, u32[]{:S(2)}) collective-permute-start(f16[16,1024]{1,0:T(8,128)(2,1)S(1)} %convert_element_type.113), channel_id=1, source_target_pairs={{0,8},{4,12},{8,0},{12,4},{1,9},{5,13},{9,1},{13,5},{2,10},{6,14},... | collective-permute-start | bytes 98312 | tf_op jit(solution)/shard_map/ppermute | solution.py:447
  33.6 3.6 %collective-permute-start.17 = (f16[16,1024]{1,0:T(8,128)(2,1)S(1)}, f16[16,1024]{1,0:T(8,128)(2,1)S(1)}, u32[]{:S(2)}, u32[]{:S(2)}) collective-permute-start(f16[16,1024]{1,0:T(8,128)(2,1)S(1)} %convert_element_type.113), channel_id=1, source_target_pairs={{0,12},{4,0},{8,4},{12,8},{1,13},{5,1},{9,5},{13,9},{2,14},{6,2},{... | collective-permute-start | bytes 98312 | tf_op jit(solution)/shard_map/ppermute | solution.py:447
  37.3 1.4 %collective-permute-start.9 = (f16[17,16,128]{2,1,0:T(8,128)(2,1)S(1)}, f16[17,16,128]{2,1,0:T(8,128)(2,1)S(1)}, u32[]{:S(2)}, u32[]{:S(2)}) collective-permute-start(f16[17,16,128]{2,1,0:T(8,128)(2,1)S(1)} %add_convert_fusion), channel_id=1, source_target_pairs={{0,12},{4,0},{8,4},{12,8},{1,13},{5,1},{9,5},{13,9},{2,14},{6,2},{... | collective-permute-start | bytes 208904 | tf_op jit(solution)/shard_map/ppermute | solution.py:468
  38.7 1.3 %collective-permute-start.10 = (f16[17,16,128]{2,1,0:T(8,128)(2,1)S(1)}, f16[17,16,128]{2,1,0:T(8,128)(2,1)S(1)}, u32[]{:S(2)}, u32[]{:S(2)}) collective-permute-start(f16[17,16,128]{2,1,0:T(8,128)(2,1)S(1)} %add_convert_fusion), channel_id=1, source_target_pairs={{0,8},{4,12},{8,0},{12,4},{1,9},{5,13},{9,1},{13,5},{2,10},{6,14},... | collective-permute-start | bytes 208904 | tf_op jit(solution)/shard_map/ppermute | solution.py:468
  40.0 1.5 %pool_likelihood.1.part_ref = f32[16,64,64]{2,1,0:T(8,128)S(1)} custom-call(bf16[16,2048]{1,0:T(8,128)(2,1)S(1)} %subtract_convert_fusion.resid_ref, bf16[64,2048]{1,0:T(8,128)(2,1)S(1)} %get-tuple-element.34.slope_ref, s32[1,2048]{1,0:T(1,128)S(1)} %bitcast.4, f32[16]{0:T(128)S(1)} %copy-done.8, f32[16,64,64]{2,1,0:T(8,128)S(1)} %get-tuple-element.41.half_ref, ...), custom_call_target="tpu_custom_call" | custom-call | tf_op jit(solution)/shard_map/pool_likelihood/pallas_call | solution.py:401
  41.6 0.7 %multiply_add_fusion = f32[16,1024]{1,0:T(8,128)} fusion(f32[16,1024]{1,0:T(8,128)S(1)} %multiply_add_fusion.1.coef_ref, f16[16,1024]{1,0:T(8,128)(2,1)S(1)} %collective-permute-done.17, f16[16,1024]{1,0:T(8,128)(2,1)S(1)} %collective-permute-done.16, f16[16,1024]{1,0:T(8,128)(2,1)S(1)} %collective-permute-done.15, ...), kind=kLoop, calls=%fused_computation.5 | loop fusion | flops 393216 | bytes 524352 | tf_op jit(solution)/shard_map/add | solution.py:525
  42.4 3.1 %collective-permute-done.10 = f16[17,16,128]{2,1,0:T(8,128)(2,1)S(1)} collective-permute-done((f16[17,16,128]{2,1,0:T(8,128)(2,1)S(1)}, f16[17,16,128]{2,1,0:T(8,128)(2,1)S(1)}, u32[]{:S(2)}, u32[]{:S(2)}) %collective-permute-start.10) | collective-permute-done | bytes 69664 | tf_op jit(solution)/shard_map/ppermute | solution.py:468
  45.5 2.2 %collective-permute-done.11 = f16[17,16,128]{2,1,0:T(8,128)(2,1)S(1)} collective-permute-done((f16[17,16,128]{2,1,0:T(8,128)(2,1)S(1)}, f16[17,16,128]{2,1,0:T(8,128)(2,1)S(1)}, u32[]{:S(2)}, u32[]{:S(2)}) %collective-permute-start.11) | collective-permute-done | bytes 69664 | tf_op jit(solution)/shard_map/ppermute | solution.py:468
  47.9 2.7 %region_step.1 = (f32[16,64,64]{2,1,0:T(8,128)}, f32[16,64,64]{2,1,0:T(8,128)}, f32[16,64,64]{2,1,0:T(8,128)}) custom-call(s32[1,64]{1,0:T(1,128)S(1)} %bitcast.7, f32[16]{0:T(128)S(1)} %copy-done.8, f32[17,64,128]{2,1,0:T(8,128)S(1)} %dynamic-slice_convert_fusion.sums_ref, f32[16,64,64]{2,1,0:T(8,128)S(1)} %copy-done.2, f32[16,64,64]{2,1,0:T(8,128)S(1)} %copy-done.5, ...), custom_call_target="tpu_custom_call" | custom-call | tf_op jit(solution)/shard_map/region_step/pallas_call | solution.py:379
  (70 shorter events, 1.2 us)
Async XLA Ops:
  4.7 7.6 %collective-permute-start = (f16[16,2048]{1,0:T(8,128)(2,1)S(1)}, f16[16,2048]{1,0:T(8,128)(2,1)S(1)}, u32[]{:S(2)}, u32[]{:S(2)}) collective-permute-start(f16[16,2048]{1,0:T(8,128)(2,1)S(1)} %convert_element_type.90), channel_id=1, source_target_pairs={{0,2},{1,3},{2,0},{3,1},{4,6},{5,7},{6,4},{7,5},{8,10},{9,11},{10,... | collective-permute-start | bytes 196616 | tf_op jit(solution)/shard_map/ppermute | solution.py:447
  7.7 4.7 %collective-permute-start.1 = (f16[16,2048]{1,0:T(8,128)(2,1)S(1)}, f16[16,2048]{1,0:T(8,128)(2,1)S(1)}, u32[]{:S(2)}, u32[]{:S(2)}) collective-permute-start(f16[16,2048]{1,0:T(8,128)(2,1)S(1)} %convert_element_type.90), channel_id=1, source_target_pairs={{0,1},{1,2},{2,3},{3,0},{4,5},{5,6},{6,7},{7,4},{8,9},{9,10},{10,1... | collective-permute-start | bytes 196616 | tf_op jit(solution)/shard_map/ppermute | solution.py:447
  7.7 4.7 %collective-permute-start.2 = (f16[16,2048]{1,0:T(8,128)(2,1)S(1)}, f16[16,2048]{1,0:T(8,128)(2,1)S(1)}, u32[]{:S(2)}, u32[]{:S(2)}) collective-permute-start(f16[16,2048]{1,0:T(8,128)(2,1)S(1)} %convert_element_type.90), channel_id=1, source_target_pairs={{0,3},{1,0},{2,1},{3,2},{4,7},{5,4},{6,5},{7,6},{8,11},{9,8},{10,9... | collective-permute-start | bytes 196616 | tf_op jit(solution)/shard_map/ppermute | solution.py:447
  12.3 10.6 %copy-start.10 = (f32[16,1024]{1,0:T(8,128)S(1)}, f32[16,1024]{1,0:T(8,128)}, u32[]{:S(2)}) copy-start(f32[16,1024]{1,0:T(8,128)} %beta_hbm.1) | copy-start | bytes 196612
  12.3 10.6 %copy-start.11 = (f32[16,1024]{1,0:T(8,128)S(1)}, f32[16,1024]{1,0:T(8,128)}, u32[]{:S(2)}) copy-start(f32[16,1024]{1,0:T(8,128)} %param.19) | copy-start | bytes 196612
  12.3 10.7 %copy-start = (bf16[2048,1024]{1,0:T(8,128)(2,1)S(1)}, bf16[2048,1024]{1,0:T(8,128)(2,1)}, u32[]{:S(2)}) copy-start(bf16[2048,1024]{1,0:T(8,128)(2,1)} %design_ref.3) | copy-start | bytes 12582916
  13.1 9.8 %collective-permute-start.3 = (f16[16,1024]{1,0:T(8,128)(2,1)S(1)}, f16[16,1024]{1,0:T(8,128)(2,1)S(1)}, u32[]{:S(2)}, u32[]{:S(2)}) collective-permute-start(f16[16,1024]{1,0:T(8,128)(2,1)S(1)} %convert_element_type.96), channel_id=1, source_target_pairs={{0,8},{4,12},{8,0},{12,4},{1,9},{5,13},{9,1},{13,5},{2,10},{6,14},... | collective-permute-start | bytes 98312 | tf_op jit(solution)/shard_map/ppermute | solution.py:447
  15.8 7.1 %collective-permute-start.4 = (f16[16,1024]{1,0:T(8,128)(2,1)S(1)}, f16[16,1024]{1,0:T(8,128)(2,1)S(1)}, u32[]{:S(2)}, u32[]{:S(2)}) collective-permute-start(f16[16,1024]{1,0:T(8,128)(2,1)S(1)} %convert_element_type.96), channel_id=1, source_target_pairs={{0,4},{4,8},{8,12},{12,0},{1,5},{5,9},{9,13},{13,1},{2,6},{6,10},{... | collective-permute-start | bytes 98312 | tf_op jit(solution)/shard_map/ppermute | solution.py:447
  17.3 5.5 %collective-permute-start.5 = (f16[16,1024]{1,0:T(8,128)(2,1)S(1)}, f16[16,1024]{1,0:T(8,128)(2,1)S(1)}, u32[]{:S(2)}, u32[]{:S(2)}) collective-permute-start(f16[16,1024]{1,0:T(8,128)(2,1)S(1)} %convert_element_type.96), channel_id=1, source_target_pairs={{0,12},{4,0},{8,4},{12,8},{1,13},{5,1},{9,5},{13,9},{2,14},{6,2},{... | collective-permute-start | bytes 98312 | tf_op jit(solution)/shard_map/ppermute | solution.py:447
  23.0 18.6 %copy-start.3 = (f32[16,1024]{1,0:T(8,128)}, f32[16,1024]{1,0:T(8,128)S(1)}, u32[]{:S(2)}) copy-start(f32[16,1024]{1,0:T(8,128)S(1)} %multiply_add_fusion.1.coef_ref) | copy-start | bytes 196612
  23.0 17.0 %copy-start.6 = (f32[16,64,64]{2,1,0:T(8,128)S(1)}, f32[16,64,64]{2,1,0:T(8,128)}, u32[]{:S(2)}) copy-start(f32[16,64,64]{2,1,0:T(8,128)} %get-tuple-element.21.u_ref) | copy-start | bytes 786436
  24.3 5.4 %collective-permute-start.12 = (f16[16,2048]{1,0:T(8,128)(2,1)S(1)}, f16[16,2048]{1,0:T(8,128)(2,1)S(1)}, u32[]{:S(2)}, u32[]{:S(2)}) collective-permute-start(f16[16,2048]{1,0:T(8,128)(2,1)S(1)} %convert_element_type.107), channel_id=1, source_target_pairs={{0,2},{1,3},{2,0},{3,1},{4,6},{5,7},{6,4},{7,5},{8,10},{9,11},{10,... | collective-permute-start | bytes 196616 | tf_op jit(solution)/shard_map/ppermute | solution.py:447
  24.9 6.8 %collective-permute-start.13 = (f16[16,2048]{1,0:T(8,128)(2,1)S(1)}, f16[16,2048]{1,0:T(8,128)(2,1)S(1)}, u32[]{:S(2)}, u32[]{:S(2)}) collective-permute-start(f16[16,2048]{1,0:T(8,128)(2,1)S(1)} %convert_element_type.107), channel_id=1, source_target_pairs={{0,1},{1,2},{2,3},{3,0},{4,5},{5,6},{6,7},{7,4},{8,9},{9,10},{10,1... | collective-permute-start | bytes 196616 | tf_op jit(solution)/shard_map/ppermute | solution.py:447
  24.9 6.8 %collective-permute-start.14 = (f16[16,2048]{1,0:T(8,128)(2,1)S(1)}, f16[16,2048]{1,0:T(8,128)(2,1)S(1)}, u32[]{:S(2)}, u32[]{:S(2)}) collective-permute-start(f16[16,2048]{1,0:T(8,128)(2,1)S(1)} %convert_element_type.107), channel_id=1, source_target_pairs={{0,3},{1,0},{2,1},{3,2},{4,7},{5,4},{6,5},{7,6},{8,11},{9,8},{10,9... | collective-permute-start | bytes 196616 | tf_op jit(solution)/shard_map/ppermute | solution.py:447
  26.7 6.9 %collective-permute-start.6 = (f16[17,16,128]{2,1,0:T(8,128)(2,1)S(1)}, f16[17,16,128]{2,1,0:T(8,128)(2,1)S(1)}, u32[]{:S(2)}, u32[]{:S(2)}) collective-permute-start(f16[17,16,128]{2,1,0:T(8,128)(2,1)S(1)} %get-tuple-element.46), channel_id=1, source_target_pairs={{0,4},{4,8},{8,12},{12,0},{1,5},{5,9},{9,13},{13,1},{2,6},{6,10},{... | collective-permute-start | bytes 208904 | tf_op jit(solution)/shard_map/ppermute | solution.py:466
  26.7 10.5 %collective-permute-start.7 = (f16[17,16,128]{2,1,0:T(8,128)(2,1)S(1)}, f16[17,16,128]{2,1,0:T(8,128)(2,1)S(1)}, u32[]{:S(2)}, u32[]{:S(2)}) collective-permute-start(f16[17,16,128]{2,1,0:T(8,128)(2,1)S(1)} %get-tuple-element.48), channel_id=1, source_target_pairs={{0,8},{4,12},{8,0},{12,4},{1,9},{5,13},{9,1},{13,5},{2,10},{6,14},... | collective-permute-start | bytes 208904 | tf_op jit(solution)/shard_map/ppermute | solution.py:466
  29.7 7.6 %collective-permute-start.8 = (f16[17,16,128]{2,1,0:T(8,128)(2,1)S(1)}, f16[17,16,128]{2,1,0:T(8,128)(2,1)S(1)}, u32[]{:S(2)}, u32[]{:S(2)}) collective-permute-start(f16[17,16,128]{2,1,0:T(8,128)(2,1)S(1)} %get-tuple-element.47), channel_id=1, source_target_pairs={{0,12},{4,0},{8,4},{12,8},{1,13},{5,1},{9,5},{13,9},{2,14},{6,2},{... | collective-permute-start | bytes 208904 | tf_op jit(solution)/shard_map/ppermute | solution.py:466
  31.7 16.2 %copy-start.5 = (f32[16,64,64]{2,1,0:T(8,128)S(1)}, f32[16,64,64]{2,1,0:T(8,128)}, u32[]{:S(2)}) copy-start(f32[16,64,64]{2,1,0:T(8,128)} %m_ref.1) | copy-start | bytes 786436
  32.4 9.1 %collective-permute-start.15 = (f16[16,1024]{1,0:T(8,128)(2,1)S(1)}, f16[16,1024]{1,0:T(8,128)(2,1)S(1)}, u32[]{:S(2)}, u32[]{:S(2)}) collective-permute-start(f16[16,1024]{1,0:T(8,128)(2,1)S(1)} %convert_element_type.113), channel_id=1, source_target_pairs={{0,8},{4,12},{8,0},{12,4},{1,9},{5,13},{9,1},{13,5},{2,10},{6,14},... | collective-permute-start | bytes 98312 | tf_op jit(solution)/shard_map/ppermute | solution.py:447
  33.4 8.2 %collective-permute-start.16 = (f16[16,1024]{1,0:T(8,128)(2,1)S(1)}, f16[16,1024]{1,0:T(8,128)(2,1)S(1)}, u32[]{:S(2)}, u32[]{:S(2)}) collective-permute-start(f16[16,1024]{1,0:T(8,128)(2,1)S(1)} %convert_element_type.113), channel_id=1, source_target_pairs={{0,4},{4,8},{8,12},{12,0},{1,5},{5,9},{9,13},{13,1},{2,6},{6,10},{... | collective-permute-start | bytes 98312 | tf_op jit(solution)/shard_map/ppermute | solution.py:447
  33.6 8.0 %collective-permute-start.17 = (f16[16,1024]{1,0:T(8,128)(2,1)S(1)}, f16[16,1024]{1,0:T(8,128)(2,1)S(1)}, u32[]{:S(2)}, u32[]{:S(2)}) collective-permute-start(f16[16,1024]{1,0:T(8,128)(2,1)S(1)} %convert_element_type.113), channel_id=1, source_target_pairs={{0,12},{4,0},{8,4},{12,8},{1,13},{5,1},{9,5},{13,9},{2,14},{6,2},{... | collective-permute-start | bytes 98312 | tf_op jit(solution)/shard_map/ppermute | solution.py:447
  37.3 5.0 %collective-permute-start.9 = (f16[17,16,128]{2,1,0:T(8,128)(2,1)S(1)}, f16[17,16,128]{2,1,0:T(8,128)(2,1)S(1)}, u32[]{:S(2)}, u32[]{:S(2)}) collective-permute-start(f16[17,16,128]{2,1,0:T(8,128)(2,1)S(1)} %add_convert_fusion), channel_id=1, source_target_pairs={{0,12},{4,0},{8,4},{12,8},{1,13},{5,1},{9,5},{13,9},{2,14},{6,2},{... | collective-permute-start | bytes 208904 | tf_op jit(solution)/shard_map/ppermute | solution.py:468
  38.7 6.7 %collective-permute-start.10 = (f16[17,16,128]{2,1,0:T(8,128)(2,1)S(1)}, f16[17,16,128]{2,1,0:T(8,128)(2,1)S(1)}, u32[]{:S(2)}, u32[]{:S(2)}) collective-permute-start(f16[17,16,128]{2,1,0:T(8,128)(2,1)S(1)} %add_convert_fusion), channel_id=1, source_target_pairs={{0,8},{4,12},{8,0},{12,4},{1,9},{5,13},{9,1},{13,5},{2,10},{6,14},... | collective-permute-start | bytes 208904 | tf_op jit(solution)/shard_map/ppermute | solution.py:468
  41.5 6.2 %collective-permute-start.11 = (f16[17,16,128]{2,1,0:T(8,128)(2,1)S(1)}, f16[17,16,128]{2,1,0:T(8,128)(2,1)S(1)}, u32[]{:S(2)}, u32[]{:S(2)}) collective-permute-start(f16[17,16,128]{2,1,0:T(8,128)(2,1)S(1)} %add_convert_fusion), channel_id=1, source_target_pairs={{0,4},{4,8},{8,12},{12,0},{1,5},{5,9},{9,13},{13,1},{2,6},{6,10},{... | collective-permute-start | bytes 208904 | tf_op jit(solution)/shard_map/ppermute | solution.py:468
  (7 other events, 63.0 us)

commit v4 on v3

--- a/solution.py
+++ b/solution.py
@@ -11,6 +11,8 @@
 OCTET = 8
 SPAN = 3
 CHUNKS = 2
+LANES = 128
+COPIES = 1
 VMEM_LIMIT = 24 * 1024 * 1024
 NT = (((1,), (1,)), ((), ()))
 NN = (((1,), (0,)), ((), ()))
@@ -212,16 +214,20 @@
 
 
 def population_gradient(resid, design):
+    planes = design.shape[1] // LANES
+
     def kernel(resid_ref, design_ref, out_ref):
-        out_ref[...] = SCALE * lax.dot_general(
+        total = SCALE * lax.dot_general(
             resid_ref[...], design_ref[...], NN, preferred_element_type=F32
         )
+        for k in range(planes):
+            out_ref[k] = total[:, k * LANES : (k + 1) * LANES]
 
     return pl.pallas_call(
         kernel,
         in_specs=[whole(), whole()],
         out_specs=whole(),
-        out_shape=jax.ShapeDtypeStruct((resid.shape[0], design.shape[1]), F32),
+        out_shape=jax.ShapeDtypeStruct((planes, resid.shape[0], LANES), F32),
         compiler_params=params(),
         name="population_gradient",
     )(resid, in_vmem(design))
@@ -280,9 +286,13 @@
     n_regions = regions.shape[1]
     pairs = chains // 2
 
-    def kernel(index_ref, step_ref, pools_ref, regions_ref, mom_ref, design_hbm, base_ref, sums_ref, kept, sem):
-        copy = pltpu.make_async_copy(design_hbm, kept, sem)
-        copy.start()
+    def kernel(index_ref, step_ref, pools_ref, regions_ref, mom_ref, design_hbm, base_ref, sums_ref, kept, sems):
+        size = design_hbm.shape[0] // COPIES
+        copies = []
+        for k in range(COPIES):
+            part = pl.ds(k * size, size)
+            copies.append(pltpu.make_async_copy(design_hbm.at[part], kept.at[part], sems.at[k]))
+            copies[k].start()
         onehot = region_onehot(index_ref, n_regions)
         chosen = chosen_regions(onehot, regions_ref[...])
         dev = [PREC * (pools_ref[c] - chosen[c]) for c in range(chains)]
@@ -295,7 +305,8 @@
         region_sums(onehot, dev, 3, store)
         count = jnp.sum(onehot, axis=1, keepdims=True)
         sums_ref[pairs] = SCALE * jnp.broadcast_to(count, (n_regions, 2 * slopes))
-        copy.wait()
+        for copy in copies:
+            copy.wait()
 
     return pl.pallas_call(
         kernel,
@@ -306,7 +317,7 @@
             jax.ShapeDtypeStruct((pairs + 1, n_regions, 2 * slopes), F32),
             pltpu.VMEM(design.shape, BF16),
         ],
-        scratch_shapes=[pltpu.SemaphoreType.DMA],
+        scratch_shapes=[pltpu.SemaphoreType.DMA((COPIES,))],
         compiler_params=params(),
         name="prior",
     )(index, step, pools, regions, momentum, in_hbm(design))
@@ -452,7 +463,7 @@
     return x
 
 
-def shared_sum(x, axis):
+def own_block(x, axis):
     size = lax.axis_size(axis)
     me = lax.axis_index(axis)
     width = x.shape[1] // size
@@ -464,10 +475,39 @@
     mine = block(0).astype(F32)
     for k in range(1, size):
         mine = mine + lax.ppermute(block(k), axis, ahead_by(k, size, 1, size)).astype(F32)
-    mine = lax.optimization_barrier(mine.astype(jnp.float16))
-    found = [mine] + [lax.ppermute(mine, axis, ahead_by(k, size, 1, size)) for k in range(1, size)]
-    back = jnp.concatenate(found[::-1], axis=1)
-    return jnp.roll(back, (me + 1) * width, axis=1).astype(F32)
+    return mine.astype(jnp.float16)
+
+
+def all_shifts(x, axis):
+    size = lax.axis_size(axis)
+    x = lax.optimization_barrier(x)
+    return [x] + [lax.ppermute(x, axis, ahead_by(k, size, 1, size)) for k in range(1, size)]
+
+
+def in_order(parts, axis):
+    size = lax.axis_size(axis)
+    me = lax.axis_index(axis)
+    width = parts[0].shape[1]
+    found = jnp.zeros((parts[0].shape[0], size * width) + parts[0].shape[2:], parts[0].dtype)
+    for k, part in enumerate(parts):
+        at = lax.rem(me + size - k, size) * width
+        found = lax.dynamic_update_slice_in_dim(found, part, at, 1)
+    return found.astype(F32)
+
+
+def total_and_blocks(gb, mine, axis):
+    size = lax.axis_size(axis)
+    if size > 4 or mine.shape[1] != gb.shape[1] or mine.shape[2] != gb.shape[2]:
+        return total_over(gb, axis), in_order(all_shifts(mine, axis), axis)
+    planes = gb.shape[0]
+    parts = all_shifts(jnp.concatenate([gb.astype(jnp.float16), mine], axis=0), axis)
+    g = [part[:planes].astype(F32) for part in parts]
+    total = g[0] if size == 1 else g[0] + g[1] if size == 2 else (g[0] + g[2]) + (g[1] + g[3])
+    return total, in_order([part[planes:] for part in parts], axis)
+
+
+def flat(planes):
+    return jnp.concatenate(list(planes), axis=1)
 
 
 def residual(part, labels):
@@ -508,8 +548,8 @@
     pools_next, pool_half, term, way_sums = pool_step(
         resid, slope, ids, index, step_size, pools, mom_base, n_regions
     )
-    sums = shared_sum(jnp.concatenate([dev_sums, way_sums], axis=0), "loan")
-    gb = total_over(gb, "loan") * (1.0 / SCALE) - total_feats * beta
+    mine = own_block(jnp.concatenate([dev_sums, way_sums], axis=0), "loan")
+    gb = flat(total_over(gb, "loan")) * (1.0 / SCALE) - total_feats * beta
     beta_half = beta_momentum + half[:, None] * gb
     beta_next = beta + step_size[:, None] * beta_half
 
@@ -518,10 +558,11 @@
     gb = population_gradient(resid, design)
     resid, gb = lax.optimization_barrier((resid, gb))
     pool_part = pool_likelihood(resid, slope, ids, step_size, pool_half, pools_next)
+    gb, sums = total_and_blocks(gb, mine, "loan")
     regions_next, region_out, pool_out = region_step(
         index, step_size, sums, regions, region_momentum, pool_part
     )
-    gb = total_over(gb, "loan") * (1.0 / SCALE) - total_feats * beta_next
+    gb = flat(gb) * (1.0 / SCALE) - total_feats * beta_next
     beta_out = beta_half + half[:, None] * gb
     return (beta_next, pools_next, regions_next, beta_out, pool_out, region_out)
 

time: 50.8 us -> 48.3 us (0.951)
  starting transfers between devices: 26 us -> 19.8 us
  waiting for transfers between devices: 5.52 us -> 8.98 us
    ppermute x12 -> x9, starting transfers between devices: 18.2 us -> 11.8 us  [total_over(): lax.ppermute(own, axis, ahead_by(k, size, stride, group))]
    ppermute x6, waiting for transfers between devices: 5.49 us -> 8.63 us  [the longest x3 4.64 us: all_shifts(): lax.ppermute(x, axis, ahead_by(k, size, 1, size))]
  transfers between devices with their start and end apart: 18 -> 15, of which waited for: 3 -> 5; matrix products, arithmetic and copies ran while one was open for 2% -> 1% of each run, Pallas kernels for 16% -> 18%
where the time goes in v4:
time: 48.3 us; the launch traced here: 48.1 us
  starting transfers between devices  19.8 us (41%)
  Pallas kernels  16.5 us (34%)
  waiting for transfers between devices  8.98 us (19%)
  other arithmetic  1.32 us (3%)
  between operations  1.17 us (2%)
    ppermute x9, starting transfers between devices, total_over(): lax.ppermute(own, axis, ahead_by(k, size, stride, group))  11.8 us
    ppermute x3, starting transfers between devices, all_shifts(): lax.ppermute(x, axis, ahead_by(k, size, 1, size))  5.77 us
    ppermute x3, waiting for transfers between devices, all_shifts(): lax.ppermute(x, axis, ahead_by(k, size, 1, size))  4.64 us
    ppermute x3, waiting for transfers between devices, own_block(): lax.ppermute(block(k), axis, ahead_by(k, size, 1, size)).astype(F32)  3.99 us
    pallas_call x1, Pallas kernels, first_logits(): pl.pallas_call(kernel, in_specs=[pl.BlockSpec(memory_space=pl.ANY)] * 4,...  3.96 us
    pallas_call x1, Pallas kernels, pool_step(): pl.pallas_call(kernel, in_specs=[whole()] * 4 + [smem()] + [whole()] * 2,...  3.13 us
    pallas_call x1, Pallas kernels, prior(): pl.pallas_call(kernel, in_specs=[whole(), smem(), whole(), whole(), whole...  2.75 us
    pallas_call x1, Pallas kernels, region_step(): pl.pallas_call(kernel, in_specs=[whole(), smem()] + [whole()] * 4, out_sp...  2.68 us
  transfers between devices with their start and end apart: 15, of which 5 were waited for; matrix products, arithmetic and copies ran while one was open for 1% of the time, Pallas kernels for 18%

profile of v4, /device:TPU:0, one launch (start us, length us, event | category | flops | bytes accessed | tf_op | source)
XLA Modules:
  0.0 48.1 jit_solution(10556316081426028599)
XLA Ops:
  0.7 4.0 %first_logits.1 = (bf16[64,2048]{1,0:T(8,128)(2,1)S(1)}, f32[16,2048]{1,0:T(8,128)S(1)}) custom-call(bf16[2048,1024]{1,0:T(8,128)(2,1)} %design_ref.3, s32[1,2048]{1,0:T(1,128)} %bitcast.66, f32[16,1024]{1,0:T(8,128)} %beta_hbm.1, f32[16,64,64]{2,1,0:T(8,128)} %base_ref.1), custom_call_target="tpu_custom_call" | custom-call | tf_op jit(solution)/shard_map/first_logits/pallas_call | solution.py:192
  4.7 3.0 %collective-permute-start = (f16[16,2048]{1,0:T(8,128)(2,1)S(1)}, f16[16,2048]{1,0:T(8,128)(2,1)S(1)}, u32[]{:S(2)}, u32[]{:S(2)}) collective-permute-start(f16[16,2048]{1,0:T(8,128)(2,1)S(1)} %convert_element_type.90), channel_id=1, source_target_pairs={{0,2},{1,3},{2,0},{3,1},{4,6},{5,7},{6,4},{7,5},{8,10},{9,11},{10,... | collective-permute-start | bytes 196616 | tf_op jit(solution)/shard_map/ppermute | solution.py:458
  7.7 1.7 %collective-permute-start.2 = (f16[16,2048]{1,0:T(8,128)(2,1)S(1)}, f16[16,2048]{1,0:T(8,128)(2,1)S(1)}, u32[]{:S(2)}, u32[]{:S(2)}) collective-permute-start(f16[16,2048]{1,0:T(8,128)(2,1)S(1)} %convert_element_type.90), channel_id=1, source_target_pairs={{0,3},{1,0},{2,1},{3,2},{4,7},{5,4},{6,5},{7,6},{8,11},{9,8},{10,9... | collective-permute-start | bytes 196616 | tf_op jit(solution)/shard_map/ppermute | solution.py:458
  9.5 2.7 %prior.1 = (f32[16,64,64]{2,1,0:T(8,128)S(1)}, f32[9,64,128]{2,1,0:T(8,128)S(1)}, bf16[2048,1024]{1,0:T(8,128)(2,1)S(1)}) custom-call(s32[1,64]{1,0:T(1,128)S(1)} %bitcast.69, f32[16]{0:T(128)S(1)} %copy-done.8, f32[16,64,64]{2,1,0:T(8,128)S(1)} %copy-done.1, f32[16,64,64]{2,1,0:T(8,128)S(1)} %copy-done.2, f32[16,64,64]{2,1,0:T(8,128)S(1)} %copy-done.4, ...), custom_call_target="tpu_custom_call" | custom-call | tf_op jit(solution)/shard_map/prior/pallas_call | solution.py:311
  12.4 0.6 %population_gradient.2 = f32[8,16,128]{2,1,0:T(8,128)S(1)} custom-call(bf16[16,2048]{1,0:T(8,128)(2,1)S(1)} %subtract_convert_fusion.1.resid_ref, bf16[2048,1024]{1,0:T(8,128)(2,1)S(1)} %get-tuple-element.29.design_ref), custom_call_target="tpu_custom_call" | custom-call | tf_op jit(solution)/shard_map/population_gradient/pallas_call | solution.py:226
  13.1 2.7 %collective-permute-start.3 = (f16[8,16,128]{2,1,0:T(8,128)(2,1)S(1)}, f16[8,16,128]{2,1,0:T(8,128)(2,1)S(1)}, u32[]{:S(2)}, u32[]{:S(2)}) collective-permute-start(f16[8,16,128]{2,1,0:T(8,128)(2,1)S(1)} %convert_element_type.96), channel_id=1, source_target_pairs={{0,8},{4,12},{8,0},{12,4},{1,9},{5,13},{9,1},{13,5},{2,10},{6,14},... | collective-permute-start | bytes 98312 | tf_op jit(solution)/shard_map/ppermute | solution.py:458
  15.8 1.6 %collective-permute-start.4 = (f16[8,16,128]{2,1,0:T(8,128)(2,1)S(1)}, f16[8,16,128]{2,1,0:T(8,128)(2,1)S(1)}, u32[]{:S(2)}, u32[]{:S(2)}) collective-permute-start(f16[8,16,128]{2,1,0:T(8,128)(2,1)S(1)} %convert_element_type.96), channel_id=1, source_target_pairs={{0,4},{4,8},{8,12},{12,0},{1,5},{5,9},{9,13},{13,1},{2,6},{6,10},{... | collective-permute-start | bytes 98312 | tf_op jit(solution)/shard_map/ppermute | solution.py:458
  17.3 2.2 %collective-permute-start.5 = (f16[8,16,128]{2,1,0:T(8,128)(2,1)S(1)}, f16[8,16,128]{2,1,0:T(8,128)(2,1)S(1)}, u32[]{:S(2)}, u32[]{:S(2)}) collective-permute-start(f16[8,16,128]{2,1,0:T(8,128)(2,1)S(1)} %convert_element_type.96), channel_id=1, source_target_pairs={{0,12},{4,0},{8,4},{12,8},{1,13},{5,1},{9,5},{13,9},{2,14},{6,2},{... | collective-permute-start | bytes 98312 | tf_op jit(solution)/shard_map/ppermute | solution.py:458
  19.6 3.1 %pool_step.1 = (f32[16,64,64]{2,1,0:T(8,128)}, f32[16,64,64]{2,1,0:T(8,128)S(1)}, f32[16,2048]{1,0:T(8,128)S(1)}, f32[8,64,128]{2,1,0:T(8,128)S(1)}) custom-call(bf16[16,2048]{1,0:T(8,128)(2,1)S(1)} %subtract_convert_fusion.1.resid_ref, bf16[64,2048]{1,0:T(8,128)(2,1)S(1)} %get-tuple-element.34.slope_ref, s32[1,2048]{1,0:T(1,128)S(1)} %bitcast.67, ...), custom_call_target="tpu_custom_call" | custom-call | tf_op jit(solution)/shard_map/pool_step/pallas_call | solution.py:348
  23.0 2.1 %collective-permute-start.11 = (f16[17,16,128]{2,1,0:T(8,128)(2,1)S(1)}, f16[17,16,128]{2,1,0:T(8,128)(2,1)S(1)}, u32[]{:S(2)}, u32[]{:S(2)}) collective-permute-start(f16[17,16,128]{2,1,0:T(8,128)(2,1)S(1)} %get-tuple-element.47), channel_id=1, source_target_pairs={{0,12},{4,0},{8,4},{12,8},{1,13},{5,1},{9,5},{13,9},{2,14},{6,2},{... | collective-permute-start | bytes 208904 | tf_op jit(solution)/shard_map/ppermute | solution.py:477
  25.4 1.2 %next_logits.1 = f32[16,2048]{1,0:T(8,128)S(1)} custom-call(bf16[2048,1024]{1,0:T(8,128)(2,1)S(1)} %copy-done, f32[16,1024]{1,0:T(8,128)S(1)} %multiply_add_fusion.1.coef_ref, f32[16,2048]{1,0:T(8,128)S(1)} %get-tuple-element.37.term_ref), custom_call_target="tpu_custom_call" | custom-call | tf_op jit(solution)/shard_map/next_logits/pallas_call | solution.py:433
  26.6 0.6 %collective-permute-start.6 = (f16[16,2048]{1,0:T(8,128)(2,1)S(1)}, f16[16,2048]{1,0:T(8,128)(2,1)S(1)}, u32[]{:S(2)}, u32[]{:S(2)}) collective-permute-start(f16[16,2048]{1,0:T(8,128)(2,1)S(1)} %convert_element_type.101), channel_id=1, source_target_pairs={{0,2},{1,3},{2,0},{3,1},{4,6},{5,7},{6,4},{7,5},{8,10},{9,11},{10,... | collective-permute-start | bytes 196616 | tf_op jit(solution)/shard_map/ppermute | solution.py:458
  27.3 2.1 %collective-permute-done.10 = f16[17,16,128]{2,1,0:T(8,128)(2,1)S(1)} collective-permute-done((f16[17,16,128]{2,1,0:T(8,128)(2,1)S(1)}, f16[17,16,128]{2,1,0:T(8,128)(2,1)S(1)}, u32[]{:S(2)}, u32[]{:S(2)}) %collective-permute-start.10) | collective-permute-done | bytes 69664 | tf_op jit(solution)/shard_map/ppermute | solution.py:477
  29.3 1.9 %collective-permute-done.9 = f16[17,16,128]{2,1,0:T(8,128)(2,1)S(1)} collective-permute-done((f16[17,16,128]{2,1,0:T(8,128)(2,1)S(1)}, f16[17,16,128]{2,1,0:T(8,128)(2,1)S(1)}, u32[]{:S(2)}, u32[]{:S(2)}) %collective-permute-start.9) | collective-permute-done | bytes 69664 | tf_op jit(solution)/shard_map/ppermute | solution.py:477
  31.3 0.3 collective-permute-done.6
  31.7 0.6 %population_gradient.3 = f32[8,16,128]{2,1,0:T(8,128)S(1)} custom-call(bf16[16,2048]{1,0:T(8,128)(2,1)S(1)} %subtract_convert_fusion.resid_ref, bf16[2048,1024]{1,0:T(8,128)(2,1)S(1)} %copy-done), custom_call_target="tpu_custom_call" | custom-call | tf_op jit(solution)/shard_map/population_gradient/pallas_call | solution.py:226
  32.5 1.4 %collective-permute-start.12 = (f16[25,16,128]{2,1,0:T(8,128)(2,1)S(1)}, f16[25,16,128]{2,1,0:T(8,128)(2,1)S(1)}, u32[]{:S(2)}, u32[]{:S(2)}) collective-permute-start(f16[25,16,128]{2,1,0:T(8,128)(2,1)S(1)} %pad_maximum_fusion.1), channel_id=1, source_target_pairs={{0,4},{4,8},{8,12},{12,0},{1,5},{5,9},{9,13},{13,1},{2,6},{6,10},{... | collective-permute-start | bytes 307208 | tf_op jit(solution)/shard_map/ppermute | solution.py:484
  33.9 3.0 %collective-permute-start.13 = (f16[25,16,128]{2,1,0:T(8,128)(2,1)S(1)}, f16[25,16,128]{2,1,0:T(8,128)(2,1)S(1)}, u32[]{:S(2)}, u32[]{:S(2)}) collective-permute-start(f16[25,16,128]{2,1,0:T(8,128)(2,1)S(1)} %pad_maximum_fusion.1), channel_id=1, source_target_pairs={{0,8},{4,12},{8,0},{12,4},{1,9},{5,13},{9,1},{13,5},{2,10},{6,14},... | collective-permute-start | bytes 307208 | tf_op jit(solution)/shard_map/ppermute | solution.py:484
  36.9 1.3 %collective-permute-start.14 = (f16[25,16,128]{2,1,0:T(8,128)(2,1)S(1)}, f16[25,16,128]{2,1,0:T(8,128)(2,1)S(1)}, u32[]{:S(2)}, u32[]{:S(2)}) collective-permute-start(f16[25,16,128]{2,1,0:T(8,128)(2,1)S(1)} %pad_maximum_fusion.1), channel_id=1, source_target_pairs={{0,12},{4,0},{8,4},{12,8},{1,13},{5,1},{9,5},{13,9},{2,14},{6,2},{... | collective-permute-start | bytes 307208 | tf_op jit(solution)/shard_map/ppermute | solution.py:484
  38.3 1.5 %pool_likelihood.1.part_ref = f32[16,64,64]{2,1,0:T(8,128)S(1)} custom-call(bf16[16,2048]{1,0:T(8,128)(2,1)S(1)} %subtract_convert_fusion.resid_ref, bf16[64,2048]{1,0:T(8,128)(2,1)S(1)} %get-tuple-element.34.slope_ref, s32[1,2048]{1,0:T(1,128)S(1)} %bitcast.68, f32[16]{0:T(128)S(1)} %copy-done.8, f32[16,64,64]{2,1,0:T(8,128)S(1)} %get-tuple-element.42.half_ref, ...), custom_call_target="tpu_custom_call" | custom-call | tf_op jit(solution)/shard_map/pool_likelihood/pallas_call | solution.py:412
  39.8 0.2 collective-permute-done.12
  40.0 4.5 %collective-permute-done.13 = f16[25,16,128]{2,1,0:T(8,128)(2,1)S(1)} collective-permute-done((f16[25,16,128]{2,1,0:T(8,128)(2,1)S(1)}, f16[25,16,128]{2,1,0:T(8,128)(2,1)S(1)}, u32[]{:S(2)}, u32[]{:S(2)}) %collective-permute-start.13) | collective-permute-done | bytes 102432 | tf_op jit(solution)/shard_map/ppermute | solution.py:484
  44.6 0.7 %multiply_add_fusion = f32[16,1024]{1,0:T(8,128)} fusion(f32[16,1024]{1,0:T(8,128)S(1)} %multiply_add_fusion.1.coef_ref, f32[16,1024]{1,0:T(8,128)S(1)} %constant_dynamic-update-slice_fusion.8, f32[16]{0:T(128)S(1)} %broadcast_multiply_fusion, f32[16,1024]{1,0:T(8,128)S(1)} %copy-done.11, f32[16,1024]{1,0:T(8,128)S(1)} %copy-done.10, ...), kind=kLoop, calls=%fused_computation.9 | loop fusion | flops 163840 | bytes 393280 | tf_op jit(solution)/shard_map/add | solution.py:566
  45.5 2.7 %region_step.1 = (f32[16,64,64]{2,1,0:T(8,128)}, f32[16,64,64]{2,1,0:T(8,128)}, f32[16,64,64]{2,1,0:T(8,128)}) custom-call(s32[1,64]{1,0:T(1,128)S(1)} %bitcast.71, f32[16]{0:T(128)S(1)} %copy-done.8, f32[17,64,128]{2,1,0:T(8,128)S(1)} %convert_element_type.113.sums_ref, f32[16,64,64]{2,1,0:T(8,128)S(1)} %copy-done.2, f32[16,64,64]{2,1,0:T(8,128)S(1)} %copy-done.5, ...), custom_call_target="tpu_custom_call" | custom-call | tf_op jit(solution)/shard_map/region_step/pallas_call | solution.py:390
  (80 shorter events, 1.1 us)
Async XLA Ops:
  0.6 8.8 %copy-start.1 = (f32[16,64,64]{2,1,0:T(8,128)S(1)}, f32[16,64,64]{2,1,0:T(8,128)}, u32[]{:S(2)}) copy-start(f32[16,64,64]{2,1,0:T(8,128)} %base_ref.1) | copy-start | bytes 786436
  0.7 8.8 %copy-start.9 = (s32[64]{0:T(128)S(1)}, s32[64]{0:T(128)}, u32[]{:S(2)}) copy-start(s32[64]{0:T(128)} %param.14) | copy-start | bytes 772
  4.7 7.6 %collective-permute-start = (f16[16,2048]{1,0:T(8,128)(2,1)S(1)}, f16[16,2048]{1,0:T(8,128)(2,1)S(1)}, u32[]{:S(2)}, u32[]{:S(2)}) collective-permute-start(f16[16,2048]{1,0:T(8,128)(2,1)S(1)} %convert_element_type.90), channel_id=1, source_target_pairs={{0,2},{1,3},{2,0},{3,1},{4,6},{5,7},{6,4},{7,5},{8,10},{9,11},{10,... | collective-permute-start | bytes 196616 | tf_op jit(solution)/shard_map/ppermute | solution.py:458
  7.7 4.6 %collective-permute-start.1 = (f16[16,2048]{1,0:T(8,128)(2,1)S(1)}, f16[16,2048]{1,0:T(8,128)(2,1)S(1)}, u32[]{:S(2)}, u32[]{:S(2)}) collective-permute-start(f16[16,2048]{1,0:T(8,128)(2,1)S(1)} %convert_element_type.90), channel_id=1, source_target_pairs={{0,1},{1,2},{2,3},{3,0},{4,5},{5,6},{6,7},{7,4},{8,9},{9,10},{10,1... | collective-permute-start | bytes 196616 | tf_op jit(solution)/shard_map/ppermute | solution.py:458
  7.7 4.6 %collective-permute-start.2 = (f16[16,2048]{1,0:T(8,128)(2,1)S(1)}, f16[16,2048]{1,0:T(8,128)(2,1)S(1)}, u32[]{:S(2)}, u32[]{:S(2)}) collective-permute-start(f16[16,2048]{1,0:T(8,128)(2,1)S(1)} %convert_element_type.90), channel_id=1, source_target_pairs={{0,3},{1,0},{2,1},{3,2},{4,7},{5,4},{6,5},{7,6},{8,11},{9,8},{10,9... | collective-permute-start | bytes 196616 | tf_op jit(solution)/shard_map/ppermute | solution.py:458
  9.5 10.1 %copy-start.7 = (s32[2048]{0:T(1024)S(1)}, s32[2048]{0:T(1024)}, u32[]{:S(2)}) copy-start(s32[2048]{0:T(1024)} %param.13) | copy-start | bytes 24580
  12.3 13.0 %copy-start.10 = (f32[16,1024]{1,0:T(8,128)S(1)}, f32[16,1024]{1,0:T(8,128)}, u32[]{:S(2)}) copy-start(f32[16,1024]{1,0:T(8,128)} %beta_hbm.1) | copy-start | bytes 196612
  12.3 13.0 %copy-start.11 = (f32[16,1024]{1,0:T(8,128)S(1)}, f32[16,1024]{1,0:T(8,128)}, u32[]{:S(2)}) copy-start(f32[16,1024]{1,0:T(8,128)} %param.19) | copy-start | bytes 196612
  12.4 13.0 %copy-start = (bf16[2048,1024]{1,0:T(8,128)(2,1)S(1)}, bf16[2048,1024]{1,0:T(8,128)(2,1)}, u32[]{:S(2)}) copy-start(bf16[2048,1024]{1,0:T(8,128)(2,1)} %design_ref.3) | copy-start | bytes 12582916
  13.1 12.0 %collective-permute-start.3 = (f16[8,16,128]{2,1,0:T(8,128)(2,1)S(1)}, f16[8,16,128]{2,1,0:T(8,128)(2,1)S(1)}, u32[]{:S(2)}, u32[]{:S(2)}) collective-permute-start(f16[8,16,128]{2,1,0:T(8,128)(2,1)S(1)} %convert_element_type.96), channel_id=1, source_target_pairs={{0,8},{4,12},{8,0},{12,4},{1,9},{5,13},{9,1},{13,5},{2,10},{6,14},... | collective-permute-start | bytes 98312 | tf_op jit(solution)/shard_map/ppermute | solution.py:458
  15.8 9.4 %collective-permute-start.4 = (f16[8,16,128]{2,1,0:T(8,128)(2,1)S(1)}, f16[8,16,128]{2,1,0:T(8,128)(2,1)S(1)}, u32[]{:S(2)}, u32[]{:S(2)}) collective-permute-start(f16[8,16,128]{2,1,0:T(8,128)(2,1)S(1)} %convert_element_type.96), channel_id=1, source_target_pairs={{0,4},{4,8},{8,12},{12,0},{1,5},{5,9},{9,13},{13,1},{2,6},{6,10},{... | collective-permute-start | bytes 98312 | tf_op jit(solution)/shard_map/ppermute | solution.py:458
  17.3 7.8 %collective-permute-start.5 = (f16[8,16,128]{2,1,0:T(8,128)(2,1)S(1)}, f16[8,16,128]{2,1,0:T(8,128)(2,1)S(1)}, u32[]{:S(2)}, u32[]{:S(2)}) collective-permute-start(f16[8,16,128]{2,1,0:T(8,128)(2,1)S(1)} %convert_element_type.96), channel_id=1, source_target_pairs={{0,12},{4,0},{8,4},{12,8},{1,13},{5,1},{9,5},{13,9},{2,14},{6,2},{... | collective-permute-start | bytes 98312 | tf_op jit(solution)/shard_map/ppermute | solution.py:458
  22.9 6.4 %collective-permute-start.10 = (f16[17,16,128]{2,1,0:T(8,128)(2,1)S(1)}, f16[17,16,128]{2,1,0:T(8,128)(2,1)S(1)}, u32[]{:S(2)}, u32[]{:S(2)}) collective-permute-start(f16[17,16,128]{2,1,0:T(8,128)(2,1)S(1)} %get-tuple-element.48), channel_id=1, source_target_pairs={{0,8},{4,12},{8,0},{12,4},{1,9},{5,13},{9,1},{13,5},{2,10},{6,14},... | collective-permute-start | bytes 208904 | tf_op jit(solution)/shard_map/ppermute | solution.py:477
  23.0 6.3 %collective-permute-start.11 = (f16[17,16,128]{2,1,0:T(8,128)(2,1)S(1)}, f16[17,16,128]{2,1,0:T(8,128)(2,1)S(1)}, u32[]{:S(2)}, u32[]{:S(2)}) collective-permute-start(f16[17,16,128]{2,1,0:T(8,128)(2,1)S(1)} %get-tuple-element.47), channel_id=1, source_target_pairs={{0,12},{4,0},{8,4},{12,8},{1,13},{5,1},{9,5},{13,9},{2,14},{6,2},{... | collective-permute-start | bytes 208904 | tf_op jit(solution)/shard_map/ppermute | solution.py:477
  25.1 6.1 %collective-permute-start.9 = (f16[17,16,128]{2,1,0:T(8,128)(2,1)S(1)}, f16[17,16,128]{2,1,0:T(8,128)(2,1)S(1)}, u32[]{:S(2)}, u32[]{:S(2)}) collective-permute-start(f16[17,16,128]{2,1,0:T(8,128)(2,1)S(1)} %get-tuple-element.46), channel_id=1, source_target_pairs={{0,4},{4,8},{8,12},{12,0},{1,5},{5,9},{9,13},{13,1},{2,6},{6,10},{... | collective-permute-start | bytes 208904 | tf_op jit(solution)/shard_map/ppermute | solution.py:477
  25.4 19.2 %copy-start.3 = (f32[16,1024]{1,0:T(8,128)}, f32[16,1024]{1,0:T(8,128)S(1)}, u32[]{:S(2)}) copy-start(f32[16,1024]{1,0:T(8,128)S(1)} %multiply_add_fusion.1.coef_ref) | copy-start | bytes 196612
  25.4 12.9 %copy-start.6 = (f32[16,64,64]{2,1,0:T(8,128)S(1)}, f32[16,64,64]{2,1,0:T(8,128)}, u32[]{:S(2)}) copy-start(f32[16,64,64]{2,1,0:T(8,128)} %get-tuple-element.21.u_ref) | copy-start | bytes 786436
  26.6 5.0 %collective-permute-start.6 = (f16[16,2048]{1,0:T(8,128)(2,1)S(1)}, f16[16,2048]{1,0:T(8,128)(2,1)S(1)}, u32[]{:S(2)}, u32[]{:S(2)}) collective-permute-start(f16[16,2048]{1,0:T(8,128)(2,1)S(1)} %convert_element_type.101), channel_id=1, source_target_pairs={{0,2},{1,3},{2,0},{3,1},{4,6},{5,7},{6,4},{7,5},{8,10},{9,11},{10,... | collective-permute-start | bytes 196616 | tf_op jit(solution)/shard_map/ppermute | solution.py:458
  27.3 4.4 %collective-permute-start.7 = (f16[16,2048]{1,0:T(8,128)(2,1)S(1)}, f16[16,2048]{1,0:T(8,128)(2,1)S(1)}, u32[]{:S(2)}, u32[]{:S(2)}) collective-permute-start(f16[16,2048]{1,0:T(8,128)(2,1)S(1)} %convert_element_type.101), channel_id=1, source_target_pairs={{0,1},{1,2},{2,3},{3,0},{4,5},{5,6},{6,7},{7,4},{8,9},{9,10},{10,1... | collective-permute-start | bytes 196616 | tf_op jit(solution)/shard_map/ppermute | solution.py:458
  29.3 2.3 %collective-permute-start.8 = (f16[16,2048]{1,0:T(8,128)(2,1)S(1)}, f16[16,2048]{1,0:T(8,128)(2,1)S(1)}, u32[]{:S(2)}, u32[]{:S(2)}) collective-permute-start(f16[16,2048]{1,0:T(8,128)(2,1)S(1)} %convert_element_type.101), channel_id=1, source_target_pairs={{0,3},{1,0},{2,1},{3,2},{4,7},{5,4},{6,5},{7,6},{8,11},{9,8},{10,9... | collective-permute-start | bytes 196616 | tf_op jit(solution)/shard_map/ppermute | solution.py:458
  31.7 13.7 %copy-start.5 = (f32[16,64,64]{2,1,0:T(8,128)S(1)}, f32[16,64,64]{2,1,0:T(8,128)}, u32[]{:S(2)}) copy-start(f32[16,64,64]{2,1,0:T(8,128)} %m_ref.1) | copy-start | bytes 786436
  32.5 7.5 %collective-permute-start.12 = (f16[25,16,128]{2,1,0:T(8,128)(2,1)S(1)}, f16[25,16,128]{2,1,0:T(8,128)(2,1)S(1)}, u32[]{:S(2)}, u32[]{:S(2)}) collective-permute-start(f16[25,16,128]{2,1,0:T(8,128)(2,1)S(1)} %pad_maximum_fusion.1), channel_id=1, source_target_pairs={{0,4},{4,8},{8,12},{12,0},{1,5},{5,9},{9,13},{13,1},{2,6},{6,10},{... | collective-permute-start | bytes 307208 | tf_op jit(solution)/shard_map/ppermute | solution.py:484
  33.9 10.6 %collective-permute-start.13 = (f16[25,16,128]{2,1,0:T(8,128)(2,1)S(1)}, f16[25,16,128]{2,1,0:T(8,128)(2,1)S(1)}, u32[]{:S(2)}, u32[]{:S(2)}) collective-permute-start(f16[25,16,128]{2,1,0:T(8,128)(2,1)S(1)} %pad_maximum_fusion.1), channel_id=1, source_target_pairs={{0,8},{4,12},{8,0},{12,4},{1,9},{5,13},{9,1},{13,5},{2,10},{6,14},... | collective-permute-start | bytes 307208 | tf_op jit(solution)/shard_map/ppermute | solution.py:484
  36.9 7.6 %collective-permute-start.14 = (f16[25,16,128]{2,1,0:T(8,128)(2,1)S(1)}, f16[25,16,128]{2,1,0:T(8,128)(2,1)S(1)}, u32[]{:S(2)}, u32[]{:S(2)}) collective-permute-start(f16[25,16,128]{2,1,0:T(8,128)(2,1)S(1)} %pad_maximum_fusion.1), channel_id=1, source_target_pairs={{0,12},{4,0},{8,4},{12,8},{1,13},{5,1},{9,5},{13,9},{2,14},{6,2},{... | collective-permute-start | bytes 307208 | tf_op jit(solution)/shard_map/ppermute | solution.py:484
  (4 other events, 35.2 us)

commit v5 on v4

--- a/solution.py
+++ b/solution.py
@@ -364,12 +364,25 @@
     )(resid, slope, ids, index, step, base, mom_base)
 
 
-def region_step(index, step, sums, regions, momentum, pool_part):
+def finish(index, step, sums, regions, momentum, pool_part, gb, beta_next, beta_half, total_feats):
     chains, owned, slopes = pool_part.shape
     n_regions = regions.shape[1]
     pairs = chains // 2
-
-    def kernel(index_ref, step_ref, sums_ref, v_ref, m_ref, part_ref, next_ref, mom_ref, pool_ref):
+    planes, _, lanes = gb.shape
+
+    def kernel(index_ref, step_ref, column_ref, sums_ref, v_ref, m_ref, part_ref, gb_ref, b_ref, bh_ref, *rest):
+        outs, (beta_ref, next_ref, mom_ref, pool_ref, sems) = rest[:4], rest[4:]
+        copies = [
+            pltpu.make_async_copy(made, out, sems.at[k])
+            for k, (made, out) in enumerate(zip((beta_ref, next_ref, mom_ref, pool_ref), outs))
+        ]
+        h = 0.5 * column_ref[...]
+        for k in range(planes):
+            cols = slice(k * lanes, (k + 1) * lanes)
+            grad = (1.0 / SCALE) * gb_ref[k] - total_feats * b_ref[:, cols]
+            beta_ref[:, cols] = bh_ref[:, cols] + h * grad
+        copies[0].start()
+
         def part(k, c):
             side = slice((c // pairs) * slopes, (c // pairs + 1) * slopes)
             return (1.0 / SCALE) * sums_ref[k + c % pairs][:, side]
@@ -383,22 +396,25 @@
             next_ref[c] = ahead
             gain = dev + PREC * (part(pairs + 1, c) - count * (ahead - v)) - PREC * ahead
             mom_ref[c] = half + h * gain
+        copies[1].start()
+        copies[2].start()
         chosen = chosen_regions(region_onehot(index_ref, n_regions), next_ref[...])
         for c in range(chains):
             pool_ref[c] = part_ref[c] + (0.5 * step_ref[c]) * (PREC * chosen[c])
-
+        copies[3].start()
+        for copy in copies:
+            copy.wait()
+
+    made = [beta_next.shape, regions.shape, regions.shape, pool_part.shape]
     return pl.pallas_call(
         kernel,
-        in_specs=[whole(), smem()] + [whole()] * 4,
-        out_specs=[whole()] * 3,
-        out_shape=[
-            jax.ShapeDtypeStruct(regions.shape, F32),
-            jax.ShapeDtypeStruct(regions.shape, F32),
-            jax.ShapeDtypeStruct(pool_part.shape, F32),
-        ],
+        in_specs=[whole(), smem()] + [whole()] * 8,
+        out_specs=[pl.BlockSpec(memory_space=pl.ANY)] * 4,
+        out_shape=[pltpu.HBM(shape, F32) for shape in made],
+        scratch_shapes=[pltpu.VMEM(shape, F32) for shape in made] + [pltpu.SemaphoreType.DMA((4,))],
         compiler_params=params(),
-        name="region_step",
-    )(index, step, sums, regions, momentum, pool_part)
+        name="finish",
+    )(index, step, step[:, None], sums, regions, momentum, pool_part, gb, beta_next, beta_half)
 
 
 def pool_likelihood(resid, slope, ids, step, half, pools_next):
@@ -559,11 +575,9 @@
     resid, gb = lax.optimization_barrier((resid, gb))
     pool_part = pool_likelihood(resid, slope, ids, step_size, pool_half, pools_next)
     gb, sums = total_and_blocks(gb, mine, "loan")
-    regions_next, region_out, pool_out = region_step(
-        index, step_size, sums, regions, region_momentum, pool_part
+    beta_out, regions_next, region_out, pool_out = finish(
+        index, step_size, sums, regions, region_momentum, pool_part, gb, beta_next, beta_half, total_feats
     )
-    gb = flat(gb) * (1.0 / SCALE) - total_feats * beta_next
-    beta_out = beta_half + half[:, None] * gb
     return (beta_next, pools_next, regions_next, beta_out, pool_out, region_out)
 
 

time: 48.3 us -> 47.4 us (0.981)
  other arithmetic: 1.32 us -> 0.62 us
    add x1 -> x0, other arithmetic: 0.71 us -> none  [body(): beta_out = beta_half + half[:, None] * gb]
where the time goes in v5:
time: 47.4 us; the launch traced here: 47.3 us
  starting transfers between devices  19.8 us (42%)
  Pallas kernels  16.4 us (35%)
  waiting for transfers between devices  8.97 us (19%)
  between operations  1.06 us (2%)
  other arithmetic  0.62 us (1%)
    ppermute x9, starting transfers between devices, total_over(): lax.ppermute(own, axis, ahead_by(k, size, stride, group))  11.8 us
    ppermute x3, starting transfers between devices, all_shifts(): lax.ppermute(x, axis, ahead_by(k, size, 1, size))  5.77 us
    ppermute x3, waiting for transfers between devices, all_shifts(): lax.ppermute(x, axis, ahead_by(k, size, 1, size))  4.62 us
    ppermute x3, waiting for transfers between devices, own_block(): lax.ppermute(block(k), axis, ahead_by(k, size, 1, size)).astype(F32)  4 us
    pallas_call x1, Pallas kernels, first_logits(): pl.pallas_call(kernel, in_specs=[pl.BlockSpec(memory_space=pl.ANY)] * 4,...  3.96 us
    pallas_call x1, Pallas kernels, pool_step(): pl.pallas_call(kernel, in_specs=[whole()] * 4 + [smem()] + [whole()] * 2,...  3.14 us
    pallas_call x1, Pallas kernels, prior(): pl.pallas_call(kernel, in_specs=[whole(), smem(), whole(), whole(), whole...  2.75 us
    pallas_call x1, Pallas kernels, finish(): pl.pallas_call(kernel, in_specs=[whole(), smem()] + [whole()] * 8, out_sp...  2.62 us
  transfers between devices with their start and end apart: 15, of which 5 were waited for; matrix products, arithmetic and copies ran while one was open for 1% of the time, Pallas kernels for 18%

profile of v5, /device:TPU:0, one launch (start us, length us, event | category | flops | bytes accessed | tf_op | source)
XLA Modules:
  0.0 47.3 jit_solution(7252817662795606406)
XLA Ops:
  0.7 4.0 %first_logits.1 = (bf16[64,2048]{1,0:T(8,128)(2,1)S(1)}, f32[16,2048]{1,0:T(8,128)S(1)}) custom-call(bf16[2048,1024]{1,0:T(8,128)(2,1)} %design_ref.3, s32[1,2048]{1,0:T(1,128)} %bitcast.35, f32[16,1024]{1,0:T(8,128)} %beta_hbm.1, f32[16,64,64]{2,1,0:T(8,128)} %base_ref.1), custom_call_target="tpu_custom_call" | custom-call | tf_op jit(solution)/shard_map/first_logits/pallas_call | solution.py:192
  4.7 3.0 %collective-permute-start = (f16[16,2048]{1,0:T(8,128)(2,1)S(1)}, f16[16,2048]{1,0:T(8,128)(2,1)S(1)}, u32[]{:S(2)}, u32[]{:S(2)}) collective-permute-start(f16[16,2048]{1,0:T(8,128)(2,1)S(1)} %convert_element_type.90), channel_id=1, source_target_pairs={{0,2},{1,3},{2,0},{3,1},{4,6},{5,7},{6,4},{7,5},{8,10},{9,11},{10,... | collective-permute-start | bytes 196616 | tf_op jit(solution)/shard_map/ppermute | solution.py:474
  7.7 1.7 %collective-permute-start.2 = (f16[16,2048]{1,0:T(8,128)(2,1)S(1)}, f16[16,2048]{1,0:T(8,128)(2,1)S(1)}, u32[]{:S(2)}, u32[]{:S(2)}) collective-permute-start(f16[16,2048]{1,0:T(8,128)(2,1)S(1)} %convert_element_type.90), channel_id=1, source_target_pairs={{0,3},{1,0},{2,1},{3,2},{4,7},{5,4},{6,5},{7,6},{8,11},{9,8},{10,9... | collective-permute-start | bytes 196616 | tf_op jit(solution)/shard_map/ppermute | solution.py:474
  9.6 2.7 %prior.1 = (f32[16,64,64]{2,1,0:T(8,128)S(1)}, f32[9,64,128]{2,1,0:T(8,128)S(1)}, bf16[2048,1024]{1,0:T(8,128)(2,1)S(1)}) custom-call(s32[1,64]{1,0:T(1,128)S(1)} %bitcast.39, f32[16]{0:T(128)S(1)} %copy-done.8, f32[16,64,64]{2,1,0:T(8,128)S(1)} %copy-done.1, f32[16,64,64]{2,1,0:T(8,128)S(1)} %copy-done.2, f32[16,64,64]{2,1,0:T(8,128)S(1)} %copy-done.4, ...), custom_call_target="tpu_custom_call" | custom-call | tf_op jit(solution)/shard_map/prior/pallas_call | solution.py:311
  12.5 0.6 %population_gradient.2 = f32[8,16,128]{2,1,0:T(8,128)S(1)} custom-call(bf16[16,2048]{1,0:T(8,128)(2,1)S(1)} %subtract_convert_fusion.1.resid_ref, bf16[2048,1024]{1,0:T(8,128)(2,1)S(1)} %get-tuple-element.30.design_ref), custom_call_target="tpu_custom_call" | custom-call | tf_op jit(solution)/shard_map/population_gradient/pallas_call | solution.py:226
  13.1 2.7 %collective-permute-start.3 = (f16[8,16,128]{2,1,0:T(8,128)(2,1)S(1)}, f16[8,16,128]{2,1,0:T(8,128)(2,1)S(1)}, u32[]{:S(2)}, u32[]{:S(2)}) collective-permute-start(f16[8,16,128]{2,1,0:T(8,128)(2,1)S(1)} %convert_element_type.96), channel_id=1, source_target_pairs={{0,8},{4,12},{8,0},{12,4},{1,9},{5,13},{9,1},{13,5},{2,10},{6,14},... | collective-permute-start | bytes 98312 | tf_op jit(solution)/shard_map/ppermute | solution.py:474
  15.8 1.6 %collective-permute-start.4 = (f16[8,16,128]{2,1,0:T(8,128)(2,1)S(1)}, f16[8,16,128]{2,1,0:T(8,128)(2,1)S(1)}, u32[]{:S(2)}, u32[]{:S(2)}) collective-permute-start(f16[8,16,128]{2,1,0:T(8,128)(2,1)S(1)} %convert_element_type.96), channel_id=1, source_target_pairs={{0,4},{4,8},{8,12},{12,0},{1,5},{5,9},{9,13},{13,1},{2,6},{6,10},{... | collective-permute-start | bytes 98312 | tf_op jit(solution)/shard_map/ppermute | solution.py:474
  17.4 2.2 %collective-permute-start.5 = (f16[8,16,128]{2,1,0:T(8,128)(2,1)S(1)}, f16[8,16,128]{2,1,0:T(8,128)(2,1)S(1)}, u32[]{:S(2)}, u32[]{:S(2)}) collective-permute-start(f16[8,16,128]{2,1,0:T(8,128)(2,1)S(1)} %convert_element_type.96), channel_id=1, source_target_pairs={{0,12},{4,0},{8,4},{12,8},{1,13},{5,1},{9,5},{13,9},{2,14},{6,2},{... | collective-permute-start | bytes 98312 | tf_op jit(solution)/shard_map/ppermute | solution.py:474
  19.6 3.1 %pool_step.1 = (f32[16,64,64]{2,1,0:T(8,128)}, f32[16,64,64]{2,1,0:T(8,128)S(1)}, f32[16,2048]{1,0:T(8,128)S(1)}, f32[8,64,128]{2,1,0:T(8,128)S(1)}) custom-call(bf16[16,2048]{1,0:T(8,128)(2,1)S(1)} %subtract_convert_fusion.1.resid_ref, bf16[64,2048]{1,0:T(8,128)(2,1)S(1)} %get-tuple-element.35.slope_ref, s32[1,2048]{1,0:T(1,128)S(1)} %bitcast.36, ...), custom_call_target="tpu_custom_call" | custom-call | tf_op jit(solution)/shard_map/pool_step/pallas_call | solution.py:348
  23.1 2.1 %collective-permute-start.11 = (f16[17,16,128]{2,1,0:T(8,128)(2,1)S(1)}, f16[17,16,128]{2,1,0:T(8,128)(2,1)S(1)}, u32[]{:S(2)}, u32[]{:S(2)}) collective-permute-start(f16[17,16,128]{2,1,0:T(8,128)(2,1)S(1)} %get-tuple-element.51), channel_id=1, source_target_pairs={{0,12},{4,0},{8,4},{12,8},{1,13},{5,1},{9,5},{13,9},{2,14},{6,2},{... | collective-permute-start | bytes 208904 | tf_op jit(solution)/shard_map/ppermute | solution.py:493
  25.4 0.1 multiply_add_fusion
  25.5 1.2 %next_logits.1 = f32[16,2048]{1,0:T(8,128)S(1)} custom-call(bf16[2048,1024]{1,0:T(8,128)(2,1)S(1)} %copy-done, f32[16,1024]{1,0:T(8,128)S(1)} %get-tuple-element.48.coef_ref.b_ref, f32[16,2048]{1,0:T(8,128)S(1)} %get-tuple-element.38.term_ref), custom_call_target="tpu_custom_call" | custom-call | tf_op jit(solution)/shard_map/next_logits/pallas_call | solution.py:449
  26.7 0.6 %collective-permute-start.6 = (f16[16,2048]{1,0:T(8,128)(2,1)S(1)}, f16[16,2048]{1,0:T(8,128)(2,1)S(1)}, u32[]{:S(2)}, u32[]{:S(2)}) collective-permute-start(f16[16,2048]{1,0:T(8,128)(2,1)S(1)} %convert_element_type.101), channel_id=1, source_target_pairs={{0,2},{1,3},{2,0},{3,1},{4,6},{5,7},{6,4},{7,5},{8,10},{9,11},{10,... | collective-permute-start | bytes 196616 | tf_op jit(solution)/shard_map/ppermute | solution.py:474
  27.3 2.1 %collective-permute-done.10 = f16[17,16,128]{2,1,0:T(8,128)(2,1)S(1)} collective-permute-done((f16[17,16,128]{2,1,0:T(8,128)(2,1)S(1)}, f16[17,16,128]{2,1,0:T(8,128)(2,1)S(1)}, u32[]{:S(2)}, u32[]{:S(2)}) %collective-permute-start.10) | collective-permute-done | bytes 69664 | tf_op jit(solution)/shard_map/ppermute | solution.py:493
  29.4 1.9 %collective-permute-done.9 = f16[17,16,128]{2,1,0:T(8,128)(2,1)S(1)} collective-permute-done((f16[17,16,128]{2,1,0:T(8,128)(2,1)S(1)}, f16[17,16,128]{2,1,0:T(8,128)(2,1)S(1)}, u32[]{:S(2)}, u32[]{:S(2)}) %collective-permute-start.9) | collective-permute-done | bytes 69664 | tf_op jit(solution)/shard_map/ppermute | solution.py:493
  31.4 0.3 collective-permute-done.6
  31.8 0.6 %population_gradient.3 = f32[8,16,128]{2,1,0:T(8,128)S(1)} custom-call(bf16[16,2048]{1,0:T(8,128)(2,1)S(1)} %subtract_convert_fusion.resid_ref, bf16[2048,1024]{1,0:T(8,128)(2,1)S(1)} %copy-done), custom_call_target="tpu_custom_call" | custom-call | tf_op jit(solution)/shard_map/population_gradient/pallas_call | solution.py:226
  32.5 1.4 %collective-permute-start.12 = (f16[25,16,128]{2,1,0:T(8,128)(2,1)S(1)}, f16[25,16,128]{2,1,0:T(8,128)(2,1)S(1)}, u32[]{:S(2)}, u32[]{:S(2)}) collective-permute-start(f16[25,16,128]{2,1,0:T(8,128)(2,1)S(1)} %pad_maximum_fusion.1), channel_id=1, source_target_pairs={{0,4},{4,8},{8,12},{12,0},{1,5},{5,9},{9,13},{13,1},{2,6},{6,10},{... | collective-permute-start | bytes 307208 | tf_op jit(solution)/shard_map/ppermute | solution.py:500
  33.9 3.0 %collective-permute-start.13 = (f16[25,16,128]{2,1,0:T(8,128)(2,1)S(1)}, f16[25,16,128]{2,1,0:T(8,128)(2,1)S(1)}, u32[]{:S(2)}, u32[]{:S(2)}) collective-permute-start(f16[25,16,128]{2,1,0:T(8,128)(2,1)S(1)} %pad_maximum_fusion.1), channel_id=1, source_target_pairs={{0,8},{4,12},{8,0},{12,4},{1,9},{5,13},{9,1},{13,5},{2,10},{6,14},... | collective-permute-start | bytes 307208 | tf_op jit(solution)/shard_map/ppermute | solution.py:500
  36.9 1.3 %collective-permute-start.14 = (f16[25,16,128]{2,1,0:T(8,128)(2,1)S(1)}, f16[25,16,128]{2,1,0:T(8,128)(2,1)S(1)}, u32[]{:S(2)}, u32[]{:S(2)}) collective-permute-start(f16[25,16,128]{2,1,0:T(8,128)(2,1)S(1)} %pad_maximum_fusion.1), channel_id=1, source_target_pairs={{0,12},{4,0},{8,4},{12,8},{1,13},{5,1},{9,5},{13,9},{2,14},{6,2},{... | collective-permute-start | bytes 307208 | tf_op jit(solution)/shard_map/ppermute | solution.py:500
  38.4 1.5 %pool_likelihood.1.part_ref = f32[16,64,64]{2,1,0:T(8,128)S(1)} custom-call(bf16[16,2048]{1,0:T(8,128)(2,1)S(1)} %subtract_convert_fusion.resid_ref, bf16[64,2048]{1,0:T(8,128)(2,1)S(1)} %get-tuple-element.35.slope_ref, s32[1,2048]{1,0:T(1,128)S(1)} %bitcast.37, f32[16]{0:T(128)S(1)} %copy-done.8, f32[16,64,64]{2,1,0:T(8,128)S(1)} %get-tuple-element.43.half_ref, ...), custom_call_target="tpu_custom_call" | custom-call | tf_op jit(solution)/shard_map/pool_likelihood/pallas_call | solution.py:428
  39.9 0.2 collective-permute-done.12
  40.1 4.4 %collective-permute-done.13 = f16[25,16,128]{2,1,0:T(8,128)(2,1)S(1)} collective-permute-done((f16[25,16,128]{2,1,0:T(8,128)(2,1)S(1)}, f16[25,16,128]{2,1,0:T(8,128)(2,1)S(1)}, u32[]{:S(2)}, u32[]{:S(2)}) %collective-permute-start.13) | collective-permute-done | bytes 102432 | tf_op jit(solution)/shard_map/ppermute | solution.py:500
  44.7 2.6 %finish.1 = (f32[16,1024]{1,0:T(8,128)}, f32[16,64,64]{2,1,0:T(8,128)}, f32[16,64,64]{2,1,0:T(8,128)}, f32[16,64,64]{2,1,0:T(8,128)}) custom-call(s32[1,64]{1,0:T(1,128)S(1)} %bitcast.41, f32[16]{0:T(128)S(1)} %copy-done.8, f32[16,1]{1,0:T(8,128)S(1)} %copy.17.column_ref, f32[17,64,128]{2,1,0:T(8,128)S(1)} %convert_element_type.113.sums_ref, ...), custom_call_target="tpu_custom_call" | custom-call | tf_op jit(solution)/shard_map/finish/pallas_call | solution.py:409
  (72 shorter events, 1.1 us)
Async XLA Ops:
  0.6 8.9 %copy-start.1 = (f32[16,64,64]{2,1,0:T(8,128)S(1)}, f32[16,64,64]{2,1,0:T(8,128)}, u32[]{:S(2)}) copy-start(f32[16,64,64]{2,1,0:T(8,128)} %base_ref.1) | copy-start | bytes 786436
  0.7 8.9 %copy-start.9 = (s32[64]{0:T(128)S(1)}, s32[64]{0:T(128)}, u32[]{:S(2)}) copy-start(s32[64]{0:T(128)} %param.14) | copy-start | bytes 772
  4.7 7.7 %collective-permute-start = (f16[16,2048]{1,0:T(8,128)(2,1)S(1)}, f16[16,2048]{1,0:T(8,128)(2,1)S(1)}, u32[]{:S(2)}, u32[]{:S(2)}) collective-permute-start(f16[16,2048]{1,0:T(8,128)(2,1)S(1)} %convert_element_type.90), channel_id=1, source_target_pairs={{0,2},{1,3},{2,0},{3,1},{4,6},{5,7},{6,4},{7,5},{8,10},{9,11},{10,... | collective-permute-start | bytes 196616 | tf_op jit(solution)/shard_map/ppermute | solution.py:474
  7.7 4.7 %collective-permute-start.1 = (f16[16,2048]{1,0:T(8,128)(2,1)S(1)}, f16[16,2048]{1,0:T(8,128)(2,1)S(1)}, u32[]{:S(2)}, u32[]{:S(2)}) collective-permute-start(f16[16,2048]{1,0:T(8,128)(2,1)S(1)} %convert_element_type.90), channel_id=1, source_target_pairs={{0,1},{1,2},{2,3},{3,0},{4,5},{5,6},{6,7},{7,4},{8,9},{9,10},{10,1... | collective-permute-start | bytes 196616 | tf_op jit(solution)/shard_map/ppermute | solution.py:474
  7.7 4.7 %collective-permute-start.2 = (f16[16,2048]{1,0:T(8,128)(2,1)S(1)}, f16[16,2048]{1,0:T(8,128)(2,1)S(1)}, u32[]{:S(2)}, u32[]{:S(2)}) collective-permute-start(f16[16,2048]{1,0:T(8,128)(2,1)S(1)} %convert_element_type.90), channel_id=1, source_target_pairs={{0,3},{1,0},{2,1},{3,2},{4,7},{5,4},{6,5},{7,6},{8,11},{9,8},{10,9... | collective-permute-start | bytes 196616 | tf_op jit(solution)/shard_map/ppermute | solution.py:474
  9.6 10.1 %copy-start.7 = (s32[2048]{0:T(1024)S(1)}, s32[2048]{0:T(1024)}, u32[]{:S(2)}) copy-start(s32[2048]{0:T(1024)} %param.13) | copy-start | bytes 24580
  12.3 13.0 %copy-start.10 = (f32[16,1024]{1,0:T(8,128)S(1)}, f32[16,1024]{1,0:T(8,128)}, u32[]{:S(2)}) copy-start(f32[16,1024]{1,0:T(8,128)} %beta_hbm.1) | copy-start | bytes 196612
  12.3 13.0 %copy-start.11 = (f32[16,1024]{1,0:T(8,128)S(1)}, f32[16,1024]{1,0:T(8,128)}, u32[]{:S(2)}) copy-start(f32[16,1024]{1,0:T(8,128)} %param.19) | copy-start | bytes 196612
  12.5 13.0 %copy-start = (bf16[2048,1024]{1,0:T(8,128)(2,1)S(1)}, bf16[2048,1024]{1,0:T(8,128)(2,1)}, u32[]{:S(2)}) copy-start(bf16[2048,1024]{1,0:T(8,128)(2,1)} %design_ref.3) | copy-start | bytes 12582916
  13.1 12.1 %collective-permute-start.3 = (f16[8,16,128]{2,1,0:T(8,128)(2,1)S(1)}, f16[8,16,128]{2,1,0:T(8,128)(2,1)S(1)}, u32[]{:S(2)}, u32[]{:S(2)}) collective-permute-start(f16[8,16,128]{2,1,0:T(8,128)(2,1)S(1)} %convert_element_type.96), channel_id=1, source_target_pairs={{0,8},{4,12},{8,0},{12,4},{1,9},{5,13},{9,1},{13,5},{2,10},{6,14},... | collective-permute-start | bytes 98312 | tf_op jit(solution)/shard_map/ppermute | solution.py:474
  15.8 9.4 %collective-permute-start.4 = (f16[8,16,128]{2,1,0:T(8,128)(2,1)S(1)}, f16[8,16,128]{2,1,0:T(8,128)(2,1)S(1)}, u32[]{:S(2)}, u32[]{:S(2)}) collective-permute-start(f16[8,16,128]{2,1,0:T(8,128)(2,1)S(1)} %convert_element_type.96), channel_id=1, source_target_pairs={{0,4},{4,8},{8,12},{12,0},{1,5},{5,9},{9,13},{13,1},{2,6},{6,10},{... | collective-permute-start | bytes 98312 | tf_op jit(solution)/shard_map/ppermute | solution.py:474
  17.4 7.8 %collective-permute-start.5 = (f16[8,16,128]{2,1,0:T(8,128)(2,1)S(1)}, f16[8,16,128]{2,1,0:T(8,128)(2,1)S(1)}, u32[]{:S(2)}, u32[]{:S(2)}) collective-permute-start(f16[8,16,128]{2,1,0:T(8,128)(2,1)S(1)} %convert_element_type.96), channel_id=1, source_target_pairs={{0,12},{4,0},{8,4},{12,8},{1,13},{5,1},{9,5},{13,9},{2,14},{6,2},{... | collective-permute-start | bytes 98312 | tf_op jit(solution)/shard_map/ppermute | solution.py:474
  23.0 6.4 %collective-permute-start.10 = (f16[17,16,128]{2,1,0:T(8,128)(2,1)S(1)}, f16[17,16,128]{2,1,0:T(8,128)(2,1)S(1)}, u32[]{:S(2)}, u32[]{:S(2)}) collective-permute-start(f16[17,16,128]{2,1,0:T(8,128)(2,1)S(1)} %get-tuple-element.52), channel_id=1, source_target_pairs={{0,8},{4,12},{8,0},{12,4},{1,9},{5,13},{9,1},{13,5},{2,10},{6,14},... | collective-permute-start | bytes 208904 | tf_op jit(solution)/shard_map/ppermute | solution.py:493
  23.1 6.3 %collective-permute-start.11 = (f16[17,16,128]{2,1,0:T(8,128)(2,1)S(1)}, f16[17,16,128]{2,1,0:T(8,128)(2,1)S(1)}, u32[]{:S(2)}, u32[]{:S(2)}) collective-permute-start(f16[17,16,128]{2,1,0:T(8,128)(2,1)S(1)} %get-tuple-element.51), channel_id=1, source_target_pairs={{0,12},{4,0},{8,4},{12,8},{1,13},{5,1},{9,5},{13,9},{2,14},{6,2},{... | collective-permute-start | bytes 208904 | tf_op jit(solution)/shard_map/ppermute | solution.py:493
  25.2 6.1 %collective-permute-start.9 = (f16[17,16,128]{2,1,0:T(8,128)(2,1)S(1)}, f16[17,16,128]{2,1,0:T(8,128)(2,1)S(1)}, u32[]{:S(2)}, u32[]{:S(2)}) collective-permute-start(f16[17,16,128]{2,1,0:T(8,128)(2,1)S(1)} %get-tuple-element.50), channel_id=1, source_target_pairs={{0,4},{4,8},{8,12},{12,0},{1,5},{5,9},{9,13},{13,1},{2,6},{6,10},{... | collective-permute-start | bytes 208904 | tf_op jit(solution)/shard_map/ppermute | solution.py:493
  25.4 19.2 %copy-start.3 = (f32[16,1024]{1,0:T(8,128)}, f32[16,1024]{1,0:T(8,128)S(1)}, u32[]{:S(2)}) copy-start(f32[16,1024]{1,0:T(8,128)S(1)} %get-tuple-element.48.coef_ref.b_ref) | copy-start | bytes 196612
  25.5 12.9 %copy-start.6 = (f32[16,64,64]{2,1,0:T(8,128)S(1)}, f32[16,64,64]{2,1,0:T(8,128)}, u32[]{:S(2)}) copy-start(f32[16,64,64]{2,1,0:T(8,128)} %get-tuple-element.22.u_ref) | copy-start | bytes 786436
  26.7 5.0 %collective-permute-start.6 = (f16[16,2048]{1,0:T(8,128)(2,1)S(1)}, f16[16,2048]{1,0:T(8,128)(2,1)S(1)}, u32[]{:S(2)}, u32[]{:S(2)}) collective-permute-start(f16[16,2048]{1,0:T(8,128)(2,1)S(1)} %convert_element_type.101), channel_id=1, source_target_pairs={{0,2},{1,3},{2,0},{3,1},{4,6},{5,7},{6,4},{7,5},{8,10},{9,11},{10,... | collective-permute-start | bytes 196616 | tf_op jit(solution)/shard_map/ppermute | solution.py:474
  27.3 4.4 %collective-permute-start.7 = (f16[16,2048]{1,0:T(8,128)(2,1)S(1)}, f16[16,2048]{1,0:T(8,128)(2,1)S(1)}, u32[]{:S(2)}, u32[]{:S(2)}) collective-permute-start(f16[16,2048]{1,0:T(8,128)(2,1)S(1)} %convert_element_type.101), channel_id=1, source_target_pairs={{0,1},{1,2},{2,3},{3,0},{4,5},{5,6},{6,7},{7,4},{8,9},{9,10},{10,1... | collective-permute-start | bytes 196616 | tf_op jit(solution)/shard_map/ppermute | solution.py:474
  29.4 2.3 %collective-permute-start.8 = (f16[16,2048]{1,0:T(8,128)(2,1)S(1)}, f16[16,2048]{1,0:T(8,128)(2,1)S(1)}, u32[]{:S(2)}, u32[]{:S(2)}) collective-permute-start(f16[16,2048]{1,0:T(8,128)(2,1)S(1)} %convert_element_type.101), channel_id=1, source_target_pairs={{0,3},{1,0},{2,1},{3,2},{4,7},{5,4},{6,5},{7,6},{8,11},{9,8},{10,9... | collective-permute-start | bytes 196616 | tf_op jit(solution)/shard_map/ppermute | solution.py:474
  31.8 12.9 %copy-start.5 = (f32[16,64,64]{2,1,0:T(8,128)S(1)}, f32[16,64,64]{2,1,0:T(8,128)}, u32[]{:S(2)}) copy-start(f32[16,64,64]{2,1,0:T(8,128)} %m_ref.1) | copy-start | bytes 786436
  32.5 7.5 %collective-permute-start.12 = (f16[25,16,128]{2,1,0:T(8,128)(2,1)S(1)}, f16[25,16,128]{2,1,0:T(8,128)(2,1)S(1)}, u32[]{:S(2)}, u32[]{:S(2)}) collective-permute-start(f16[25,16,128]{2,1,0:T(8,128)(2,1)S(1)} %pad_maximum_fusion.1), channel_id=1, source_target_pairs={{0,4},{4,8},{8,12},{12,0},{1,5},{5,9},{9,13},{13,1},{2,6},{6,10},{... | collective-permute-start | bytes 307208 | tf_op jit(solution)/shard_map/ppermute | solution.py:500
  33.9 10.6 %collective-permute-start.13 = (f16[25,16,128]{2,1,0:T(8,128)(2,1)S(1)}, f16[25,16,128]{2,1,0:T(8,128)(2,1)S(1)}, u32[]{:S(2)}, u32[]{:S(2)}) collective-permute-start(f16[25,16,128]{2,1,0:T(8,128)(2,1)S(1)} %pad_maximum_fusion.1), channel_id=1, source_target_pairs={{0,8},{4,12},{8,0},{12,4},{1,9},{5,13},{9,1},{13,5},{2,10},{6,14},... | collective-permute-start | bytes 307208 | tf_op jit(solution)/shard_map/ppermute | solution.py:500
  36.9 7.6 %collective-permute-start.14 = (f16[25,16,128]{2,1,0:T(8,128)(2,1)S(1)}, f16[25,16,128]{2,1,0:T(8,128)(2,1)S(1)}, u32[]{:S(2)}, u32[]{:S(2)}) collective-permute-start(f16[25,16,128]{2,1,0:T(8,128)(2,1)S(1)} %pad_maximum_fusion.1), channel_id=1, source_target_pairs={{0,12},{4,0},{8,4},{12,8},{1,13},{5,1},{9,5},{13,9},{2,14},{6,2},{... | collective-permute-start | bytes 307208 | tf_op jit(solution)/shard_map/ppermute | solution.py:500
  (4 other events, 35.3 us)
